TPU v7x, 32 devices: a whole 2x2x4 slice. The times are simulated.
32 devices in a mesh: wide: 16 (over z, y, core), narrow: 2 (over x).
Axes of the slice: x: 2, y: 2, z: 4, core: 2. Of those that a mesh axis runs over, the one named last changes fastest.
Arguments:
- pressure: float32 [64, 512, 1024], P(('narrow', 'wide')), may hold values from -6 to 6
- relax_freq: float32 [2], replicated, may hold values from 4 to 64
- relax_depth: float32 [2], replicated, may hold values from 0.1 to 0.6
Outputs:
- advanced: float32 [64, 512, 1024], P(('narrow', 'wide'))
All inputs are finite; a program needn't handle non-finite values.
Results may differ from a plain program's by a relative error of at most 0.000084.
Values sent between devices are 32-bit elements; how exact they have to be, the bound alone decides.
No kernel may reach another device: no remote copies, remote signals or barrier semaphores. Data moves between devices by JAX's collectives and lax.ppermute only.
A program may use at most 128 MiB of HBM per device.

v0:
```python
import functools

import jax
import jax.numpy as jnp
import ml_dtypes
import numpy as np
from jax import lax
from jax.experimental import pallas as pl
from jax.experimental.pallas import tpu as pltpu
from jax.sharding import PartitionSpec as P

SUBSTEPS = 3
WAVE_BREAKING = 0.1
RATE_TOP = 0.2

GANG = 4
SERIES = 2 * SUBSTEPS
LANES = 128
VMEM_LIMIT = 20 * 1024 * 1024
CHUNKS = (((0, 0, 6),), ((0, 6, 2), (1, 0, 4)), ((1, 4, 4),))
MEMBER, ABOVE, BELOW = range(3)
SCALARS = 3
ORDER = ("D0", "D2", "E0", "E1", "E2", "C0", "C1", "C2", "I1", "I2")


def pieces_of(chunk, per_parity):
    unit = per_parity // 8
    return tuple((parity, unit * first, unit * count) for parity, first, count in chunk)


def split_high_low(table):
    high = table.astype(np.float32).astype(ml_dtypes.bfloat16)
    low = (table - high.astype(np.float64)).astype(ml_dtypes.bfloat16)
    return jnp.asarray(high), jnp.asarray(low)


def transform_tables(piece, per_parity, n_time):
    parity, first, count = piece
    member = np.arange(GANG)[:, None]
    bins = 2 * (member * per_parity + first + np.arange(count)) + parity
    half = n_time // 2
    angles = ((bins[..., None] * np.arange(half)) % n_time) * (2.0 * np.pi / n_time)
    weights = np.where(bins == 0, 1.0, 2.0)[..., None] / n_time
    forward = np.stack([np.cos(angles), -np.sin(angles)], axis=1)
    inverse = np.stack([np.cos(angles) * weights, -np.sin(angles) * weights], axis=1)
    return split_high_low(forward.reshape(-1, half)), split_high_low(inverse.reshape(-1, half))


def halves(values):
    high = values.astype(jnp.bfloat16)
    return high, (values - high.astype(jnp.float32)).astype(jnp.bfloat16)


def product(left, right, dims):
    dot = functools.partial(
        lax.dot_general, dimension_numbers=(dims, ((), ())), preferred_element_type=jnp.float32
    )
    return dot(left[0], right[0]) + (dot(left[0], right[1]) + dot(left[1], right[0]))


def partner_rows(table, member, count):
    rows = [
        table[pl.ds(pl.multiple_of((member ^ d) * 2 * count, 2 * count), 2 * count)]
        for d in range(GANG)
    ]
    return jnp.concatenate(rows, axis=0)


def pass_on(info, token):
    for place in range(SCALARS):
        token[place] = info[place]


def forward_kernel(chunks, per_parity, info, freq, depth, pressure, *refs):
    n_tables = 2 * sum(len(pieces) for pieces in chunks)
    tables = iter(refs[:n_tables])
    n_outs = GANG * len(chunks)
    outs = refs[n_tables : n_tables + n_outs]
    token = refs[n_tables + n_outs]
    factors = refs[n_tables + n_outs + 1 :]
    rows, block, n_time = pressure.shape
    half = n_time // 2
    member = info[MEMBER]
    pass_on(info, token)

    @pl.when(pl.program_id(0) == 0)
    def relaxation():
        for chunk, pieces in enumerate(chunks):
            share = factors[2 * chunk].shape[1]
            place = lax.broadcasted_iota(jnp.int32, (8, LANES * pl.cdiv(share, LANES)), 1)
            for d in range(GANG):
                bins = jnp.zeros(place.shape, jnp.int32)
                offset = 0
                for parity, first, count in pieces:
                    here = 2 * ((member ^ d) * per_parity + first - offset + place) + parity
                    bins = jnp.where(place >= offset, here, bins)
                    offset += count
                bins = bins.astype(jnp.float32)
                total_re = jnp.zeros(bins.shape, jnp.float32)
                total_im = jnp.zeros(bins.shape, jnp.float32)
                for process in range(2):
                    ratio = bins / freq[process]
                    scaled = depth[process] / (1.0 + ratio * ratio)
                    total_re = total_re + scaled * ratio * ratio
                    total_im = total_im + scaled * ratio
                amplitude = jnp.exp(-total_re)
                for part, values in enumerate(
                    (amplitude * jnp.cos(total_im), -amplitude * jnp.sin(total_im))
                ):
                    column = values.T[:share, :1]
                    factors[2 * chunk + part][d] = jnp.broadcast_to(column, (share, block))

    wave = pressure[...].reshape(rows * block, n_time)
    lane = lax.broadcasted_iota(jnp.int32, wave.shape, 1)
    squared = wave * wave
    after = jnp.where(lane == n_time - 1, 0.0, pltpu.roll(squared, n_time - 1, 1))
    before = jnp.where(lane == 0, 0.0, pltpu.roll(squared, 1, 1))
    steep = wave + WAVE_BREAKING * 0.25 * (after - before)
    early, late = steep[:, :half], steep[:, half:]
    folded = {}
    for parity in sorted(set(piece[0] for pieces in chunks for piece in pieces)):
        folded[parity] = halves(early - late if parity else early + late)
    for chunk, pieces in enumerate(chunks):
        factor_re, factor_im = factors[2 * chunk : 2 * chunk + 2]
        offset = 0
        for parity, first, count in pieces:
            table = [partner_rows(next(tables), member, count) for _ in range(2)]
            spectrum = product(table, folded[parity], ((1,), (1,)))
            spectrum = spectrum.reshape(GANG, 2, count, rows * block)
            for d in range(GANG):
                here = slice(offset, offset + count)
                fr, fi = factor_re[d, here], factor_im[d, here]
                out = outs[GANG * chunk + d]
                for row in range(rows):
                    across = slice(row * block, (row + 1) * block)
                    real, imag = spectrum[d, 0, :, across], spectrum[d, 1, :, across]
                    out[row, here] = real * fr - imag * fi
                    out[rows + row, here] = real * fi + imag * fr
            offset += count


def cost(microseconds):
    return pl.CostEstimate(
        flops=int(microseconds * 1153000000),
        bytes_accessed=int(microseconds * 3690000),
        transcendentals=0,
    )


def scalars():
    return pl.BlockSpec(memory_space=pltpu.SMEM)


def token_shape():
    return jax.ShapeDtypeStruct((SCALARS,), jnp.int32)


def in_hbm(array):
    return pltpu.with_memory_space_constraint(array, pltpu.HBM)


def forward_chunks(info, pressure, relax_freq, relax_depth, tables, chunks, per_parity):
    rows, width, n_time = pressure.shape
    flat = [in_hbm(t) for chunk in tables for pair in chunk for t in pair]
    out_specs, out_shape, scratch = [], [], []
    for pieces in chunks:
        share = sum(piece[2] for piece in pieces)
        block = pl.BlockSpec((2 * rows, share, LANES), lambda i: (0, 0, i))
        out_specs += [block] * GANG
        out_shape += [jax.ShapeDtypeStruct((2 * rows, share, width), jnp.float32)] * GANG
        scratch += [pltpu.VMEM((GANG, share, LANES), jnp.float32)] * 2
    outs = pl.pallas_call(
        functools.partial(forward_kernel, chunks, per_parity),
        grid=(width // LANES,),
        in_specs=[scalars()] * 3
        + [pl.BlockSpec((rows, LANES, n_time), lambda i: (0, i, 0))]
        + [pl.BlockSpec(t.shape, lambda i: (0, 0)) for t in flat],
        out_specs=out_specs + [scalars()],
        out_shape=out_shape + [token_shape()],
        scratch_shapes=scratch,
        compiler_params=pltpu.CompilerParams(vmem_limit_bytes=VMEM_LIMIT),
        cost_estimate=cost(2 + 2 * len(chunks)),
    )(info, relax_freq, relax_depth, in_hbm(pressure), *flat)
    return outs[-1], [outs[GANG * c : GANG * c + GANG] for c in range(len(chunks))]


def bin_rates(pieces, per_parity, member, half_bins, tile, shape):
    start, offset = 0, 0
    for parity, first, count in pieces:
        here = 2 * (member * per_parity + first + 8 * tile - offset) + parity
        start = jnp.where(8 * tile >= offset, here, start)
        offset += count
    bins = (start + 2 * lax.broadcasted_iota(jnp.int32, shape, 0)).astype(jnp.float32)
    return RATE_TOP * jnp.minimum(bins, 1.0) * jnp.minimum(1.0, half_bins / jnp.maximum(bins, 1.0))


def lateral(width):
    lane = lax.broadcasted_iota(jnp.int32, (8, LANES), 1)
    first_lane, last_lane = lane == 0, lane == LANES - 1

    def apply(center):
        pieces = [center[:, at : at + LANES] for at in range(0, width, LANES)]
        left = [0.0] + [pltpu.roll(piece, 1, 1) for piece in pieces]
        right = [pltpu.roll(piece, LANES - 1, 1) for piece in pieces] + [0.0]
        sides = [
            jnp.where(first_lane, left[n], left[n + 1])
            + jnp.where(last_lane, right[n + 1], right[n])
            - 4.0 * piece
            for n, piece in enumerate(pieces)
        ]
        return jnp.concatenate(sides, axis=1)

    return apply


def evolve_kernel(pieces, per_parity, half_bins, info, *refs):
    parts = refs[:GANG]
    done, top, bottom, token, real, imag = refs[GANG:]
    member = info[MEMBER]
    pass_on(info, token)
    units, share, width = parts[0].shape
    rows = units // 2
    count = GANG * rows
    side = lateral(width)

    def advance(field, other, scale):
        before, center = None, other[0]
        for row in range(count):
            after = other[row + 1] if row < count - 1 else None
            laplace = side(center)
            if before is not None:
                laplace = laplace + before
            if after is not None:
                laplace = laplace + after
            field[row] = field[row] + scale * laplace
            before, center = center, after

    def keep(place, here, field):
        top[place, here], bottom[place, here] = field[0], field[count - 1]

    def tile(index, carry):
        here = pl.ds(pl.multiple_of(8 * index, 8), 8)
        rate = bin_rates(pieces, per_parity, member, half_bins, index, (8, width))
        for d in range(GANG):
            first = (member ^ d) * rows
            for row in range(rows):
                real[first + row] = parts[d][row, here]
                imag[first + row] = parts[d][rows + row, here]
        for step in range(SUBSTEPS):
            keep(2 * step, here, imag)
            advance(real, imag, -rate)
            keep(2 * step + 1, here, real)
            advance(imag, real, rate)
        for row in range(count):
            done[row, here] = real[row]
            done[count + row, here] = imag[row]
        return carry

    lax.fori_loop(0, share // 8, tile, 0)


def in_vmem(count):
    return [pl.BlockSpec(memory_space=pltpu.VMEM)] * count


def evolve_chunk(info, parts, pieces, per_parity, half_bins):
    units, share, width = parts[0].shape
    count = GANG * units // 2
    scratch = pltpu.VMEM((count, 8, width), jnp.float32)
    sizes = (2 * count, SERIES, SERIES)
    return pl.pallas_call(
        functools.partial(evolve_kernel, pieces, per_parity, half_bins),
        in_specs=[scalars()] + in_vmem(GANG),
        out_specs=in_vmem(3) + [scalars()],
        out_shape=[jax.ShapeDtypeStruct((n, share, width), jnp.float32) for n in sizes]
        + [token_shape()],
        scratch_shapes=[scratch, scratch],
        compiler_params=pltpu.CompilerParams(vmem_limit_bytes=VMEM_LIMIT),
        cost_estimate=cost(3.0),
    )(info, *parts)


def correct_kernel(pieces, per_parity, half_bins, info, done, top, bottom, above, below, *refs):
    outs = refs[:GANG]
    token, total, near_re, near_im, far_re, far_im = refs[GANG:]
    member = info[MEMBER]
    pass_on(info, token)
    units, share, width = done.shape
    count = units // 2
    rows = count // GANG
    side = lateral(width)

    def advance(field, source, edge, scale, half_step, deep):
        before, center = edge, source[0] if half_step > 0 else None
        for row in range(deep):
            after = source[row + 1] if row + 1 < half_step else None
            around = before
            if center is not None:
                around = around + side(center)
            if after is not None:
                around = around + after
            change = scale * around
            field[row] = field[row] + change if row < half_step - 1 else change
            before, center = center, after

    def tile(index, carry):
        here = pl.ds(pl.multiple_of(8 * index, 8), 8)
        rate = bin_rates(pieces, per_parity, member, half_bins, index, (8, width))
        for unit in range(units):
            total[unit] = done[unit, here]
        for own, other, flag, order in (
            (top, above, info[ABOVE], range(count)),
            (bottom, below, info[BELOW], range(count - 1, -1, -1)),
        ):
            rate_far = rate * flag.astype(jnp.float32)
            for half_step in range(SERIES):
                own_edge, far_edge = own[half_step, here], other[half_step, here]
                near, near_from = (near_re, near_im) if half_step % 2 == 0 else (near_im, near_re)
                back, back_from = (far_re, far_im) if half_step % 2 == 0 else (far_im, far_re)
                sign = 1.0 if half_step % 2 else -1.0
                if half_step > 0:
                    own_edge = own_edge + near_from[0]
                    far_edge = far_edge + back_from[0]
                reach = min(half_step + 1, SERIES - 1 - half_step)
                advance(near, near_from, far_edge, sign * rate, half_step, half_step + 1)
                advance(back, back_from, own_edge, sign * rate_far, half_step, reach)
            for row in range(SERIES - 1):
                total[order[row]] = total[order[row]] + near_re[row]
            for row in range(SERIES):
                total[count + order[row]] = total[count + order[row]] + near_im[row]
        for d in range(GANG):
            first = (member ^ d) * rows
            for row in range(rows):
                outs[d][row, here] = total[first + row]
                outs[d][rows + row, here] = total[count + first + row]
        return carry

    lax.fori_loop(0, share // 8, tile, 0)


def correct_chunk(info, state, pieces, per_parity, half_bins):
    units, share, width = state[0].shape
    shape = jax.ShapeDtypeStruct((units // GANG, share, width), jnp.float32)
    strip = pltpu.VMEM((SERIES, 8, width), jnp.float32)
    return pl.pallas_call(
        functools.partial(correct_kernel, pieces, per_parity, half_bins),
        in_specs=[scalars()] + in_vmem(5),
        out_specs=in_vmem(GANG) + [scalars()],
        out_shape=[shape] * GANG + [token_shape()],
        scratch_shapes=[pltpu.VMEM((units, 8, width), jnp.float32)] + [strip] * 4,
        compiler_params=pltpu.CompilerParams(vmem_limit_bytes=VMEM_LIMIT),
        cost_estimate=cost(3.5),
    )(info, *state)


def inverse_kernel(chunks, held, last, info, *refs):
    n_parts = GANG * len(chunks)
    n_tables = 2 * sum(len(pieces) for pieces in chunks)
    parts, tables = refs[:n_parts], iter(refs[n_parts : n_parts + n_tables])
    refs = refs[n_parts + n_tables :]
    prior, outs, token = dict(zip(held, refs)), refs[len(held) : -1], refs[-1]
    member = info[MEMBER]
    rows, block = parts[0].shape[0] // 2, parts[0].shape[2]
    half = outs[0].shape[2] // 2 if last else outs[0].shape[2]
    pass_on(info, token)
    sums = {parity: prior[parity][...].reshape(rows * block, half) for parity in held}
    for chunk, pieces in enumerate(chunks):
        offset = 0
        for parity, first, count in pieces:
            pair = [partner_rows(next(tables), member, count) for _ in range(2)]
            here = slice(offset, offset + count)
            packed = [
                jnp.concatenate([part[n * rows + row, here] for row in range(rows)], axis=1)
                for part in parts[GANG * chunk : GANG * chunk + GANG]
                for n in range(2)
            ]
            packed = jnp.concatenate(packed, axis=0).T
            term = product(halves(packed), pair, ((1,), (0,)))
            sums[parity] = sums[parity] + term if parity in sums else term
            offset += count
    if last:
        outs[0][:, :, :half] = (sums[0] + sums[1]).reshape(rows, block, half)
        outs[0][:, :, half:] = (sums[0] - sums[1]).reshape(rows, block, half)
    else:
        for out, parity in zip(outs, sorted(sums)):
            out[...] = sums[parity].reshape(rows, block, half)


def inverse_chunks(info, parts, tables, chunks, sums, last):
    rows, width = parts[0][0].shape[0] // 2, parts[0][0].shape[2]
    half = tables[0][0][0].shape[1]
    flat = [t for chunk in tables for pair in chunk for t in pair]
    held = sorted(sums)
    fresh = sorted(set(held) | set(piece[0] for pieces in chunks for piece in pieces))
    state = pl.BlockSpec((rows, LANES, half), lambda i: (0, i, 0))
    state_shape = jax.ShapeDtypeStruct((rows, width, half), jnp.float32)
    if last:
        out_specs = [pl.BlockSpec((rows, LANES, 2 * half), lambda i: (0, i, 0))]
        out_shape = [jax.ShapeDtypeStruct((rows, width, 2 * half), jnp.float32)]
    else:
        out_specs, out_shape = [state] * len(fresh), [state_shape] * len(fresh)
    in_specs = [scalars()]
    for chunk in parts:
        in_specs += [pl.BlockSpec(chunk[0].shape[:2] + (LANES,), lambda i: (0, 0, i))] * GANG
    outs = pl.pallas_call(
        functools.partial(inverse_kernel, chunks, held, last),
        grid=(width // LANES,),
        in_specs=in_specs
        + [pl.BlockSpec(t.shape, lambda i: (0, 0)) for t in flat]
        + [state] * len(held),
        out_specs=out_specs + [scalars()],
        out_shape=out_shape + [token_shape()],
        compiler_params=pltpu.CompilerParams(vmem_limit_bytes=VMEM_LIMIT),
        cost_estimate=cost(2 + 2 * len(chunks)),
    )(info, *[part for chunk in parts for part in chunk], *flat, *[sums[p] for p in held])
    return outs[-1], outs[0] if last else dict(zip(fresh, outs))


def shards(narrow, wide, axes, pressure, relax_freq, relax_depth):
    rows, width, n_time = pressure.shape
    n_freq = n_time // 2
    per_parity = n_freq // (2 * GANG)
    half_bins = float(n_freq // 2)
    blocks = narrow * wide // GANG

    def device(block, member):
        n, w = divmod(block * GANG + member, wide)
        return w * narrow + n if axes[0] == "wide" else n * wide + w

    swaps = [
        [(device(b, m), device(b, m ^ d)) for b in range(blocks) for m in range(GANG)]
        for d in range(GANG)
    ]
    down = [(device(b, m), device(b + 1, m)) for b in range(blocks - 1) for m in range(GANG)]
    up = [(target, source) for source, target in down]

    place = lax.axis_index("narrow") * wide + lax.axis_index("wide")
    block = place // GANG
    info = [place % GANG, block > 0, block < blocks - 1]
    info = jnp.stack([jnp.asarray(value, jnp.int32) for value in info])

    def swap(parts):
        return [parts[0]] + [lax.ppermute(parts[d], axes, swaps[d]) for d in range(1, GANG)]

    chunks = [pieces_of(chunk, per_parity) for chunk in CHUNKS]
    tables = [[transform_tables(piece, per_parity, n_time) for piece in c] for c in chunks]
    forward = [[pair[0] for pair in c] for c in tables]
    inverse = [[pair[1] for pair in c] for c in tables]
    held = [None] * len(chunks)
    inputs = (pressure, relax_freq, relax_depth)
    sums, begun, finished = {}, 0, 0
    for kernel, c in [(step[0], int(step[1:])) for step in ORDER]:
        shape = (chunks[c], per_parity, half_bins)
        if kernel == "D":
            some, begun = slice(begun, c + 1), c + 1
            info, parts = forward_chunks(info, *inputs, forward[some], chunks[some], per_parity)
            held[some] = [swap(part) for part in parts]
        elif kernel == "E":
            done, top, bottom, info = evolve_chunk(info, held[c], *shape)
            above = lax.ppermute(bottom, axes, down)
            below = lax.ppermute(top, axes, up)
            held[c] = (done, top, bottom, above, below)
        elif kernel == "C":
            *parts, info = correct_chunk(info, held[c], *shape)
            held[c] = swap(parts)
        else:
            some, finished, last = slice(finished, c + 1), c + 1, c + 1 == len(chunks)
            info, sums = inverse_chunks(info, held[some], inverse[some], chunks[some], sums, last)
    return sums


def solution(mesh):
    narrow, wide = mesh.shape["narrow"], mesh.shape["wide"]
    placed = (P(("narrow", "wide"), None, None), P(), P())
    return jax.shard_map(
        functools.partial(shards, narrow, wide, tuple(mesh.axis_names)),
        mesh=mesh,
        in_specs=placed,
        out_specs=P(("narrow", "wide"), None, None),
        check_vma=False,
    )
```

profile of v0, /device:TPU:3, one launch (start us, length us, event | category | flops | bytes accessed | tf_op | source)
XLA Modules:
  0.0 151.6 jit_solution(4811108024289434774)
XLA Ops:
  1.4 7.0 %shard_map.181 = (f32[4,48,512]{2,1,0:T(8,128)S(1)}, f32[4,48,512]{2,1,0:T(8,128)S(1)}, f32[4,48,512]{2,1,0:T(8,128)S(1)}, f32[4,48,512]{2,1,0:T(8,128)S(1)}, s32[3]{0:T(128)S(1)}) custom-call(s32[3]{0:T(128)S(1)} %pad_add_fusion.info, f32[2]{0:T(128)S(1)} %copy-done, f32[2]{0:T(128)S(1)} %copy-done.2, f32[2,512,1024]{2,1,0:T(8,128)} %pressure.3, ...), custom_call_target="tpu_custom_call" | custom-call | flops 4611999744 | bytes 14760000 | tf_op jit(solution)/shard_map/pallas_call | solution.py:172
  10.9 8.8 %shard_map.182 = (f32[4,48,512]{2,1,0:T(8,128)S(1)}, f32[4,48,512]{2,1,0:T(8,128)S(1)}, f32[4,48,512]{2,1,0:T(8,128)S(1)}, f32[4,48,512]{2,1,0:T(8,128)S(1)}, f3...) custom-call(s32[3]{0:T(128)S(1)} %get-tuple-element.50.info, ...), custom_call_target="tpu_custom_call" | custom-call | flops 6918000128 | bytes 22140000 | tf_op jit(solution)/shard_map/pallas_call | solution.py:172
  21.9 7.0 %collective-permute-done.2.refs_3_ = f32[4,48,512]{2,1,0:T(8,128)S(1)} collective-permute-done((f32[4,48,512]{2,1,0:T(8,128)S(1)}, f32[4,48,512]{2,1,0:T(8,128)S(1)}, u32[]{:S(2)}, u32[]{:S(2)}) %collective-permute-start.2) | collective-permute-done | bytes 393248 | tf_op jit(solution)/shard_map/ppermute | solution.py:443
  30.1 4.2 %shard_map.183 = (f32[16,48,512]{2,1,0:T(8,128)S(1)}, f32[6,48,512]{2,1,0:T(8,128)S(1)}, f32[6,48,512]{2,1,0:T(8,128)S(1)}, s32[3]{0:T(128)S(1)}) custom-call(s32[3]{0:T(128)S(1)} %get-tuple-element.51.info, f32[4,48,512]{2,1,0:T(8,128)S(1)} %get-tuple-element.52.refs_0_, f32[4,48,512]{2,1,0:T(8,128)S(1)} %collective-permute-done.refs_1_, ...), custom_call_target="tpu_custom_call" | custom-call | flops 3459000064 | bytes 11070000 | tf_op jit(solution)/shard_map/pallas_call | solution.py:271
  36.7 5.2 %collective-permute-start.10 = (f32[6,48,512]{2,1,0:T(8,128)S(1)}, f32[6,48,512]{2,1,0:T(8,128)S(1)}, u32[]{:S(2)}, u32[]{:S(2)}) collective-permute-start(f32[6,48,512]{2,1,0:T(8,128)S(1)} %get-tuple-element.68.top), channel_id=1, source_target_pairs={{8,0},{10,2},{12,4},{14,6},{16,8},{18,10},{20,12},{22,14},{24,16},... | collective-permute-start | bytes 1769480 | tf_op jit(solution)/shard_map/ppermute | solution.py:461
  41.9 4.1 %collective-permute-done.5.refs_3_ = f32[4,48,512]{2,1,0:T(8,128)S(1)} collective-permute-done((f32[4,48,512]{2,1,0:T(8,128)S(1)}, f32[4,48,512]{2,1,0:T(8,128)S(1)}, u32[]{:S(2)}, u32[]{:S(2)}) %collective-permute-start.5) | collective-permute-done | bytes 393248 | tf_op jit(solution)/shard_map/ppermute | solution.py:443
  46.0 3.2 %collective-permute-start.9 = (f32[6,48,512]{2,1,0:T(8,128)S(1)}, f32[6,48,512]{2,1,0:T(8,128)S(1)}, u32[]{:S(2)}, u32[]{:S(2)}) collective-permute-start(f32[6,48,512]{2,1,0:T(8,128)S(1)} %get-tuple-element.69.bottom), channel_id=1, source_target_pairs={{0,8},{2,10},{4,12},{6,14},{8,16},{10,18},{12,20},{14,22},{16,24},... | collective-permute-start | bytes 1769480 | tf_op jit(solution)/shard_map/ppermute | solution.py:460
  49.2 4.2 %shard_map.184 = (f32[16,48,512]{2,1,0:T(8,128)S(1)}, f32[6,48,512]{2,1,0:T(8,128)S(1)}, f32[6,48,512]{2,1,0:T(8,128)S(1)}, s32[3]{0:T(128)S(1)}) custom-call(s32[3]{0:T(128)S(1)} %get-tuple-element.56.info, f32[4,48,512]{2,1,0:T(8,128)S(1)} %get-tuple-element.57.refs_0_, f32[4,48,512]{2,1,0:T(8,128)S(1)} %collective-permute-done.3.refs_1_, ...), custom_call_target="tpu_custom_call" | custom-call | flops 3459000064 | bytes 11070000 | tf_op jit(solution)/shard_map/pallas_call | solution.py:271
  53.4 3.2 %collective-permute-start.11 = (f32[6,48,512]{2,1,0:T(8,128)S(1)}, f32[6,48,512]{2,1,0:T(8,128)S(1)}, u32[]{:S(2)}, u32[]{:S(2)}) collective-permute-start(f32[6,48,512]{2,1,0:T(8,128)S(1)} %get-tuple-element.73.bottom), channel_id=1, source_target_pairs={{0,8},{2,10},{4,12},{6,14},{8,16},{10,18},{12,20},{14,22},{16,24},... | collective-permute-start | bytes 1769480 | tf_op jit(solution)/shard_map/ppermute | solution.py:460
  56.7 4.8 %collective-permute-start.12 = (f32[6,48,512]{2,1,0:T(8,128)S(1)}, f32[6,48,512]{2,1,0:T(8,128)S(1)}, u32[]{:S(2)}, u32[]{:S(2)}) collective-permute-start(f32[6,48,512]{2,1,0:T(8,128)S(1)} %get-tuple-element.72.top), channel_id=1, source_target_pairs={{8,0},{10,2},{12,4},{14,6},{16,8},{18,10},{20,12},{22,14},{24,16},... | collective-permute-start | bytes 1769480 | tf_op jit(solution)/shard_map/ppermute | solution.py:461
  61.4 3.0 %shard_map.185 = (f32[16,32,512]{2,1,0:T(8,128)S(1)}, f32[6,32,512]{2,1,0:T(8,128)S(1)}, f32[6,32,512]{2,1,0:T(8,128)S(1)}, s32[3]{0:T(128)S(1)}) custom-call(s32[3]{0:T(128)S(1)} %get-tuple-element.61.info, f32[4,32,512]{2,1,0:T(8,128)S(1)} %get-tuple-element.62.refs_0_, f32[4,32,512]{2,1,0:T(8,128)S(1)} %collective-permute-done.6.refs_1_, ...), custom_call_target="tpu_custom_call" | custom-call | flops 3459000064 | bytes 11070000 | tf_op jit(solution)/shard_map/pallas_call | solution.py:271
  66.4 6.1 %collective-permute-start.14 = (f32[6,32,512]{2,1,0:T(8,128)S(1)}, f32[6,32,512]{2,1,0:T(8,128)S(1)}, u32[]{:S(2)}, u32[]{:S(2)}) collective-permute-start(f32[6,32,512]{2,1,0:T(8,128)S(1)} %get-tuple-element.76.top), channel_id=1, source_target_pairs={{8,0},{10,2},{12,4},{14,6},{16,8},{18,10},{20,12},{22,14},{24,16},... | collective-permute-start | bytes 1179656 | tf_op jit(solution)/shard_map/ppermute | solution.py:461
  72.4 4.8 %shard_map.186 = (f32[4,48,512]{2,1,0:T(8,128)S(1)}, f32[4,48,512]{2,1,0:T(8,128)S(1)}, f32[4,48,512]{2,1,0:T(8,128)S(1)}, f32[4,48,512]{2,1,0:T(8,128)S(1)}, s32[3]{0:T(128)S(1)}) custom-call(s32[3]{0:T(128)S(1)} %get-tuple-element.66.info, f32[16,48,512]{2,1,0:T(8,128)S(1)} %get-tuple-element.67.done, f32[6,48,512]{2,1,0:T(8,128)S(1)} %get-tuple-element.68.top, ...), custom_call_target="tpu_custom_call" | custom-call | flops 4035500032 | bytes 12915000 | tf_op jit(solution)/shard_map/pallas_call | solution.py:345
  79.4 11.8 %collective-permute-done.12.below = f32[6,48,512]{2,1,0:T(8,128)S(1)} collective-permute-done((f32[6,48,512]{2,1,0:T(8,128)S(1)}, f32[6,48,512]{2,1,0:T(8,128)S(1)}, u32[]{:S(2)}, u32[]{:S(2)}) %collective-permute-start.12) | collective-permute-done | bytes 589856 | tf_op jit(solution)/shard_map/ppermute | solution.py:461
  91.2 4.8 %shard_map.187 = (f32[4,48,512]{2,1,0:T(8,128)S(1)}, f32[4,48,512]{2,1,0:T(8,128)S(1)}, f32[4,48,512]{2,1,0:T(8,128)S(1)}, f32[4,48,512]{2,1,0:T(8,128)S(1)}, s32[3]{0:T(128)S(1)}) custom-call(s32[3]{0:T(128)S(1)} %get-tuple-element.70.info, f32[16,48,512]{2,1,0:T(8,128)S(1)} %get-tuple-element.71.done, f32[6,48,512]{2,1,0:T(8,128)S(1)} %get-tuple-element.72.top, ...), custom_call_target="tpu_custom_call" | custom-call | flops 4035500032 | bytes 12915000 | tf_op jit(solution)/shard_map/pallas_call | solution.py:345
  96.0 4.1 %collective-permute-start.18 = (f32[4,48,512]{2,1,0:T(8,128)S(1)}, f32[4,48,512]{2,1,0:T(8,128)S(1)}, u32[]{:S(2)}, u32[]{:S(2)}) collective-permute-start(f32[4,48,512]{2,1,0:T(8,128)S(1)} %get-tuple-element.84), channel_id=1, source_target_pairs={{0,2},{2,0},{4,6},{6,4},{8,10},{10,8},{12,14},{14,12},{16,18},{18,... | collective-permute-start | bytes 1179656 | tf_op jit(solution)/shard_map/ppermute | solution.py:443
  104.6 3.5 %collective-permute-done.14.below = f32[6,32,512]{2,1,0:T(8,128)S(1)} collective-permute-done((f32[6,32,512]{2,1,0:T(8,128)S(1)}, f32[6,32,512]{2,1,0:T(8,128)S(1)}, u32[]{:S(2)}, u32[]{:S(2)}) %collective-permute-start.14) | collective-permute-done | bytes 393248 | tf_op jit(solution)/shard_map/ppermute | solution.py:461
  111.9 3.6 %shard_map.188 = (f32[4,32,512]{2,1,0:T(8,128)S(1)}, f32[4,32,512]{2,1,0:T(8,128)S(1)}, f32[4,32,512]{2,1,0:T(8,128)S(1)}, f32[4,32,512]{2,1,0:T(8,128)S(1)}, s32[3]{0:T(128)S(1)}) custom-call(s32[3]{0:T(128)S(1)} %get-tuple-element.74.info, f32[16,32,512]{2,1,0:T(8,128)S(1)} %get-tuple-element.75.done, f32[6,32,512]{2,1,0:T(8,128)S(1)} %get-tuple-element.76.top, ...), custom_call_target="tpu_custom_call" | custom-call | flops 4035500032 | bytes 12915000 | tf_op jit(solution)/shard_map/pallas_call | solution.py:345
  115.6 4.2 %collective-permute-done.20.refs_7_ = f32[4,48,512]{2,1,0:T(8,128)S(1)} collective-permute-done((f32[4,48,512]{2,1,0:T(8,128)S(1)}, f32[4,48,512]{2,1,0:T(8,128)S(1)}, u32[]{:S(2)}, u32[]{:S(2)}) %collective-permute-start.20) | collective-permute-done | bytes 393248 | tf_op jit(solution)/shard_map/ppermute | solution.py:443
  121.3 6.4 %collective-permute-done.16.refs_2_ = f32[4,48,512]{2,1,0:T(8,128)S(1)} collective-permute-done((f32[4,48,512]{2,1,0:T(8,128)S(1)}, f32[4,48,512]{2,1,0:T(8,128)S(1)}, u32[]{:S(2)}, u32[]{:S(2)}) %collective-permute-start.16) | collective-permute-done | bytes 393248 | tf_op jit(solution)/shard_map/ppermute | solution.py:443
  127.7 9.0 %collective-permute-done.17.refs_3_ = f32[4,48,512]{2,1,0:T(8,128)S(1)} collective-permute-done((f32[4,48,512]{2,1,0:T(8,128)S(1)}, f32[4,48,512]{2,1,0:T(8,128)S(1)}, u32[]{:S(2)}, u32[]{:S(2)}) %collective-permute-start.17) | collective-permute-done | bytes 393248 | tf_op jit(solution)/shard_map/ppermute | solution.py:443
  136.8 6.1 %shard_map.189 = (f32[2,512,512]{2,1,0:T(8,128)S(1)}, f32[2,512,512]{2,1,0:T(8,128)S(1)}, s32[3]{0:T(128)S(1)}) custom-call(s32[3]{0:T(128)S(1)} %get-tuple-element.78.info, f32[4,48,512]{2,1,0:T(8,128)S(1)} %get-tuple-element.79.refs_0_, f32[4,48,512]{2,1,0:T(8,128)S(1)} %collective-permute-done.15.refs_1_, ...), custom_call_target="tpu_custom_call" | custom-call | flops 6918000128 | bytes 22140000 | tf_op jit(solution)/shard_map/pallas_call | solution.py:405
  142.9 4.6 %collective-permute-done.23.refs_3_ = f32[4,32,512]{2,1,0:T(8,128)S(1)} collective-permute-done((f32[4,32,512]{2,1,0:T(8,128)S(1)}, f32[4,32,512]{2,1,0:T(8,128)S(1)}, u32[]{:S(2)}, u32[]{:S(2)}) %collective-permute-start.23) | collective-permute-done | bytes 262176 | tf_op jit(solution)/shard_map/ppermute | solution.py:443
  147.5 4.1 %shard_map.190 = (f32[2,512,1024]{2,1,0:T(8,128)}, s32[3]{0:T(128)}) custom-call(s32[3]{0:T(128)S(1)} %get-tuple-element.87.info, f32[4,32,512]{2,1,0:T(8,128)S(1)} %get-tuple-element.88.refs_0_, f32[4,32,512]{2,1,0:T(8,128)S(1)} %collective-permute-done.21.refs_1_, f32[4,32,512]{2,1,0:T(8,128)S(1)} %collective-permute-done.22.refs_2_, ...), custom_call_target="tpu_custom_call" | custom-call | flops 4611999744 | bytes 14760000 | tf_op jit(solution)/shard_map/pallas_call | solution.py:405
  (59 shorter events, 23.6 us)
Async XLA Ops:
  8.4 12.8 %collective-permute-start = (f32[4,48,512]{2,1,0:T(8,128)S(1)}, f32[4,48,512]{2,1,0:T(8,128)S(1)}, u32[]{:S(2)}, u32[]{:S(2)}) collective-permute-start(f32[4,48,512]{2,1,0:T(8,128)S(1)} %get-tuple-element.53), channel_id=1, source_target_pairs={{0,2},{2,0},{4,6},{6,4},{8,10},{10,8},{12,14},{14,12},{16,18},{18,... | collective-permute-start | bytes 1179656 | tf_op jit(solution)/shard_map/ppermute | solution.py:443
  9.2 12.7 %collective-permute-start.1 = (f32[4,48,512]{2,1,0:T(8,128)S(1)}, f32[4,48,512]{2,1,0:T(8,128)S(1)}, u32[]{:S(2)}, u32[]{:S(2)}) collective-permute-start(f32[4,48,512]{2,1,0:T(8,128)S(1)} %get-tuple-element.54), channel_id=1, source_target_pairs={{0,4},{2,6},{4,0},{6,2},{8,12},{10,14},{12,8},{14,10},{16,20},{18,... | collective-permute-start | bytes 1179656 | tf_op jit(solution)/shard_map/ppermute | solution.py:443
  10.4 18.5 %collective-permute-start.2 = (f32[4,48,512]{2,1,0:T(8,128)S(1)}, f32[4,48,512]{2,1,0:T(8,128)S(1)}, u32[]{:S(2)}, u32[]{:S(2)}) collective-permute-start(f32[4,48,512]{2,1,0:T(8,128)S(1)} %get-tuple-element.55), channel_id=1, source_target_pairs={{0,6},{2,4},{4,2},{6,0},{8,14},{10,12},{12,10},{14,8},{16,22},{18,... | collective-permute-start | bytes 1179656 | tf_op jit(solution)/shard_map/ppermute | solution.py:443
  19.7 14.6 %collective-permute-start.3 = (f32[4,48,512]{2,1,0:T(8,128)S(1)}, f32[4,48,512]{2,1,0:T(8,128)S(1)}, u32[]{:S(2)}, u32[]{:S(2)}) collective-permute-start(f32[4,48,512]{2,1,0:T(8,128)S(1)} %get-tuple-element.58), channel_id=1, source_target_pairs={{0,2},{2,0},{4,6},{6,4},{8,10},{10,8},{12,14},{14,12},{16,18},{18,... | collective-permute-start | bytes 1179656 | tf_op jit(solution)/shard_map/ppermute | solution.py:443
  19.9 16.8 %collective-permute-start.4 = (f32[4,48,512]{2,1,0:T(8,128)S(1)}, f32[4,48,512]{2,1,0:T(8,128)S(1)}, u32[]{:S(2)}, u32[]{:S(2)}) collective-permute-start(f32[4,48,512]{2,1,0:T(8,128)S(1)} %get-tuple-element.59), channel_id=1, source_target_pairs={{0,4},{2,6},{4,0},{6,2},{8,12},{10,14},{12,8},{14,10},{16,20},{18,... | collective-permute-start | bytes 1179656 | tf_op jit(solution)/shard_map/ppermute | solution.py:443
  21.2 24.9 %collective-permute-start.5 = (f32[4,48,512]{2,1,0:T(8,128)S(1)}, f32[4,48,512]{2,1,0:T(8,128)S(1)}, u32[]{:S(2)}, u32[]{:S(2)}) collective-permute-start(f32[4,48,512]{2,1,0:T(8,128)S(1)} %get-tuple-element.60), channel_id=1, source_target_pairs={{0,6},{2,4},{4,2},{6,0},{8,14},{10,12},{12,10},{14,8},{16,22},{18,... | collective-permute-start | bytes 1179656 | tf_op jit(solution)/shard_map/ppermute | solution.py:443
  21.9 31.5 %collective-permute-start.6 = (f32[4,32,512]{2,1,0:T(8,128)S(1)}, f32[4,32,512]{2,1,0:T(8,128)S(1)}, u32[]{:S(2)}, u32[]{:S(2)}) collective-permute-start(f32[4,32,512]{2,1,0:T(8,128)S(1)} %get-tuple-element.63), channel_id=1, source_target_pairs={{0,2},{2,0},{4,6},{6,4},{8,10},{10,8},{12,14},{14,12},{16,18},{18,... | collective-permute-start | bytes 786440 | tf_op jit(solution)/shard_map/ppermute | solution.py:443
  28.9 27.8 %collective-permute-start.7 = (f32[4,32,512]{2,1,0:T(8,128)S(1)}, f32[4,32,512]{2,1,0:T(8,128)S(1)}, u32[]{:S(2)}, u32[]{:S(2)}) collective-permute-start(f32[4,32,512]{2,1,0:T(8,128)S(1)} %get-tuple-element.64), channel_id=1, source_target_pairs={{0,4},{2,6},{4,0},{6,2},{8,12},{10,14},{12,8},{14,10},{16,20},{18,... | collective-permute-start | bytes 786440 | tf_op jit(solution)/shard_map/ppermute | solution.py:443
  34.3 27.1 %collective-permute-start.8 = (f32[4,32,512]{2,1,0:T(8,128)S(1)}, f32[4,32,512]{2,1,0:T(8,128)S(1)}, u32[]{:S(2)}, u32[]{:S(2)}) collective-permute-start(f32[4,32,512]{2,1,0:T(8,128)S(1)} %get-tuple-element.65), channel_id=1, source_target_pairs={{0,6},{2,4},{4,2},{6,0},{8,14},{10,12},{12,10},{14,8},{16,22},{18,... | collective-permute-start | bytes 786440 | tf_op jit(solution)/shard_map/ppermute | solution.py:443
  36.7 29.6 %collective-permute-start.10 = (f32[6,48,512]{2,1,0:T(8,128)S(1)}, f32[6,48,512]{2,1,0:T(8,128)S(1)}, u32[]{:S(2)}, u32[]{:S(2)}) collective-permute-start(f32[6,48,512]{2,1,0:T(8,128)S(1)} %get-tuple-element.68.top), channel_id=1, source_target_pairs={{8,0},{10,2},{12,4},{14,6},{16,8},{18,10},{20,12},{22,14},{24,16},... | collective-permute-start | bytes 1769480 | tf_op jit(solution)/shard_map/ppermute | solution.py:461
  46.0 26.4 %collective-permute-start.9 = (f32[6,48,512]{2,1,0:T(8,128)S(1)}, f32[6,48,512]{2,1,0:T(8,128)S(1)}, u32[]{:S(2)}, u32[]{:S(2)}) collective-permute-start(f32[6,48,512]{2,1,0:T(8,128)S(1)} %get-tuple-element.69.bottom), channel_id=1, source_target_pairs={{0,8},{2,10},{4,12},{6,14},{8,16},{10,18},{12,20},{14,22},{16,24},... | collective-permute-start | bytes 1769480 | tf_op jit(solution)/shard_map/ppermute | solution.py:460
  53.4 26.0 %collective-permute-start.11 = (f32[6,48,512]{2,1,0:T(8,128)S(1)}, f32[6,48,512]{2,1,0:T(8,128)S(1)}, u32[]{:S(2)}, u32[]{:S(2)}) collective-permute-start(f32[6,48,512]{2,1,0:T(8,128)S(1)} %get-tuple-element.73.bottom), channel_id=1, source_target_pairs={{0,8},{2,10},{4,12},{6,14},{8,16},{10,18},{12,20},{14,22},{16,24},... | collective-permute-start | bytes 1769480 | tf_op jit(solution)/shard_map/ppermute | solution.py:460
  56.7 34.5 %collective-permute-start.12 = (f32[6,48,512]{2,1,0:T(8,128)S(1)}, f32[6,48,512]{2,1,0:T(8,128)S(1)}, u32[]{:S(2)}, u32[]{:S(2)}) collective-permute-start(f32[6,48,512]{2,1,0:T(8,128)S(1)} %get-tuple-element.72.top), channel_id=1, source_target_pairs={{8,0},{10,2},{12,4},{14,6},{16,8},{18,10},{20,12},{22,14},{24,16},... | collective-permute-start | bytes 1769480 | tf_op jit(solution)/shard_map/ppermute | solution.py:461
  64.4 37.4 %collective-permute-start.13 = (f32[6,32,512]{2,1,0:T(8,128)S(1)}, f32[6,32,512]{2,1,0:T(8,128)S(1)}, u32[]{:S(2)}, u32[]{:S(2)}) collective-permute-start(f32[6,32,512]{2,1,0:T(8,128)S(1)} %get-tuple-element.77.bottom), channel_id=1, source_target_pairs={{0,8},{2,10},{4,12},{6,14},{8,16},{10,18},{12,20},{14,22},{16,24},... | collective-permute-start | bytes 1179656 | tf_op jit(solution)/shard_map/ppermute | solution.py:460
  66.4 41.7 %collective-permute-start.14 = (f32[6,32,512]{2,1,0:T(8,128)S(1)}, f32[6,32,512]{2,1,0:T(8,128)S(1)}, u32[]{:S(2)}, u32[]{:S(2)}) collective-permute-start(f32[6,32,512]{2,1,0:T(8,128)S(1)} %get-tuple-element.76.top), channel_id=1, source_target_pairs={{8,0},{10,2},{12,4},{14,6},{16,8},{18,10},{20,12},{22,14},{24,16},... | collective-permute-start | bytes 1179656 | tf_op jit(solution)/shard_map/ppermute | solution.py:461
  96.0 13.3 %collective-permute-start.18 = (f32[4,48,512]{2,1,0:T(8,128)S(1)}, f32[4,48,512]{2,1,0:T(8,128)S(1)}, u32[]{:S(2)}, u32[]{:S(2)}) collective-permute-start(f32[4,48,512]{2,1,0:T(8,128)S(1)} %get-tuple-element.84), channel_id=1, source_target_pairs={{0,2},{2,0},{4,6},{6,4},{8,10},{10,8},{12,14},{14,12},{16,18},{18,... | collective-permute-start | bytes 1179656 | tf_op jit(solution)/shard_map/ppermute | solution.py:443
  100.1 15.4 %collective-permute-start.19 = (f32[4,48,512]{2,1,0:T(8,128)S(1)}, f32[4,48,512]{2,1,0:T(8,128)S(1)}, u32[]{:S(2)}, u32[]{:S(2)}) collective-permute-start(f32[4,48,512]{2,1,0:T(8,128)S(1)} %get-tuple-element.85), channel_id=1, source_target_pairs={{0,4},{2,6},{4,0},{6,2},{8,12},{10,14},{12,8},{14,10},{16,20},{18,... | collective-permute-start | bytes 1179656 | tf_op jit(solution)/shard_map/ppermute | solution.py:443
  101.4 18.5 %collective-permute-start.20 = (f32[4,48,512]{2,1,0:T(8,128)S(1)}, f32[4,48,512]{2,1,0:T(8,128)S(1)}, u32[]{:S(2)}, u32[]{:S(2)}) collective-permute-start(f32[4,48,512]{2,1,0:T(8,128)S(1)} %get-tuple-element.86), channel_id=1, source_target_pairs={{0,6},{2,4},{4,2},{6,0},{8,14},{10,12},{12,10},{14,8},{16,22},{18,... | collective-permute-start | bytes 1179656 | tf_op jit(solution)/shard_map/ppermute | solution.py:443
  101.8 19.3 %collective-permute-start.15 = (f32[4,48,512]{2,1,0:T(8,128)S(1)}, f32[4,48,512]{2,1,0:T(8,128)S(1)}, u32[]{:S(2)}, u32[]{:S(2)}) collective-permute-start(f32[4,48,512]{2,1,0:T(8,128)S(1)} %get-tuple-element.80), channel_id=1, source_target_pairs={{0,2},{2,0},{4,6},{6,4},{8,10},{10,8},{12,14},{14,12},{16,18},{18,... | collective-permute-start | bytes 1179656 | tf_op jit(solution)/shard_map/ppermute | solution.py:443
  108.0 19.6 %collective-permute-start.16 = (f32[4,48,512]{2,1,0:T(8,128)S(1)}, f32[4,48,512]{2,1,0:T(8,128)S(1)}, u32[]{:S(2)}, u32[]{:S(2)}) collective-permute-start(f32[4,48,512]{2,1,0:T(8,128)S(1)} %get-tuple-element.81), channel_id=1, source_target_pairs={{0,4},{2,6},{4,0},{6,2},{8,12},{10,14},{12,8},{14,10},{16,20},{18,... | collective-permute-start | bytes 1179656 | tf_op jit(solution)/shard_map/ppermute | solution.py:443
  109.3 27.4 %collective-permute-start.17 = (f32[4,48,512]{2,1,0:T(8,128)S(1)}, f32[4,48,512]{2,1,0:T(8,128)S(1)}, u32[]{:S(2)}, u32[]{:S(2)}) collective-permute-start(f32[4,48,512]{2,1,0:T(8,128)S(1)} %get-tuple-element.82), channel_id=1, source_target_pairs={{0,6},{2,4},{4,2},{6,0},{8,14},{10,12},{12,10},{14,8},{16,22},{18,... | collective-permute-start | bytes 1179656 | tf_op jit(solution)/shard_map/ppermute | solution.py:443
  115.6 27.4 %collective-permute-start.21 = (f32[4,32,512]{2,1,0:T(8,128)S(1)}, f32[4,32,512]{2,1,0:T(8,128)S(1)}, u32[]{:S(2)}, u32[]{:S(2)}) collective-permute-start(f32[4,32,512]{2,1,0:T(8,128)S(1)} %get-tuple-element.89), channel_id=1, source_target_pairs={{0,2},{2,0},{4,6},{6,4},{8,10},{10,8},{12,14},{14,12},{16,18},{18,... | collective-permute-start | bytes 786440 | tf_op jit(solution)/shard_map/ppermute | solution.py:443
  119.9 23.1 %collective-permute-start.22 = (f32[4,32,512]{2,1,0:T(8,128)S(1)}, f32[4,32,512]{2,1,0:T(8,128)S(1)}, u32[]{:S(2)}, u32[]{:S(2)}) collective-permute-start(f32[4,32,512]{2,1,0:T(8,128)S(1)} %get-tuple-element.90), channel_id=1, source_target_pairs={{0,4},{2,6},{4,0},{6,2},{8,12},{10,14},{12,8},{14,10},{16,20},{18,... | collective-permute-start | bytes 786440 | tf_op jit(solution)/shard_map/ppermute | solution.py:443
  121.1 26.4 %collective-permute-start.23 = (f32[4,32,512]{2,1,0:T(8,128)S(1)}, f32[4,32,512]{2,1,0:T(8,128)S(1)}, u32[]{:S(2)}, u32[]{:S(2)}) collective-permute-start(f32[4,32,512]{2,1,0:T(8,128)S(1)} %get-tuple-element.91), channel_id=1, source_target_pairs={{0,6},{2,4},{4,2},{6,0},{8,14},{10,12},{12,10},{14,8},{16,22},{18,... | collective-permute-start | bytes 786440 | tf_op jit(solution)/shard_map/ppermute | solution.py:443
  (12 other events, 190.6 us)
where the time goes:
time: 154 us; the launch traced here: 152 us
  waiting for transfers between devices  54.9 us (36%)
  Pallas kernels  50.6 us (33%)
  starting transfers between devices  44.4 us (29%)
    ppermute x18, waiting for transfers between devices, swap(): lax.ppermute(parts[d], axes, swaps[d])  37.5 us
    ppermute x18, starting transfers between devices, swap(): lax.ppermute(parts[d], axes, swaps[d])  20 us
    ppermute x3, starting transfers between devices, shards(): below = lax.ppermute(top, axes, up)  16 us
    pallas_call x2, Pallas kernels, forward_chunks(): pl.pallas_call(functools.partial(forward_kernel, chunks, per_parity), gri...  15.8 us
    ppermute x3, waiting for transfers between devices, shards(): below = lax.ppermute(top, axes, up)  15.2 us
    pallas_call x3, Pallas kernels, correct_chunk(): pl.pallas_call(functools.partial(correct_kernel, pieces, per_parity, half...  13.2 us
    pallas_call x3, Pallas kernels, evolve_chunk(): pl.pallas_call(functools.partial(evolve_kernel, pieces, per_parity, half_...  11.3 us
    pallas_call x2, Pallas kernels, inverse_chunks(): pl.pallas_call(functools.partial(inverse_kernel, chunks, held, last), gri...  10.2 us
  transfers between devices with their start and end apart: 24, of which 10 were waited for; matrix products, arithmetic and copies ran while one was open for 0% of the time, Pallas kernels for 26%

commit v1 on v0

--- a/solution.py
+++ b/solution.py
@@ -17,10 +17,10 @@
 SERIES = 2 * SUBSTEPS
 LANES = 128
 VMEM_LIMIT = 20 * 1024 * 1024
-CHUNKS = (((0, 0, 6),), ((0, 6, 2), (1, 0, 4)), ((1, 4, 4),))
+CHUNKS = (((0, 0, 4),), ((0, 4, 4),), ((1, 0, 4),), ((1, 4, 4),))
 MEMBER, ABOVE, BELOW = range(3)
 SCALARS = 3
-ORDER = ("D0", "D2", "E0", "E1", "E2", "C0", "C1", "C2", "I1", "I2")
+ORDER = ("D1", "D3", "E0", "E1", "C0", "E2", "C1", "E3", "I0", "C2", "I1", "C3", "I2", "I3")
 
 
 def pieces_of(chunk, per_parity):
@@ -141,7 +141,7 @@
 
 def cost(microseconds):
     return pl.CostEstimate(
-        flops=int(microseconds * 1153000000),
+        flops=int(microseconds * 1153000),
         bytes_accessed=int(microseconds * 3690000),
         transcendentals=0,
     )

time: 154 us -> 125 us (0.81); the launches traced: 152 us -> 124 us
  waiting for transfers between devices: 54.9 us -> 17.4 us
  starting transfers between devices: 44.4 us -> 49.8 us
  Pallas kernels: 50.6 us -> 55.3 us
    ppermute x18 -> x24, waiting for transfers between devices: 37.5 us -> 15.9 us  [swap(): lax.ppermute(parts[d], axes, swaps[d])]
    ppermute x3 -> x4, waiting for transfers between devices: 15.2 us -> 0.01 us  [shards(): below = lax.ppermute(top, axes, up)]
    ppermute x3 -> x4, starting transfers between devices: 16 us -> 20.6 us  [shards(): below = lax.ppermute(top, axes, up)]
    pallas_call x2 -> x4, Pallas kernels: 10.2 us -> 14.2 us  [inverse_chunks(): pl.pallas_call(functools.partial(inverse_kernel, chunks, held, last), gri...]
    ppermute x18 -> x24, starting transfers between devices: 20 us -> 21.5 us  [swap(): lax.ppermute(parts[d], axes, swaps[d])]
    pallas_call x3 -> x4, Pallas kernels: 13.2 us -> 14.4 us  [correct_chunk(): pl.pallas_call(functools.partial(correct_kernel, pieces, per_parity, half...]
    ppermute x3 -> x4, starting transfers between devices: 8.32 us -> 7.68 us  [shards(): above = lax.ppermute(bottom, axes, down)]
    pallas_call x3 -> x4, Pallas kernels: 11.3 us -> 11.9 us  [evolve_chunk(): pl.pallas_call(functools.partial(evolve_kernel, pieces, per_parity, half_...]
  transfers between devices with their start and end apart: 24 -> 32, of which waited for: 10 -> 7; matrix products, arithmetic and copies ran while one was open for 0% -> 0% of each run, Pallas kernels for 26% -> 35%
where the time goes in v1:
time: 125 us; the launch traced here: 124 us
  Pallas kernels  55.3 us (44%)
  starting transfers between devices  49.8 us (40%)
  waiting for transfers between devices  17.4 us (14%)
  local copies, waits for them, and re-layouts  1.37 us (1%)
    ppermute x24, starting transfers between devices, swap(): lax.ppermute(parts[d], axes, swaps[d])  21.5 us
    ppermute x4, starting transfers between devices, shards(): below = lax.ppermute(top, axes, up)  20.6 us
    ppermute x24, waiting for transfers between devices, swap(): lax.ppermute(parts[d], axes, swaps[d])  15.9 us
    pallas_call x2, Pallas kernels, forward_chunks(): pl.pallas_call(functools.partial(forward_kernel, chunks, per_parity), gri...  15 us
    pallas_call x4, Pallas kernels, correct_chunk(): pl.pallas_call(functools.partial(correct_kernel, pieces, per_parity, half...  14.4 us
    pallas_call x4, Pallas kernels, inverse_chunks(): pl.pallas_call(functools.partial(inverse_kernel, chunks, held, last), gri...  14.2 us
    pallas_call x4, Pallas kernels, evolve_chunk(): pl.pallas_call(functools.partial(evolve_kernel, pieces, per_parity, half_...  11.9 us
    ppermute x4, starting transfers between devices, shards(): above = lax.ppermute(bottom, axes, down)  7.68 us
  transfers between devices with their start and end apart: 32, of which 7 were waited for; matrix products, arithmetic and copies ran while one was open for 0% of the time, Pallas kernels for 35%

profile of v1, /device:TPU:3, one launch (start us, length us, event | category | flops | bytes accessed | tf_op | source)
XLA Modules:
  0.0 124.3 jit_solution(12183085975520312982)
XLA Ops:
  1.4 7.5 %shard_map.181 = (f32[4,32,512]{2,1,0:T(8,128)S(1)}, f32[4,32,512]{2,1,0:T(8,128)S(1)}, f32[4,32,512]{2,1,0:T(8,128)S(1)}, f32[4,32,512]{2,1,0:T(8,128)S(1)}, f3...) custom-call(s32[3]{0:T(128)S(1)} %pad_add_fusion.info, ...), custom_call_target="tpu_custom_call" | custom-call | flops 6918000 | bytes 22140000 | tf_op jit(solution)/shard_map/pallas_call | solution.py:172
  13.5 7.5 %shard_map.182 = (f32[4,32,512]{2,1,0:T(8,128)S(1)}, f32[4,32,512]{2,1,0:T(8,128)S(1)}, f32[4,32,512]{2,1,0:T(8,128)S(1)}, f32[4,32,512]{2,1,0:T(8,128)S(1)}, f3...) custom-call(s32[3]{0:T(128)S(1)} %get-tuple-element.67.info, ...), custom_call_target="tpu_custom_call" | custom-call | flops 6918000 | bytes 22140000 | tf_op jit(solution)/shard_map/pallas_call | solution.py:172
  21.0 2.8 %collective-permute-done.2.refs_3_ = f32[4,32,512]{2,1,0:T(8,128)S(1)} collective-permute-done((f32[4,32,512]{2,1,0:T(8,128)S(1)}, f32[4,32,512]{2,1,0:T(8,128)S(1)}, u32[]{:S(2)}, u32[]{:S(2)}) %collective-permute-start.2) | collective-permute-done | bytes 262176 | tf_op jit(solution)/shard_map/ppermute | solution.py:443
  23.7 3.0 %shard_map.183 = (f32[16,32,512]{2,1,0:T(8,128)S(1)}, f32[6,32,512]{2,1,0:T(8,128)S(1)}, f32[6,32,512]{2,1,0:T(8,128)S(1)}, s32[3]{0:T(128)S(1)}) custom-call(s32[3]{0:T(128)S(1)} %get-tuple-element.68.info, f32[4,32,512]{2,1,0:T(8,128)S(1)} %get-tuple-element.69.refs_0_, f32[4,32,512]{2,1,0:T(8,128)S(1)} %collective-permute-done.refs_1_, ...), custom_call_target="tpu_custom_call" | custom-call | flops 3459000 | bytes 11070000 | tf_op jit(solution)/shard_map/pallas_call | solution.py:271
  26.7 5.2 %collective-permute-start.7 = (f32[6,32,512]{2,1,0:T(8,128)S(1)}, f32[6,32,512]{2,1,0:T(8,128)S(1)}, u32[]{:S(2)}, u32[]{:S(2)}) collective-permute-start(f32[6,32,512]{2,1,0:T(8,128)S(1)} %get-tuple-element.80.top), channel_id=1, source_target_pairs={{8,0},{10,2},{12,4},{14,6},{16,8},{18,10},{20,12},{22,14},{24,16},... | collective-permute-start | bytes 1179656 | tf_op jit(solution)/shard_map/ppermute | solution.py:461
  36.1 3.0 %shard_map.184 = (f32[16,32,512]{2,1,0:T(8,128)S(1)}, f32[6,32,512]{2,1,0:T(8,128)S(1)}, f32[6,32,512]{2,1,0:T(8,128)S(1)}, s32[3]{0:T(128)S(1)}) custom-call(s32[3]{0:T(128)S(1)} %get-tuple-element.73.info, f32[4,32,512]{2,1,0:T(8,128)S(1)} %get-tuple-element.74.refs_0_, f32[4,32,512]{2,1,0:T(8,128)S(1)} %collective-permute-done.3.refs_1_, ...), custom_call_target="tpu_custom_call" | custom-call | flops 3459000 | bytes 11070000 | tf_op jit(solution)/shard_map/pallas_call | solution.py:271
  39.1 6.0 %collective-permute-start.12 = (f32[6,32,512]{2,1,0:T(8,128)S(1)}, f32[6,32,512]{2,1,0:T(8,128)S(1)}, u32[]{:S(2)}, u32[]{:S(2)}) collective-permute-start(f32[6,32,512]{2,1,0:T(8,128)S(1)} %get-tuple-element.89.top), channel_id=1, source_target_pairs={{8,0},{10,2},{12,4},{14,6},{16,8},{18,10},{20,12},{22,14},{24,16},... | collective-permute-start | bytes 1179656 | tf_op jit(solution)/shard_map/ppermute | solution.py:461
  52.0 3.6 %shard_map.185 = (f32[4,32,512]{2,1,0:T(8,128)S(1)}, f32[4,32,512]{2,1,0:T(8,128)S(1)}, f32[4,32,512]{2,1,0:T(8,128)S(1)}, f32[4,32,512]{2,1,0:T(8,128)S(1)}, s32[3]{0:T(128)S(1)}) custom-call(s32[3]{0:T(128)S(1)} %get-tuple-element.78.info, f32[16,32,512]{2,1,0:T(8,128)S(1)} %get-tuple-element.79.done, f32[6,32,512]{2,1,0:T(8,128)S(1)} %get-tuple-element.80.top, ...), custom_call_target="tpu_custom_call" | custom-call | flops 4035500 | bytes 12915000 | tf_op jit(solution)/shard_map/pallas_call | solution.py:345
  55.6 3.0 %shard_map.186 = (f32[16,32,512]{2,1,0:T(8,128)S(1)}, f32[6,32,512]{2,1,0:T(8,128)S(1)}, f32[6,32,512]{2,1,0:T(8,128)S(1)}, s32[3]{0:T(128)S(1)}) custom-call(s32[3]{0:T(128)S(1)} %get-tuple-element.82.info, f32[4,32,512]{2,1,0:T(8,128)S(1)} %get-tuple-element.83.refs_0_, f32[4,32,512]{2,1,0:T(8,128)S(1)} %collective-permute-done.8.refs_1_, ...), custom_call_target="tpu_custom_call" | custom-call | flops 3459000 | bytes 11070000 | tf_op jit(solution)/shard_map/pallas_call | solution.py:271
  58.7 4.3 %collective-permute-start.20 = (f32[6,32,512]{2,1,0:T(8,128)S(1)}, f32[6,32,512]{2,1,0:T(8,128)S(1)}, u32[]{:S(2)}, u32[]{:S(2)}) collective-permute-start(f32[6,32,512]{2,1,0:T(8,128)S(1)} %get-tuple-element.103.top), channel_id=1, source_target_pairs={{8,0},{10,2},{12,4},{14,6},{16,8},{18,10},{20,12},{22,14},{24,16},... | collective-permute-start | bytes 1179656 | tf_op jit(solution)/shard_map/ppermute | solution.py:461
  66.9 2.0 %collective-permute-start.18 = (f32[4,32,512]{2,1,0:T(8,128)S(1)}, f32[4,32,512]{2,1,0:T(8,128)S(1)}, u32[]{:S(2)}, u32[]{:S(2)}) collective-permute-start(f32[4,32,512]{2,1,0:T(8,128)S(1)} %get-tuple-element.100), channel_id=1, source_target_pairs={{0,6},{2,4},{4,2},{6,0},{8,14},{10,12},{12,10},{14,8},{16,22},{18,... | collective-permute-start | bytes 786440 | tf_op jit(solution)/shard_map/ppermute | solution.py:443
  68.9 3.6 %shard_map.187 = (f32[4,32,512]{2,1,0:T(8,128)S(1)}, f32[4,32,512]{2,1,0:T(8,128)S(1)}, f32[4,32,512]{2,1,0:T(8,128)S(1)}, f32[4,32,512]{2,1,0:T(8,128)S(1)}, s32[3]{0:T(128)S(1)}) custom-call(s32[3]{0:T(128)S(1)} %get-tuple-element.87.info, f32[16,32,512]{2,1,0:T(8,128)S(1)} %get-tuple-element.88.done, f32[6,32,512]{2,1,0:T(8,128)S(1)} %get-tuple-element.89.top, ...), custom_call_target="tpu_custom_call" | custom-call | flops 4035500 | bytes 12915000 | tf_op jit(solution)/shard_map/pallas_call | solution.py:345
  72.6 3.0 %shard_map.188 = (f32[16,32,512]{2,1,0:T(8,128)S(1)}, f32[6,32,512]{2,1,0:T(8,128)S(1)}, f32[6,32,512]{2,1,0:T(8,128)S(1)}, s32[3]{0:T(128)S(1)}) custom-call(s32[3]{0:T(128)S(1)} %get-tuple-element.91.info, f32[4,32,512]{2,1,0:T(8,128)S(1)} %get-tuple-element.92.refs_0_, f32[4,32,512]{2,1,0:T(8,128)S(1)} %collective-permute-done.13.refs_1_, ...), custom_call_target="tpu_custom_call" | custom-call | flops 3459000 | bytes 11070000 | tf_op jit(solution)/shard_map/pallas_call | solution.py:271
  75.6 5.0 %collective-permute-start.25 = (f32[6,32,512]{2,1,0:T(8,128)S(1)}, f32[6,32,512]{2,1,0:T(8,128)S(1)}, u32[]{:S(2)}, u32[]{:S(2)}) collective-permute-start(f32[6,32,512]{2,1,0:T(8,128)S(1)} %get-tuple-element.113.top), channel_id=1, source_target_pairs={{8,0},{10,2},{12,4},{14,6},{16,8},{18,10},{20,12},{22,14},{24,16},... | collective-permute-start | bytes 1179656 | tf_op jit(solution)/shard_map/ppermute | solution.py:461
  85.8 3.2 %shard_map.189 = (f32[2,512,512]{2,1,0:T(8,128)S(1)}, s32[3]{0:T(128)S(1)}) custom-call(s32[3]{0:T(128)S(1)} %get-tuple-element.96.info, f32[4,32,512]{2,1,0:T(8,128)S(1)} %get-tuple-element.97.refs_0_, f32[4,32,512]{2,1,0:T(8,128)S(1)} %collective-permute-done.16.refs_1_, f32[4,32,512]{2,1,0:T(8,128)S(1)} %collective-permute-done.17.refs_2_, ...), custom_call_target="tpu_custom_call" | custom-call | flops 4612000 | bytes 14760000 | tf_op jit(solution)/shard_map/pallas_call | solution.py:405
  89.1 3.6 %shard_map.190 = (f32[4,32,512]{2,1,0:T(8,128)S(1)}, f32[4,32,512]{2,1,0:T(8,128)S(1)}, f32[4,32,512]{2,1,0:T(8,128)S(1)}, f32[4,32,512]{2,1,0:T(8,128)S(1)}, s32[3]{0:T(128)S(1)}) custom-call(s32[3]{0:T(128)S(1)} %get-tuple-element.101.info, f32[16,32,512]{2,1,0:T(8,128)S(1)} %get-tuple-element.102.done, f32[6,32,512]{2,1,0:T(8,128)S(1)} %get-tuple-element.103.top, ...), custom_call_target="tpu_custom_call" | custom-call | flops 4035500 | bytes 12915000 | tf_op jit(solution)/shard_map/pallas_call | solution.py:345
  93.7 3.8 %collective-permute-done.23.refs_3_ = f32[4,32,512]{2,1,0:T(8,128)S(1)} collective-permute-done((f32[4,32,512]{2,1,0:T(8,128)S(1)}, f32[4,32,512]{2,1,0:T(8,128)S(1)}, u32[]{:S(2)}, u32[]{:S(2)}) %collective-permute-start.23) | collective-permute-done | bytes 262176 | tf_op jit(solution)/shard_map/ppermute | solution.py:443
  97.5 3.4 %shard_map.191 = (f32[2,512,512]{2,1,0:T(8,128)S(1)}, s32[3]{0:T(128)S(1)}) custom-call(s32[3]{0:T(128)S(1)} %get-tuple-element.105.info, f32[4,32,512]{2,1,0:T(8,128)S(1)} %get-tuple-element.106.refs_0_, f32[4,32,512]{2,1,0:T(8,128)S(1)} %collective-permute-done.21.refs_1_, f32[4,32,512]{2,1,0:T(8,128)S(1)} %collective-permute-done.22.refs_2_, ...), custom_call_target="tpu_custom_call" | custom-call | flops 4612000 | bytes 14760000 | tf_op jit(solution)/shard_map/pallas_call | solution.py:405
  100.9 3.6 %shard_map.192 = (f32[4,32,512]{2,1,0:T(8,128)S(1)}, f32[4,32,512]{2,1,0:T(8,128)S(1)}, f32[4,32,512]{2,1,0:T(8,128)S(1)}, f32[4,32,512]{2,1,0:T(8,128)S(1)}, s32[3]{0:T(128)S(1)}) custom-call(s32[3]{0:T(128)S(1)} %get-tuple-element.111.info, f32[16,32,512]{2,1,0:T(8,128)S(1)} %get-tuple-element.112.done, f32[6,32,512]{2,1,0:T(8,128)S(1)} %get-tuple-element.113.top, ...), custom_call_target="tpu_custom_call" | custom-call | flops 4035500 | bytes 12915000 | tf_op jit(solution)/shard_map/pallas_call | solution.py:345
  104.6 2.0 %collective-permute-start.29 = (f32[4,32,512]{2,1,0:T(8,128)S(1)}, f32[4,32,512]{2,1,0:T(8,128)S(1)}, u32[]{:S(2)}, u32[]{:S(2)}) collective-permute-start(f32[4,32,512]{2,1,0:T(8,128)S(1)} %get-tuple-element.123), channel_id=1, source_target_pairs={{0,2},{2,0},{4,6},{6,4},{8,10},{10,8},{12,14},{14,12},{16,18},{18,... | collective-permute-start | bytes 786440 | tf_op jit(solution)/shard_map/ppermute | solution.py:443
  108.3 3.5 %shard_map.193 = (f32[2,512,512]{2,1,0:T(8,128)S(1)}, f32[2,512,512]{2,1,0:T(8,128)S(1)}, s32[3]{0:T(128)S(1)}) custom-call(s32[3]{0:T(128)S(1)} %get-tuple-element.115.info, f32[4,32,512]{2,1,0:T(8,128)S(1)} %get-tuple-element.116.refs_0_, f32[4,32,512]{2,1,0:T(8,128)S(1)} %collective-permute-done.26.refs_1_, ...), custom_call_target="tpu_custom_call" | custom-call | flops 4612000 | bytes 14760000 | tf_op jit(solution)/shard_map/pallas_call | solution.py:405
  111.8 2.6 %collective-permute-done.30.refs_2_ = f32[4,32,512]{2,1,0:T(8,128)S(1)} collective-permute-done((f32[4,32,512]{2,1,0:T(8,128)S(1)}, f32[4,32,512]{2,1,0:T(8,128)S(1)}, u32[]{:S(2)}, u32[]{:S(2)}) %collective-permute-start.30) | collective-permute-done | bytes 262176 | tf_op jit(solution)/shard_map/ppermute | solution.py:443
  114.5 5.8 %collective-permute-done.31.refs_3_ = f32[4,32,512]{2,1,0:T(8,128)S(1)} collective-permute-done((f32[4,32,512]{2,1,0:T(8,128)S(1)}, f32[4,32,512]{2,1,0:T(8,128)S(1)}, u32[]{:S(2)}, u32[]{:S(2)}) %collective-permute-start.31) | collective-permute-done | bytes 262176 | tf_op jit(solution)/shard_map/ppermute | solution.py:443
  120.2 4.1 %shard_map.194 = (f32[2,512,1024]{2,1,0:T(8,128)}, s32[3]{0:T(128)}) custom-call(s32[3]{0:T(128)S(1)} %get-tuple-element.121.info, f32[4,32,512]{2,1,0:T(8,128)S(1)} %get-tuple-element.122.refs_0_, f32[4,32,512]{2,1,0:T(8,128)S(1)} %collective-permute-done.29.refs_1_, f32[4,32,512]{2,1,0:T(8,128)S(1)} %collective-permute-done.30.refs_2_, ...), custom_call_target="tpu_custom_call" | custom-call | flops 4612000 | bytes 14760000 | tf_op jit(solution)/shard_map/pallas_call | solution.py:405
  (79 shorter events, 29.0 us)
Async XLA Ops:
  9.6 11.4 %collective-permute-start.1 = (f32[4,32,512]{2,1,0:T(8,128)S(1)}, f32[4,32,512]{2,1,0:T(8,128)S(1)}, u32[]{:S(2)}, u32[]{:S(2)}) collective-permute-start(f32[4,32,512]{2,1,0:T(8,128)S(1)} %get-tuple-element.71), channel_id=1, source_target_pairs={{0,4},{2,6},{4,0},{6,2},{8,12},{10,14},{12,8},{14,10},{16,20},{18,... | collective-permute-start | bytes 786440 | tf_op jit(solution)/shard_map/ppermute | solution.py:443
  10.9 12.9 %collective-permute-start.2 = (f32[4,32,512]{2,1,0:T(8,128)S(1)}, f32[4,32,512]{2,1,0:T(8,128)S(1)}, u32[]{:S(2)}, u32[]{:S(2)}) collective-permute-start(f32[4,32,512]{2,1,0:T(8,128)S(1)} %get-tuple-element.72), channel_id=1, source_target_pairs={{0,6},{2,4},{4,2},{6,0},{8,14},{10,12},{12,10},{14,8},{16,22},{18,... | collective-permute-start | bytes 786440 | tf_op jit(solution)/shard_map/ppermute | solution.py:443
  11.3 22.5 %collective-permute-start.3 = (f32[4,32,512]{2,1,0:T(8,128)S(1)}, f32[4,32,512]{2,1,0:T(8,128)S(1)}, u32[]{:S(2)}, u32[]{:S(2)}) collective-permute-start(f32[4,32,512]{2,1,0:T(8,128)S(1)} %get-tuple-element.75), channel_id=1, source_target_pairs={{0,2},{2,0},{4,6},{6,4},{8,10},{10,8},{12,14},{14,12},{16,18},{18,... | collective-permute-start | bytes 786440 | tf_op jit(solution)/shard_map/ppermute | solution.py:443
  11.5 22.5 %collective-permute-start.4 = (f32[4,32,512]{2,1,0:T(8,128)S(1)}, f32[4,32,512]{2,1,0:T(8,128)S(1)}, u32[]{:S(2)}, u32[]{:S(2)}) collective-permute-start(f32[4,32,512]{2,1,0:T(8,128)S(1)} %get-tuple-element.76), channel_id=1, source_target_pairs={{0,4},{2,6},{4,0},{6,2},{8,12},{10,14},{12,8},{14,10},{16,20},{18,... | collective-permute-start | bytes 786440 | tf_op jit(solution)/shard_map/ppermute | solution.py:443
  12.7 22.5 %collective-permute-start.5 = (f32[4,32,512]{2,1,0:T(8,128)S(1)}, f32[4,32,512]{2,1,0:T(8,128)S(1)}, u32[]{:S(2)}, u32[]{:S(2)}) collective-permute-start(f32[4,32,512]{2,1,0:T(8,128)S(1)} %get-tuple-element.77), channel_id=1, source_target_pairs={{0,6},{2,4},{4,2},{6,0},{8,14},{10,12},{12,10},{14,8},{16,22},{18,... | collective-permute-start | bytes 786440 | tf_op jit(solution)/shard_map/ppermute | solution.py:443
  26.7 21.3 %collective-permute-start.7 = (f32[6,32,512]{2,1,0:T(8,128)S(1)}, f32[6,32,512]{2,1,0:T(8,128)S(1)}, u32[]{:S(2)}, u32[]{:S(2)}) collective-permute-start(f32[6,32,512]{2,1,0:T(8,128)S(1)} %get-tuple-element.80.top), channel_id=1, source_target_pairs={{8,0},{10,2},{12,4},{14,6},{16,8},{18,10},{20,12},{22,14},{24,16},... | collective-permute-start | bytes 1179656 | tf_op jit(solution)/shard_map/ppermute | solution.py:461
  31.9 18.0 %collective-permute-start.6 = (f32[6,32,512]{2,1,0:T(8,128)S(1)}, f32[6,32,512]{2,1,0:T(8,128)S(1)}, u32[]{:S(2)}, u32[]{:S(2)}) collective-permute-start(f32[6,32,512]{2,1,0:T(8,128)S(1)} %get-tuple-element.81.bottom), channel_id=1, source_target_pairs={{0,8},{2,10},{4,12},{6,14},{8,16},{10,18},{12,20},{14,22},{16,24},... | collective-permute-start | bytes 1179656 | tf_op jit(solution)/shard_map/ppermute | solution.py:460
  34.0 11.1 %collective-permute-start.9 = (f32[4,32,512]{2,1,0:T(8,128)S(1)}, f32[4,32,512]{2,1,0:T(8,128)S(1)}, u32[]{:S(2)}, u32[]{:S(2)}) collective-permute-start(f32[4,32,512]{2,1,0:T(8,128)S(1)} %get-tuple-element.85), channel_id=1, source_target_pairs={{0,4},{2,6},{4,0},{6,2},{8,12},{10,14},{12,8},{14,10},{16,20},{18,... | collective-permute-start | bytes 786440 | tf_op jit(solution)/shard_map/ppermute | solution.py:443
  35.3 12.7 %collective-permute-start.10 = (f32[4,32,512]{2,1,0:T(8,128)S(1)}, f32[4,32,512]{2,1,0:T(8,128)S(1)}, u32[]{:S(2)}, u32[]{:S(2)}) collective-permute-start(f32[4,32,512]{2,1,0:T(8,128)S(1)} %get-tuple-element.86), channel_id=1, source_target_pairs={{0,6},{2,4},{4,2},{6,0},{8,14},{10,12},{12,10},{14,8},{16,22},{18,... | collective-permute-start | bytes 786440 | tf_op jit(solution)/shard_map/ppermute | solution.py:443
  39.1 25.8 %collective-permute-start.12 = (f32[6,32,512]{2,1,0:T(8,128)S(1)}, f32[6,32,512]{2,1,0:T(8,128)S(1)}, u32[]{:S(2)}, u32[]{:S(2)}) collective-permute-start(f32[6,32,512]{2,1,0:T(8,128)S(1)} %get-tuple-element.89.top), channel_id=1, source_target_pairs={{8,0},{10,2},{12,4},{14,6},{16,8},{18,10},{20,12},{22,14},{24,16},... | collective-permute-start | bytes 1179656 | tf_op jit(solution)/shard_map/ppermute | solution.py:461
  45.1 21.8 %collective-permute-start.11 = (f32[6,32,512]{2,1,0:T(8,128)S(1)}, f32[6,32,512]{2,1,0:T(8,128)S(1)}, u32[]{:S(2)}, u32[]{:S(2)}) collective-permute-start(f32[6,32,512]{2,1,0:T(8,128)S(1)} %get-tuple-element.90.bottom), channel_id=1, source_target_pairs={{0,8},{2,10},{4,12},{6,14},{8,16},{10,18},{12,20},{14,22},{16,24},... | collective-permute-start | bytes 1179656 | tf_op jit(solution)/shard_map/ppermute | solution.py:460
  50.0 13.0 %collective-permute-start.15 = (f32[4,32,512]{2,1,0:T(8,128)S(1)}, f32[4,32,512]{2,1,0:T(8,128)S(1)}, u32[]{:S(2)}, u32[]{:S(2)}) collective-permute-start(f32[4,32,512]{2,1,0:T(8,128)S(1)} %get-tuple-element.95), channel_id=1, source_target_pairs={{0,6},{2,4},{4,2},{6,0},{8,14},{10,12},{12,10},{14,8},{16,22},{18,... | collective-permute-start | bytes 786440 | tf_op jit(solution)/shard_map/ppermute | solution.py:443
  55.6 16.9 %collective-permute-start.16 = (f32[4,32,512]{2,1,0:T(8,128)S(1)}, f32[4,32,512]{2,1,0:T(8,128)S(1)}, u32[]{:S(2)}, u32[]{:S(2)}) collective-permute-start(f32[4,32,512]{2,1,0:T(8,128)S(1)} %get-tuple-element.98), channel_id=1, source_target_pairs={{0,2},{2,0},{4,6},{6,4},{8,10},{10,8},{12,14},{14,12},{16,18},{18,... | collective-permute-start | bytes 786440 | tf_op jit(solution)/shard_map/ppermute | solution.py:443
  58.7 23.9 %collective-permute-start.20 = (f32[6,32,512]{2,1,0:T(8,128)S(1)}, f32[6,32,512]{2,1,0:T(8,128)S(1)}, u32[]{:S(2)}, u32[]{:S(2)}) collective-permute-start(f32[6,32,512]{2,1,0:T(8,128)S(1)} %get-tuple-element.103.top), channel_id=1, source_target_pairs={{8,0},{10,2},{12,4},{14,6},{16,8},{18,10},{20,12},{22,14},{24,16},... | collective-permute-start | bytes 1179656 | tf_op jit(solution)/shard_map/ppermute | solution.py:461
  63.0 20.9 %collective-permute-start.19 = (f32[6,32,512]{2,1,0:T(8,128)S(1)}, f32[6,32,512]{2,1,0:T(8,128)S(1)}, u32[]{:S(2)}, u32[]{:S(2)}) collective-permute-start(f32[6,32,512]{2,1,0:T(8,128)S(1)} %get-tuple-element.104.bottom), channel_id=1, source_target_pairs={{0,8},{2,10},{4,12},{6,14},{8,16},{10,18},{12,20},{14,22},{16,24},... | collective-permute-start | bytes 1179656 | tf_op jit(solution)/shard_map/ppermute | solution.py:460
  66.9 13.7 %collective-permute-start.18 = (f32[4,32,512]{2,1,0:T(8,128)S(1)}, f32[4,32,512]{2,1,0:T(8,128)S(1)}, u32[]{:S(2)}, u32[]{:S(2)}) collective-permute-start(f32[4,32,512]{2,1,0:T(8,128)S(1)} %get-tuple-element.100), channel_id=1, source_target_pairs={{0,6},{2,4},{4,2},{6,0},{8,14},{10,12},{12,10},{14,8},{16,22},{18,... | collective-permute-start | bytes 786440 | tf_op jit(solution)/shard_map/ppermute | solution.py:443
  72.5 20.2 %collective-permute-start.21 = (f32[4,32,512]{2,1,0:T(8,128)S(1)}, f32[4,32,512]{2,1,0:T(8,128)S(1)}, u32[]{:S(2)}, u32[]{:S(2)}) collective-permute-start(f32[4,32,512]{2,1,0:T(8,128)S(1)} %get-tuple-element.107), channel_id=1, source_target_pairs={{0,2},{2,0},{4,6},{6,4},{8,10},{10,8},{12,14},{14,12},{16,18},{18,... | collective-permute-start | bytes 786440 | tf_op jit(solution)/shard_map/ppermute | solution.py:443
  75.6 25.3 %collective-permute-start.25 = (f32[6,32,512]{2,1,0:T(8,128)S(1)}, f32[6,32,512]{2,1,0:T(8,128)S(1)}, u32[]{:S(2)}, u32[]{:S(2)}) collective-permute-start(f32[6,32,512]{2,1,0:T(8,128)S(1)} %get-tuple-element.113.top), channel_id=1, source_target_pairs={{8,0},{10,2},{12,4},{14,6},{16,8},{18,10},{20,12},{22,14},{24,16},... | collective-permute-start | bytes 1179656 | tf_op jit(solution)/shard_map/ppermute | solution.py:461
  80.6 20.3 %collective-permute-start.24 = (f32[6,32,512]{2,1,0:T(8,128)S(1)}, f32[6,32,512]{2,1,0:T(8,128)S(1)}, u32[]{:S(2)}, u32[]{:S(2)}) collective-permute-start(f32[6,32,512]{2,1,0:T(8,128)S(1)} %get-tuple-element.114.bottom), channel_id=1, source_target_pairs={{0,8},{2,10},{4,12},{6,14},{8,16},{10,18},{12,20},{14,22},{16,24},... | collective-permute-start | bytes 1179656 | tf_op jit(solution)/shard_map/ppermute | solution.py:460
  83.8 13.7 %collective-permute-start.23 = (f32[4,32,512]{2,1,0:T(8,128)S(1)}, f32[4,32,512]{2,1,0:T(8,128)S(1)}, u32[]{:S(2)}, u32[]{:S(2)}) collective-permute-start(f32[4,32,512]{2,1,0:T(8,128)S(1)} %get-tuple-element.109), channel_id=1, source_target_pairs={{0,6},{2,4},{4,2},{6,0},{8,14},{10,12},{12,10},{14,8},{16,22},{18,... | collective-permute-start | bytes 786440 | tf_op jit(solution)/shard_map/ppermute | solution.py:443
  92.7 13.9 %collective-permute-start.26 = (f32[4,32,512]{2,1,0:T(8,128)S(1)}, f32[4,32,512]{2,1,0:T(8,128)S(1)}, u32[]{:S(2)}, u32[]{:S(2)}) collective-permute-start(f32[4,32,512]{2,1,0:T(8,128)S(1)} %get-tuple-element.117), channel_id=1, source_target_pairs={{0,2},{2,0},{4,6},{6,4},{8,10},{10,8},{12,14},{14,12},{16,18},{18,... | collective-permute-start | bytes 786440 | tf_op jit(solution)/shard_map/ppermute | solution.py:443
  92.8 15.5 %collective-permute-start.27 = (f32[4,32,512]{2,1,0:T(8,128)S(1)}, f32[4,32,512]{2,1,0:T(8,128)S(1)}, u32[]{:S(2)}, u32[]{:S(2)}) collective-permute-start(f32[4,32,512]{2,1,0:T(8,128)S(1)} %get-tuple-element.118), channel_id=1, source_target_pairs={{0,4},{2,6},{4,0},{6,2},{8,12},{10,14},{12,8},{14,10},{16,20},{18,... | collective-permute-start | bytes 786440 | tf_op jit(solution)/shard_map/ppermute | solution.py:443
  97.5 10.8 %collective-permute-start.28 = (f32[4,32,512]{2,1,0:T(8,128)S(1)}, f32[4,32,512]{2,1,0:T(8,128)S(1)}, u32[]{:S(2)}, u32[]{:S(2)}) collective-permute-start(f32[4,32,512]{2,1,0:T(8,128)S(1)} %get-tuple-element.119), channel_id=1, source_target_pairs={{0,6},{2,4},{4,2},{6,0},{8,14},{10,12},{12,10},{14,8},{16,22},{18,... | collective-permute-start | bytes 786440 | tf_op jit(solution)/shard_map/ppermute | solution.py:443
  106.6 13.7 %collective-permute-start.31 = (f32[4,32,512]{2,1,0:T(8,128)S(1)}, f32[4,32,512]{2,1,0:T(8,128)S(1)}, u32[]{:S(2)}, u32[]{:S(2)}) collective-permute-start(f32[4,32,512]{2,1,0:T(8,128)S(1)} %get-tuple-element.125), channel_id=1, source_target_pairs={{0,6},{2,4},{4,2},{6,0},{8,14},{10,12},{12,10},{14,8},{16,22},{18,... | collective-permute-start | bytes 786440 | tf_op jit(solution)/shard_map/ppermute | solution.py:443
  (20 other events, 212.8 us)

commit v2 on v1

--- a/solution.py
+++ b/solution.py
@@ -16,11 +16,13 @@
 GANG = 4
 SERIES = 2 * SUBSTEPS
 LANES = 128
+WIDE = 256
 VMEM_LIMIT = 20 * 1024 * 1024
 CHUNKS = (((0, 0, 4),), ((0, 4, 4),), ((1, 0, 4),), ((1, 4, 4),))
-MEMBER, ABOVE, BELOW = range(3)
-SCALARS = 3
-ORDER = ("D1", "D3", "E0", "E1", "C0", "E2", "C1", "E3", "I0", "C2", "I1", "C3", "I2", "I3")
+MEMBER, ABOVE, BELOW, ODD = range(4)
+SCALARS = 4
+DIRECT_OUT, DIRECT_BACK = (0, 1, 2), (0, 1, 2, 3)
+ORDER = ("D1", "D3", "E0", "E1", "R3", "C0", "E2", "C1", "E3", "I0", "C2", "I1", "C3", "I2", "I3")
 
 
 def pieces_of(chunk, per_parity):
@@ -58,6 +60,37 @@
     return dot(left[0], right[0]) + (dot(left[0], right[1]) + dot(left[1], right[0]))
 
 
+def sent_blocks(refs):
+    if len(refs) == GANG:
+        return list(refs)
+    own, mates, pair = refs
+    return [own, mates.at[0], pair.at[0], mates.at[1]]
+
+
+def received_blocks(refs):
+    if len(refs) == GANG:
+        return list(refs)
+    own, mates, pair = refs
+    return [own, mates.at[0], pair.at[0], pair.at[1]]
+
+
+def part_arrays(shape, block, over):
+    doubled = (False, True, True) if over else (False,) * GANG
+    shapes = [
+        jax.ShapeDtypeStruct((2,) + shape if two else shape, jnp.float32) for two in doubled
+    ]
+    specs = [
+        pl.BlockSpec(((2,) if two else ()) + block, lambda i, two=two: (0,) * (2 + two) + (i,))
+        for two in doubled
+    ]
+    return shapes, specs
+
+
+def split(refs, counts):
+    places = [sum(counts[:n]) for n in range(len(counts) + 1)]
+    return [list(refs[a:b]) for a, b in zip(places, places[1:])]
+
+
 def partner_rows(table, member, count):
     rows = [
         table[pl.ds(pl.multiple_of((member ^ d) * 2 * count, 2 * count), 2 * count)]
@@ -71,11 +104,37 @@
         token[place] = info[place]
 
 
-def forward_kernel(chunks, per_parity, info, freq, depth, pressure, *refs):
+def steepened_and_folded(wave, squared, parity):
+    half = wave.shape[1] // 2
+    sign = -1.0 if parity else 1.0
+
+    def fold(values, at):
+        return values[:, at : at + LANES] + sign * values[:, half + at : half + at + LANES]
+
+    lane = lax.broadcasted_iota(jnp.int32, (wave.shape[0], LANES), 1)
+    pieces = [fold(squared, at) for at in range(0, half, LANES)]
+    last_early = sign * squared[:, half - LANES : half]
+    first_late = squared[:, half : half + LANES]
+    before = [pltpu.roll(piece, 1, 1) for piece in [last_early] + pieces]
+    after = [pltpu.roll(piece, LANES - 1, 1) for piece in pieces + [first_late]]
+    steep = [
+        fold(wave, LANES * n)
+        + WAVE_BREAKING
+        * 0.25
+        * (
+            jnp.where(lane == LANES - 1, after[n + 1], after[n])
+            - jnp.where(lane == 0, before[n], before[n + 1])
+        )
+        for n in range(half // LANES)
+    ]
+    return jnp.concatenate(steep, axis=1)
+
+
+def forward_kernel(chunks, counts, per_parity, info, freq, depth, pressure, *refs):
     n_tables = 2 * sum(len(pieces) for pieces in chunks)
     tables = iter(refs[:n_tables])
-    n_outs = GANG * len(chunks)
-    outs = refs[n_tables : n_tables + n_outs]
+    n_outs = sum(counts)
+    outs = [sent_blocks(some) for some in split(refs[n_tables:], counts)]
     token = refs[n_tables + n_outs]
     factors = refs[n_tables + n_outs + 1 :]
     rows, block, n_time = pressure.shape
@@ -111,15 +170,10 @@
                     factors[2 * chunk + part][d] = jnp.broadcast_to(column, (share, block))
 
     wave = pressure[...].reshape(rows * block, n_time)
-    lane = lax.broadcasted_iota(jnp.int32, wave.shape, 1)
     squared = wave * wave
-    after = jnp.where(lane == n_time - 1, 0.0, pltpu.roll(squared, n_time - 1, 1))
-    before = jnp.where(lane == 0, 0.0, pltpu.roll(squared, 1, 1))
-    steep = wave + WAVE_BREAKING * 0.25 * (after - before)
-    early, late = steep[:, :half], steep[:, half:]
     folded = {}
     for parity in sorted(set(piece[0] for pieces in chunks for piece in pieces)):
-        folded[parity] = halves(early - late if parity else early + late)
+        folded[parity] = halves(steepened_and_folded(wave, squared, parity))
     for chunk, pieces in enumerate(chunks):
         factor_re, factor_im = factors[2 * chunk : 2 * chunk + 2]
         offset = 0
@@ -130,7 +184,7 @@
             for d in range(GANG):
                 here = slice(offset, offset + count)
                 fr, fi = factor_re[d, here], factor_im[d, here]
-                out = outs[GANG * chunk + d]
+                out = outs[chunk][d]
                 for row in range(rows):
                     across = slice(row * block, (row + 1) * block)
                     real, imag = spectrum[d, 0, :, across], spectrum[d, 1, :, across]
@@ -159,18 +213,20 @@
     return pltpu.with_memory_space_constraint(array, pltpu.HBM)
 
 
-def forward_chunks(info, pressure, relax_freq, relax_depth, tables, chunks, per_parity):
+def forward_chunks(info, pressure, relax_freq, relax_depth, tables, chunks, over, per_parity):
     rows, width, n_time = pressure.shape
     flat = [in_hbm(t) for chunk in tables for pair in chunk for t in pair]
     out_specs, out_shape, scratch = [], [], []
-    for pieces in chunks:
+    counts = [3 if one else GANG for one in over]
+    for pieces, one in zip(chunks, over):
         share = sum(piece[2] for piece in pieces)
-        block = pl.BlockSpec((2 * rows, share, LANES), lambda i: (0, 0, i))
-        out_specs += [block] * GANG
-        out_shape += [jax.ShapeDtypeStruct((2 * rows, share, width), jnp.float32)] * GANG
+        shape = (2 * rows, share)
+        shapes, specs = part_arrays(shape + (width,), shape + (LANES,), one)
+        out_specs += specs
+        out_shape += shapes
         scratch += [pltpu.VMEM((GANG, share, LANES), jnp.float32)] * 2
     outs = pl.pallas_call(
-        functools.partial(forward_kernel, chunks, per_parity),
+        functools.partial(forward_kernel, chunks, counts, per_parity),
         grid=(width // LANES,),
         in_specs=[scalars()] * 3
         + [pl.BlockSpec((rows, LANES, n_time), lambda i: (0, i, 0))]
@@ -180,22 +236,26 @@
         scratch_shapes=scratch,
         compiler_params=pltpu.CompilerParams(vmem_limit_bytes=VMEM_LIMIT),
         cost_estimate=cost(2 + 2 * len(chunks)),
-    )(info, relax_freq, relax_depth, in_hbm(pressure), *flat)
-    return outs[-1], [outs[GANG * c : GANG * c + GANG] for c in range(len(chunks))]
-
-
-def bin_rates(pieces, per_parity, member, half_bins, tile, shape):
+    )(info, in_hbm(relax_freq), in_hbm(relax_depth), in_hbm(pressure), *flat)
+    return outs[-1], split(outs, counts)
+
+
+def tile_of(share):
+    return 16 if share % 16 == 0 else 8
+
+
+def bin_rates(pieces, per_parity, member, half_bins, place, shape):
     start, offset = 0, 0
     for parity, first, count in pieces:
-        here = 2 * (member * per_parity + first + 8 * tile - offset) + parity
-        start = jnp.where(8 * tile >= offset, here, start)
+        here = 2 * (member * per_parity + first + place - offset) + parity
+        start = jnp.where(place >= offset, here, start)
         offset += count
     bins = (start + 2 * lax.broadcasted_iota(jnp.int32, shape, 0)).astype(jnp.float32)
     return RATE_TOP * jnp.minimum(bins, 1.0) * jnp.minimum(1.0, half_bins / jnp.maximum(bins, 1.0))
 
 
-def lateral(width):
-    lane = lax.broadcasted_iota(jnp.int32, (8, LANES), 1)
+def lateral(height, width):
+    lane = lax.broadcasted_iota(jnp.int32, (height, LANES), 1)
     first_lane, last_lane = lane == 0, lane == LANES - 1
 
     def apply(center):
@@ -214,14 +274,15 @@
 
 
 def evolve_kernel(pieces, per_parity, half_bins, info, *refs):
-    parts = refs[:GANG]
-    done, top, bottom, token, real, imag = refs[GANG:]
-    member = info[MEMBER]
+    *parts, done, even_sent, odd_sent, token, real, imag = refs
+    parts = received_blocks(parts)
+    member, is_odd = info[MEMBER], info[ODD] != 0
     pass_on(info, token)
     units, share, width = parts[0].shape
     rows = units // 2
     count = GANG * rows
-    side = lateral(width)
+    height = tile_of(share)
+    side = lateral(height, width)
 
     def advance(field, other, scale):
         before, center = None, other[0]
@@ -236,11 +297,14 @@
             before, center = center, after
 
     def keep(place, here, field):
-        top[place, here], bottom[place, here] = field[0], field[count - 1]
+        top, bottom = field[0], field[count - 1]
+        even_sent[place, here] = jnp.where(is_odd, top, bottom)
+        odd_sent[place, here] = jnp.where(is_odd, bottom, top)
 
     def tile(index, carry):
-        here = pl.ds(pl.multiple_of(8 * index, 8), 8)
-        rate = bin_rates(pieces, per_parity, member, half_bins, index, (8, width))
+        place = pl.multiple_of(height * index, height)
+        here = pl.ds(place, height)
+        rate = bin_rates(pieces, per_parity, member, half_bins, place, (height, width))
         for d in range(GANG):
             first = (member ^ d) * rows
             for row in range(rows):
@@ -256,7 +320,7 @@
             done[count + row, here] = imag[row]
         return carry
 
-    lax.fori_loop(0, share // 8, tile, 0)
+    lax.fori_loop(0, share // height, tile, 0)
 
 
 def in_vmem(count):
@@ -266,11 +330,11 @@
 def evolve_chunk(info, parts, pieces, per_parity, half_bins):
     units, share, width = parts[0].shape
     count = GANG * units // 2
-    scratch = pltpu.VMEM((count, 8, width), jnp.float32)
+    scratch = pltpu.VMEM((count, tile_of(share), width), jnp.float32)
     sizes = (2 * count, SERIES, SERIES)
     return pl.pallas_call(
         functools.partial(evolve_kernel, pieces, per_parity, half_bins),
-        in_specs=[scalars()] + in_vmem(GANG),
+        in_specs=[scalars()] + in_vmem(len(parts)),
         out_specs=in_vmem(3) + [scalars()],
         out_shape=[jax.ShapeDtypeStruct((n, share, width), jnp.float32) for n in sizes]
         + [token_shape()],
@@ -280,15 +344,18 @@
     )(info, *parts)
 
 
-def correct_kernel(pieces, per_parity, half_bins, info, done, top, bottom, above, below, *refs):
-    outs = refs[:GANG]
-    token, total, near_re, near_im, far_re, far_im = refs[GANG:]
-    member = info[MEMBER]
+def correct_kernel(
+    pieces, per_parity, half_bins, info, done, even_sent, odd_sent, even_got, odd_got, *refs
+):
+    *outs, token, total = refs[:-8]
+    outs, strips = sent_blocks(outs), refs[-8:]
+    member, is_odd = info[MEMBER], info[ODD] != 0
     pass_on(info, token)
     units, share, width = done.shape
     count = units // 2
     rows = count // GANG
-    side = lateral(width)
+    height = tile_of(share)
+    side = lateral(height, width)
 
     def advance(field, source, edge, scale, half_step, deep):
         before, center = edge, source[0] if half_step > 0 else None
@@ -304,26 +371,34 @@
             before, center = center, after
 
     def tile(index, carry):
-        here = pl.ds(pl.multiple_of(8 * index, 8), 8)
-        rate = bin_rates(pieces, per_parity, member, half_bins, index, (8, width))
+        place = pl.multiple_of(height * index, height)
+        here = pl.ds(place, height)
+        rate = bin_rates(pieces, per_parity, member, half_bins, place, (height, width))
         for unit in range(units):
             total[unit] = done[unit, here]
-        for own, other, flag, order in (
-            (top, above, info[ABOVE], range(count)),
-            (bottom, below, info[BELOW], range(count - 1, -1, -1)),
-        ):
-            rate_far = rate * flag.astype(jnp.float32)
-            for half_step in range(SERIES):
-                own_edge, far_edge = own[half_step, here], other[half_step, here]
-                near, near_from = (near_re, near_im) if half_step % 2 == 0 else (near_im, near_re)
-                back, back_from = (far_re, far_im) if half_step % 2 == 0 else (far_im, far_re)
-                sign = 1.0 if half_step % 2 else -1.0
+        even, odd = (even_sent, even_got), (odd_sent, odd_got)
+        edges = (
+            (even, odd, info[ABOVE], strips[:4], range(count)),
+            (odd, even, info[BELOW], strips[4:], range(count - 1, -1, -1)),
+        )
+        for half_step in range(SERIES):
+            for if_odd, if_even, flag, (near_re, near_im, far_re, far_im), _ in edges:
+                own_edge, far_edge = (
+                    jnp.where(is_odd, one[half_step, here], two[half_step, here])
+                    for one, two in zip(if_odd, if_even)
+                )
+                of_imag = half_step % 2
+                near, near_from = (near_im, near_re) if of_imag else (near_re, near_im)
+                far, far_from = (far_im, far_re) if of_imag else (far_re, far_im)
+                scale = rate if of_imag else -rate
                 if half_step > 0:
                     own_edge = own_edge + near_from[0]
-                    far_edge = far_edge + back_from[0]
-                reach = min(half_step + 1, SERIES - 1 - half_step)
-                advance(near, near_from, far_edge, sign * rate, half_step, half_step + 1)
-                advance(back, back_from, own_edge, sign * rate_far, half_step, reach)
+                    far_edge = far_edge + far_from[0]
+                back = min(half_step + 1, SERIES - 1 - half_step)
+                advance(near, near_from, far_edge, scale, half_step, half_step + 1)
+                scale = scale * flag.astype(jnp.float32)
+                advance(far, far_from, own_edge, scale, half_step, back)
+        for _, _, _, (near_re, near_im, _, _), order in edges:
             for row in range(SERIES - 1):
                 total[order[row]] = total[order[row]] + near_re[row]
             for row in range(SERIES):
@@ -335,32 +410,51 @@
                 outs[d][rows + row, here] = total[count + first + row]
         return carry
 
-    lax.fori_loop(0, share // 8, tile, 0)
-
-
-def correct_chunk(info, state, pieces, per_parity, half_bins):
+    lax.fori_loop(0, share // height, tile, 0)
+
+
+def correct_chunk(info, state, over, pieces, per_parity, half_bins):
     units, share, width = state[0].shape
-    shape = jax.ShapeDtypeStruct((units // GANG, share, width), jnp.float32)
-    strip = pltpu.VMEM((SERIES, 8, width), jnp.float32)
+    shape = (units // GANG, share, width)
+    shapes = part_arrays(shape, shape, over)[0]
+    strip = pltpu.VMEM((SERIES, tile_of(share), width), jnp.float32)
     return pl.pallas_call(
         functools.partial(correct_kernel, pieces, per_parity, half_bins),
         in_specs=[scalars()] + in_vmem(5),
-        out_specs=in_vmem(GANG) + [scalars()],
-        out_shape=[shape] * GANG + [token_shape()],
-        scratch_shapes=[pltpu.VMEM((units, 8, width), jnp.float32)] + [strip] * 4,
+        out_specs=in_vmem(len(shapes)) + [scalars()],
+        out_shape=shapes + [token_shape()],
+        scratch_shapes=[pltpu.VMEM((units, tile_of(share), width), jnp.float32)] + [strip] * 8,
         compiler_params=pltpu.CompilerParams(vmem_limit_bytes=VMEM_LIMIT),
         cost_estimate=cost(3.5),
     )(info, *state)
 
 
-def inverse_kernel(chunks, held, last, info, *refs):
-    n_parts = GANG * len(chunks)
+def relay_kernel(info, mates, held, pair, token):
+    pair[1] = mates[1]
+    pass_on(info, token)
+
+
+def relay(info, mates, pair):
+    return pl.pallas_call(
+        relay_kernel,
+        in_specs=[scalars()] + in_vmem(2),
+        out_specs=in_vmem(1) + [scalars()],
+        out_shape=[jax.ShapeDtypeStruct(pair.shape, pair.dtype), token_shape()],
+        input_output_aliases={2: 0},
+        compiler_params=pltpu.CompilerParams(vmem_limit_bytes=VMEM_LIMIT),
+        cost_estimate=cost(0.5),
+    )(info, mates, pair)
+
+
+def inverse_kernel(chunks, counts, held, last, info, *refs):
+    n_parts = sum(counts)
     n_tables = 2 * sum(len(pieces) for pieces in chunks)
-    parts, tables = refs[:n_parts], iter(refs[n_parts : n_parts + n_tables])
+    parts = [received_blocks(some) for some in split(refs, counts)]
+    tables = iter(refs[n_parts : n_parts + n_tables])
     refs = refs[n_parts + n_tables :]
     prior, outs, token = dict(zip(held, refs)), refs[len(held) : -1], refs[-1]
     member = info[MEMBER]
-    rows, block = parts[0].shape[0] // 2, parts[0].shape[2]
+    rows, block = parts[0][0].shape[0] // 2, parts[0][0].shape[2]
     half = outs[0].shape[2] // 2 if last else outs[0].shape[2]
     pass_on(info, token)
     sums = {parity: prior[parity][...].reshape(rows * block, half) for parity in held}
@@ -371,7 +465,7 @@
             here = slice(offset, offset + count)
             packed = [
                 jnp.concatenate([part[n * rows + row, here] for row in range(rows)], axis=1)
-                for part in parts[GANG * chunk : GANG * chunk + GANG]
+                for part in parts[chunk]
                 for n in range(2)
             ]
             packed = jnp.concatenate(packed, axis=0).T
@@ -392,19 +486,21 @@
     flat = [t for chunk in tables for pair in chunk for t in pair]
     held = sorted(sums)
     fresh = sorted(set(held) | set(piece[0] for pieces in chunks for piece in pieces))
-    state = pl.BlockSpec((rows, LANES, half), lambda i: (0, i, 0))
+    state = pl.BlockSpec((rows, WIDE, half), lambda i: (0, i, 0))
     state_shape = jax.ShapeDtypeStruct((rows, width, half), jnp.float32)
     if last:
-        out_specs = [pl.BlockSpec((rows, LANES, 2 * half), lambda i: (0, i, 0))]
+        out_specs = [pl.BlockSpec((rows, WIDE, 2 * half), lambda i: (0, i, 0))]
         out_shape = [jax.ShapeDtypeStruct((rows, width, 2 * half), jnp.float32)]
     else:
         out_specs, out_shape = [state] * len(fresh), [state_shape] * len(fresh)
     in_specs = [scalars()]
+    counts = [len(chunk) for chunk in parts]
     for chunk in parts:
-        in_specs += [pl.BlockSpec(chunk[0].shape[:2] + (LANES,), lambda i: (0, 0, i))] * GANG
+        shape = chunk[0].shape
+        in_specs += part_arrays(shape, shape[:2] + (WIDE,), len(chunk) == 3)[1]
     outs = pl.pallas_call(
-        functools.partial(inverse_kernel, chunks, held, last),
-        grid=(width // LANES,),
+        functools.partial(inverse_kernel, chunks, counts, held, last),
+        grid=(width // WIDE,),
         in_specs=in_specs
         + [pl.BlockSpec(t.shape, lambda i: (0, 0)) for t in flat]
         + [state] * len(held),
@@ -431,16 +527,29 @@
         [(device(b, m), device(b, m ^ d)) for b in range(blocks) for m in range(GANG)]
         for d in range(GANG)
     ]
-    down = [(device(b, m), device(b + 1, m)) for b in range(blocks - 1) for m in range(GANG)]
-    up = [(target, source) for source, target in down]
+    pairs = [
+        [
+            (device(b + side, m), device(b + 1 - side, m))
+            for b in range(odd, blocks - 1, 2)
+            for m in range(GANG)
+            for side in range(2)
+        ]
+        for odd in range(2)
+    ]
 
     place = lax.axis_index("narrow") * wide + lax.axis_index("wide")
     block = place // GANG
-    info = [place % GANG, block > 0, block < blocks - 1]
+    info = [place % GANG, block > 0, block < blocks - 1, block % 2]
     info = jnp.stack([jnp.asarray(value, jnp.int32) for value in info])
 
-    def swap(parts):
-        return [parts[0]] + [lax.ppermute(parts[d], axes, swaps[d]) for d in range(1, GANG)]
+    def swap(values, d):
+        return lax.ppermute(values, axes, swaps[d])
+
+    def send(parts):
+        if len(parts) == GANG:
+            return [parts[0]] + [swap(parts[d], d) for d in range(1, GANG)]
+        own, mates, pair = parts
+        return [own, swap(mates, 1), pair]
 
     chunks = [pieces_of(chunk, per_parity) for chunk in CHUNKS]
     tables = [[transform_tables(piece, per_parity, n_time) for piece in c] for c in chunks]
@@ -453,16 +562,21 @@
         shape = (chunks[c], per_parity, half_bins)
         if kernel == "D":
             some, begun = slice(begun, c + 1), c + 1
-            info, parts = forward_chunks(info, *inputs, forward[some], chunks[some], per_parity)
-            held[some] = [swap(part) for part in parts]
+            over = [n not in DIRECT_OUT for n in range(some.start, some.stop)]
+            kind = (forward[some], chunks[some], over)
+            info, parts = forward_chunks(info, *inputs, *kind, per_parity)
+            held[some] = [send(part) for part in parts]
+        elif kernel == "R":
+            own, mates, pair = held[c]
+            pair, info = relay(info, mates, pair)
+            held[c] = [own, mates, swap(pair, 2)]
         elif kernel == "E":
-            done, top, bottom, info = evolve_chunk(info, held[c], *shape)
-            above = lax.ppermute(bottom, axes, down)
-            below = lax.ppermute(top, axes, up)
-            held[c] = (done, top, bottom, above, below)
+            done, *sent, info = evolve_chunk(info, held[c], *shape)
+            got = [lax.ppermute(values, axes, pairs[odd]) for odd, values in enumerate(sent)]
+            held[c] = (done, *sent, *got)
         elif kernel == "C":
-            *parts, info = correct_chunk(info, held[c], *shape)
-            held[c] = swap(parts)
+            *parts, info = correct_chunk(info, held[c], c not in DIRECT_BACK, *shape)
+            held[c] = send(parts)
         else:
             some, finished, last = slice(finished, c + 1), c + 1, c + 1 == len(chunks)
             info, sums = inverse_chunks(info, held[some], inverse[some], chunks[some], sums, last)

time: 125 us -> 128 us (1.024)
  waiting for transfers between devices: 17.4 us -> 43.1 us
  starting transfers between devices: 49.8 us -> 35.1 us
  Pallas kernels: 55.3 us -> 49.5 us
  local copies, waits for them, and re-layouts: 1.37 us -> 0.05 us
    ppermute x32 -> x31, waiting for transfers between devices: 17.4 us -> 43.1 us  [the longest x23 40.9 us: swap(): return lax.ppermute(values, axes, swaps[d])]
    ppermute x32 -> x31, starting transfers between devices: 49.8 us -> 35.1 us  [the longest x8 19.4 us: shards(): lax.ppermute(values, axes, pairs[odd])]
    pallas_call x4, Pallas kernels: 14.4 us -> 11.3 us  [correct_chunk(): pl.pallas_call(functools.partial(correct_kernel, pieces, per_parity, half...]
    pallas_call x6 -> x7, Pallas kernels: 29.1 us -> 26.5 us  [the longest x2 13.7 us: forward_chunks(): pl.pallas_call(functools.partial(forward_kernel, chunks, counts, per_pari...]
    unnamed x24 -> x16, local copies, waits for them, and re-layouts: 1.37 us -> 0.05 us
  transfers between devices with their start and end apart: 32 -> 31, of which waited for: 7 -> 11; matrix products, arithmetic and copies ran while one was open for 0% -> 0% of each run, Pallas kernels for 35% -> 31%
where the time goes in v2:
time: 128 us
  Pallas kernels  49.5 us (39%)
  waiting for transfers between devices  43.1 us (34%)
  starting transfers between devices  35.1 us (27%)
    ppermute x23, waiting for transfers between devices, swap(): return lax.ppermute(values, axes, swaps[d])  40.9 us
    ppermute x8, starting transfers between devices, shards(): lax.ppermute(values, axes, pairs[odd])  19.4 us
    ppermute x23, starting transfers between devices, swap(): return lax.ppermute(values, axes, swaps[d])  15.7 us
    pallas_call x2, Pallas kernels, forward_chunks(): pl.pallas_call(functools.partial(forward_kernel, chunks, counts, per_pari...  13.7 us
    pallas_call x4, Pallas kernels, inverse_chunks(): pl.pallas_call(functools.partial(inverse_kernel, chunks, counts, held, la...  11.7 us
    pallas_call x4, Pallas kernels, evolve_chunk(): pl.pallas_call(functools.partial(evolve_kernel, pieces, per_parity, half_...  11.6 us
    pallas_call x4, Pallas kernels, correct_chunk(): pl.pallas_call(functools.partial(correct_kernel, pieces, per_parity, half...  11.3 us
  transfers between devices with their start and end apart: 31, of which 11 were waited for; matrix products, arithmetic and copies ran while one was open for 0% of the time, Pallas kernels for 31%

profile of v2, /device:TPU:3, one launch (start us, length us, event | category | flops | bytes accessed | tf_op | source)
XLA Modules:
  0.0 128.2 jit_solution(10896150135854572317)
XLA Ops:
  0.1 6.8 %shard_map.181 = (f32[4,32,512]{2,1,0:T(8,128)S(1)}, f32[4,32,512]{2,1,0:T(8,128)S(1)}, f32[4,32,512]{2,1,0:T(8,128)S(1)}, f32[4,32,512]{2,1,0:T(8,128)S(1)}, f3...) custom-call(s32[4]{0:T(128)S(1)} %pad_add_fusion.info, ...), custom_call_target="tpu_custom_call" | custom-call | flops 6918000 | bytes 22140000 | tf_op jit(solution)/shard_map/pallas_call | solution.py:228
  10.8 6.9 %shard_map.182 = (f32[4,32,512]{2,1,0:T(8,128)S(1)}, f32[4,32,512]{2,1,0:T(8,128)S(1)}, f32[4,32,512]{2,1,0:T(8,128)S(1)}, f32[4,32,512]{2,1,0:T(8,128)S(1)}, f3...) custom-call(s32[4]{0:T(128)S(1)} %get-tuple-element.68.info, ...), custom_call_target="tpu_custom_call" | custom-call | flops 6918000 | bytes 22140000 | tf_op jit(solution)/shard_map/pallas_call | solution.py:228
  18.6 3.2 %collective-permute-done.2.refs_3_ = f32[4,32,512]{2,1,0:T(8,128)S(1)} collective-permute-done((f32[4,32,512]{2,1,0:T(8,128)S(1)}, f32[4,32,512]{2,1,0:T(8,128)S(1)}, u32[]{:S(2)}, u32[]{:S(2)}) %collective-permute-start.2) | collective-permute-done | bytes 262176 | tf_op jit(solution)/shard_map/ppermute | solution.py:546
  21.8 2.9 %shard_map.183 = (f32[16,32,512]{2,1,0:T(8,128)S(1)}, f32[6,32,512]{2,1,0:T(8,128)S(1)}, f32[6,32,512]{2,1,0:T(8,128)S(1)}, s32[4]{0:T(128)S(1)}) custom-call(s32[4]{0:T(128)S(1)} %get-tuple-element.69.info, f32[4,32,512]{2,1,0:T(8,128)S(1)} %get-tuple-element.70.refs_0_, f32[4,32,512]{2,1,0:T(8,128)S(1)} %collective-permute-done.refs_1_, ...), custom_call_target="tpu_custom_call" | custom-call | flops 3459000 | bytes 11070000 | tf_op jit(solution)/shard_map/pallas_call | solution.py:335
  26.1 4.0 %collective-permute-start.8 = (f32[6,32,512]{2,1,0:T(8,128)S(1)}, f32[6,32,512]{2,1,0:T(8,128)S(1)}, u32[]{:S(2)}, u32[]{:S(2)}) collective-permute-start(f32[6,32,512]{2,1,0:T(8,128)S(1)} %get-tuple-element.85.odd_sent), channel_id=1, source_target_pairs={{8,16},{16,8},{10,18},{18,10},{12,20},{20,12},{14,22},{22,14},{24,... | collective-permute-start | bytes 1179656 | tf_op jit(solution)/shard_map/ppermute | solution.py:575
  34.1 2.9 %shard_map.184 = (f32[16,32,512]{2,1,0:T(8,128)S(1)}, f32[6,32,512]{2,1,0:T(8,128)S(1)}, f32[6,32,512]{2,1,0:T(8,128)S(1)}, s32[4]{0:T(128)S(1)}) custom-call(s32[4]{0:T(128)S(1)} %get-tuple-element.74.info, f32[4,32,512]{2,1,0:T(8,128)S(1)} %get-tuple-element.75.refs_0_, f32[4,32,512]{2,1,0:T(8,128)S(1)} %collective-permute-done.3.refs_1_, ...), custom_call_target="tpu_custom_call" | custom-call | flops 3459000 | bytes 11070000 | tf_op jit(solution)/shard_map/pallas_call | solution.py:335
  38.4 4.0 %collective-permute-start.13 = (f32[6,32,512]{2,1,0:T(8,128)S(1)}, f32[6,32,512]{2,1,0:T(8,128)S(1)}, u32[]{:S(2)}, u32[]{:S(2)}) collective-permute-start(f32[6,32,512]{2,1,0:T(8,128)S(1)} %get-tuple-element.94.odd_sent), channel_id=1, source_target_pairs={{8,16},{16,8},{10,18},{18,10},{12,20},{20,12},{14,22},{22,14},{24,... | collective-permute-start | bytes 1179656 | tf_op jit(solution)/shard_map/ppermute | solution.py:575
  48.2 2.8 %shard_map.186 = (f32[4,32,512]{2,1,0:T(8,128)S(1)}, f32[4,32,512]{2,1,0:T(8,128)S(1)}, f32[4,32,512]{2,1,0:T(8,128)S(1)}, f32[4,32,512]{2,1,0:T(8,128)S(1)}, s32[4]{0:T(128)S(1)}) custom-call(s32[4]{0:T(128)S(1)} %get-tuple-element.82.info, f32[16,32,512]{2,1,0:T(8,128)S(1)} %get-tuple-element.83.done, f32[6,32,512]{2,1,0:T(8,128)S(1)} %get-tuple-element.84.even_sent, ...), custom_call_target="tpu_custom_call" | custom-call | flops 4035500 | bytes 12915000 | tf_op jit(solution)/shard_map/pallas_call | solution.py:421
  51.1 12.2 %collective-permute-done.11.refs_3_ = f32[4,32,512]{2,1,0:T(8,128)S(1)} collective-permute-done((f32[4,32,512]{2,1,0:T(8,128)S(1)}, f32[4,32,512]{2,1,0:T(8,128)S(1)}, u32[]{:S(2)}, u32[]{:S(2)}) %collective-permute-start.11) | collective-permute-done | bytes 262176 | tf_op jit(solution)/shard_map/ppermute | solution.py:546
  63.2 2.9 %shard_map.187 = (f32[16,32,512]{2,1,0:T(8,128)S(1)}, f32[6,32,512]{2,1,0:T(8,128)S(1)}, f32[6,32,512]{2,1,0:T(8,128)S(1)}, s32[4]{0:T(128)S(1)}) custom-call(s32[4]{0:T(128)S(1)} %get-tuple-element.86.info, f32[4,32,512]{2,1,0:T(8,128)S(1)} %get-tuple-element.87.refs_0_, f32[4,32,512]{2,1,0:T(8,128)S(1)} %collective-permute-done.9.refs_1_, ...), custom_call_target="tpu_custom_call" | custom-call | flops 3459000 | bytes 11070000 | tf_op jit(solution)/shard_map/pallas_call | solution.py:335
  66.4 3.9 %collective-permute-start.19 = (f32[6,32,512]{2,1,0:T(8,128)S(1)}, f32[6,32,512]{2,1,0:T(8,128)S(1)}, u32[]{:S(2)}, u32[]{:S(2)}) collective-permute-start(f32[6,32,512]{2,1,0:T(8,128)S(1)} %get-tuple-element.106.odd_sent), channel_id=1, source_target_pairs={{8,16},{16,8},{10,18},{18,10},{12,20},{20,12},{14,22},{22,14},{24,... | collective-permute-start | bytes 1179656 | tf_op jit(solution)/shard_map/ppermute | solution.py:575
  71.5 2.8 %shard_map.188 = (f32[4,32,512]{2,1,0:T(8,128)S(1)}, f32[4,32,512]{2,1,0:T(8,128)S(1)}, f32[4,32,512]{2,1,0:T(8,128)S(1)}, f32[4,32,512]{2,1,0:T(8,128)S(1)}, s32[4]{0:T(128)S(1)}) custom-call(s32[4]{0:T(128)S(1)} %get-tuple-element.91.info, f32[16,32,512]{2,1,0:T(8,128)S(1)} %get-tuple-element.92.done, f32[6,32,512]{2,1,0:T(8,128)S(1)} %get-tuple-element.93.even_sent, ...), custom_call_target="tpu_custom_call" | custom-call | flops 4035500 | bytes 12915000 | tf_op jit(solution)/shard_map/pallas_call | solution.py:421
  75.2 2.9 %shard_map.189 = (f32[16,32,512]{2,1,0:T(8,128)S(1)}, f32[6,32,512]{2,1,0:T(8,128)S(1)}, f32[6,32,512]{2,1,0:T(8,128)S(1)}, s32[4]{0:T(128)S(1)}) custom-call(s32[4]{0:T(128)S(1)} %get-tuple-element.95.info, f32[4,32,512]{2,1,0:T(8,128)S(1)} %get-tuple-element.96.refs_0_, f32[2,4,32,512]{3,2,1,0:T(8,128)S(1)} %collective-permute-done.6.mates.refs_1_, ...), custom_call_target="tpu_custom_call" | custom-call | flops 3459000 | bytes 11070000 | tf_op jit(solution)/shard_map/pallas_call | solution.py:335
  78.7 5.3 %collective-permute-done.17.refs_3_ = f32[4,32,512]{2,1,0:T(8,128)S(1)} collective-permute-done((f32[4,32,512]{2,1,0:T(8,128)S(1)}, f32[4,32,512]{2,1,0:T(8,128)S(1)}, u32[]{:S(2)}, u32[]{:S(2)}) %collective-permute-start.17) | collective-permute-done | bytes 262176 | tf_op jit(solution)/shard_map/ppermute | solution.py:546
  84.1 4.5 %collective-permute-start.24 = (f32[6,32,512]{2,1,0:T(8,128)S(1)}, f32[6,32,512]{2,1,0:T(8,128)S(1)}, u32[]{:S(2)}, u32[]{:S(2)}) collective-permute-start(f32[6,32,512]{2,1,0:T(8,128)S(1)} %get-tuple-element.116.odd_sent), channel_id=1, source_target_pairs={{8,16},{16,8},{10,18},{18,10},{12,20},{20,12},{14,22},{22,14},{24,... | collective-permute-start | bytes 1179656 | tf_op jit(solution)/shard_map/ppermute | solution.py:575
  90.6 2.6 %shard_map.190 = (f32[2,512,512]{2,1,0:T(8,128)S(1)}, s32[4]{0:T(128)S(1)}) custom-call(s32[4]{0:T(128)S(1)} %get-tuple-element.98.info, f32[4,32,512]{2,1,0:T(8,128)S(1)} %get-tuple-element.99.refs_0_, f32[4,32,512]{2,1,0:T(8,128)S(1)} %collective-permute-done.15.refs_1_, f32[4,32,512]{2,1,0:T(8,128)S(1)} %collective-permute-done.16.refs_2_, ...), custom_call_target="tpu_custom_call" | custom-call | flops 4612000 | bytes 14760000 | tf_op jit(solution)/shard_map/pallas_call | solution.py:501
  93.2 2.8 %shard_map.191 = (f32[4,32,512]{2,1,0:T(8,128)S(1)}, f32[4,32,512]{2,1,0:T(8,128)S(1)}, f32[4,32,512]{2,1,0:T(8,128)S(1)}, f32[4,32,512]{2,1,0:T(8,128)S(1)}, s32[4]{0:T(128)S(1)}) custom-call(s32[4]{0:T(128)S(1)} %get-tuple-element.103.info, f32[16,32,512]{2,1,0:T(8,128)S(1)} %get-tuple-element.104.done, f32[6,32,512]{2,1,0:T(8,128)S(1)} %get-tuple-element.105.even_sent, ...), custom_call_target="tpu_custom_call" | custom-call | flops 4035500 | bytes 12915000 | tf_op jit(solution)/shard_map/pallas_call | solution.py:421
  96.8 6.2 %collective-permute-done.22.refs_3_ = f32[4,32,512]{2,1,0:T(8,128)S(1)} collective-permute-done((f32[4,32,512]{2,1,0:T(8,128)S(1)}, f32[4,32,512]{2,1,0:T(8,128)S(1)}, u32[]{:S(2)}, u32[]{:S(2)}) %collective-permute-start.22) | collective-permute-done | bytes 262176 | tf_op jit(solution)/shard_map/ppermute | solution.py:546
  103.0 2.7 %shard_map.192 = (f32[2,512,512]{2,1,0:T(8,128)S(1)}, s32[4]{0:T(128)S(1)}) custom-call(s32[4]{0:T(128)S(1)} %get-tuple-element.107.info, f32[4,32,512]{2,1,0:T(8,128)S(1)} %get-tuple-element.108.refs_0_, f32[4,32,512]{2,1,0:T(8,128)S(1)} %collective-permute-done.20.refs_1_, f32[4,32,512]{2,1,0:T(8,128)S(1)} %collective-permute-done.21.refs_2_, ...), custom_call_target="tpu_custom_call" | custom-call | flops 4612000 | bytes 14760000 | tf_op jit(solution)/shard_map/pallas_call | solution.py:501
  105.8 2.8 %shard_map.193 = (f32[4,32,512]{2,1,0:T(8,128)S(1)}, f32[4,32,512]{2,1,0:T(8,128)S(1)}, f32[4,32,512]{2,1,0:T(8,128)S(1)}, f32[4,32,512]{2,1,0:T(8,128)S(1)}, s32[4]{0:T(128)S(1)}) custom-call(s32[4]{0:T(128)S(1)} %get-tuple-element.113.info, f32[16,32,512]{2,1,0:T(8,128)S(1)} %get-tuple-element.114.done, f32[6,32,512]{2,1,0:T(8,128)S(1)} %get-tuple-element.115.even_sent, ...), custom_call_target="tpu_custom_call" | custom-call | flops 4035500 | bytes 12915000 | tf_op jit(solution)/shard_map/pallas_call | solution.py:421
  110.9 3.4 %collective-permute-done.27.refs_3_ = f32[4,32,512]{2,1,0:T(8,128)S(1)} collective-permute-done((f32[4,32,512]{2,1,0:T(8,128)S(1)}, f32[4,32,512]{2,1,0:T(8,128)S(1)}, u32[]{:S(2)}, u32[]{:S(2)}) %collective-permute-start.27) | collective-permute-done | bytes 262176 | tf_op jit(solution)/shard_map/ppermute | solution.py:546
  114.3 2.9 %shard_map.194 = (f32[2,512,512]{2,1,0:T(8,128)S(1)}, f32[2,512,512]{2,1,0:T(8,128)S(1)}, s32[4]{0:T(128)S(1)}) custom-call(s32[4]{0:T(128)S(1)} %get-tuple-element.117.info, f32[4,32,512]{2,1,0:T(8,128)S(1)} %get-tuple-element.118.refs_0_, f32[4,32,512]{2,1,0:T(8,128)S(1)} %collective-permute-done.25.refs_1_, ...), custom_call_target="tpu_custom_call" | custom-call | flops 4612000 | bytes 14760000 | tf_op jit(solution)/shard_map/pallas_call | solution.py:501
  118.7 6.1 %collective-permute-done.30.refs_3_ = f32[4,32,512]{2,1,0:T(8,128)S(1)} collective-permute-done((f32[4,32,512]{2,1,0:T(8,128)S(1)}, f32[4,32,512]{2,1,0:T(8,128)S(1)}, u32[]{:S(2)}, u32[]{:S(2)}) %collective-permute-start.30) | collective-permute-done | bytes 262176 | tf_op jit(solution)/shard_map/ppermute | solution.py:546
  124.8 3.4 %shard_map.195 = (f32[2,512,1024]{2,1,0:T(8,128)}, s32[4]{0:T(128)}) custom-call(s32[4]{0:T(128)S(1)} %get-tuple-element.123.info, f32[4,32,512]{2,1,0:T(8,128)S(1)} %get-tuple-element.124.refs_0_, f32[4,32,512]{2,1,0:T(8,128)S(1)} %collective-permute-done.28.refs_1_, f32[4,32,512]{2,1,0:T(8,128)S(1)} %collective-permute-done.29.refs_2_, ...), custom_call_target="tpu_custom_call" | custom-call | flops 4612000 | bytes 14760000 | tf_op jit(solution)/shard_map/pallas_call | solution.py:501
  (70 shorter events, 26.7 us)
Async XLA Ops:
  8.9 12.9 %collective-permute-start.2 = (f32[4,32,512]{2,1,0:T(8,128)S(1)}, f32[4,32,512]{2,1,0:T(8,128)S(1)}, u32[]{:S(2)}, u32[]{:S(2)}) collective-permute-start(f32[4,32,512]{2,1,0:T(8,128)S(1)} %get-tuple-element.73), channel_id=1, source_target_pairs={{0,6},{2,4},{4,2},{6,0},{8,14},{10,12},{12,10},{14,8},{16,22},{18,... | collective-permute-start | bytes 786440 | tf_op jit(solution)/shard_map/ppermute | solution.py:546
  9.4 16.7 %collective-permute-start.3 = (f32[4,32,512]{2,1,0:T(8,128)S(1)}, f32[4,32,512]{2,1,0:T(8,128)S(1)}, u32[]{:S(2)}, u32[]{:S(2)}) collective-permute-start(f32[4,32,512]{2,1,0:T(8,128)S(1)} %get-tuple-element.76), channel_id=1, source_target_pairs={{0,2},{2,0},{4,6},{6,4},{8,10},{10,8},{12,14},{14,12},{16,18},{18,... | collective-permute-start | bytes 786440 | tf_op jit(solution)/shard_map/ppermute | solution.py:546
  9.5 20.6 %collective-permute-start.4 = (f32[4,32,512]{2,1,0:T(8,128)S(1)}, f32[4,32,512]{2,1,0:T(8,128)S(1)}, u32[]{:S(2)}, u32[]{:S(2)}) collective-permute-start(f32[4,32,512]{2,1,0:T(8,128)S(1)} %get-tuple-element.77), channel_id=1, source_target_pairs={{0,4},{2,6},{4,0},{6,2},{8,12},{10,14},{12,8},{14,10},{16,20},{18,... | collective-permute-start | bytes 786440 | tf_op jit(solution)/shard_map/ppermute | solution.py:546
  17.7 20.7 %collective-permute-start.6 = (f32[2,4,32,512]{3,2,1,0:T(8,128)S(1)}, f32[2,4,32,512]{3,2,1,0:T(8,128)S(1)}, u32[]{:S(2)}, u32[]{:S(2)}) collective-permute-start(f32[2,4,32,512]{3,2,1,0:T(8,128)S(1)} %get-tuple-element.80), channel_id=1, source_target_pairs={{0,2},{2,0},{4,6},{6,4},{8,10},{10,8},{12,14},{14,12},{16,18},{18,... | collective-permute-start | bytes 1572872 | tf_op jit(solution)/shard_map/ppermute | solution.py:546
  18.4 14.5 %collective-permute-start.5 = (f32[4,32,512]{2,1,0:T(8,128)S(1)}, f32[4,32,512]{2,1,0:T(8,128)S(1)}, u32[]{:S(2)}, u32[]{:S(2)}) collective-permute-start(f32[4,32,512]{2,1,0:T(8,128)S(1)} %get-tuple-element.78), channel_id=1, source_target_pairs={{0,6},{2,4},{4,2},{6,0},{8,14},{10,12},{12,10},{14,8},{16,22},{18,... | collective-permute-start | bytes 786440 | tf_op jit(solution)/shard_map/ppermute | solution.py:546
  24.7 18.9 %collective-permute-start.7 = (f32[6,32,512]{2,1,0:T(8,128)S(1)}, f32[6,32,512]{2,1,0:T(8,128)S(1)}, u32[]{:S(2)}, u32[]{:S(2)}) collective-permute-start(f32[6,32,512]{2,1,0:T(8,128)S(1)} %get-tuple-element.84.even_sent), channel_id=1, source_target_pairs={{0,8},{8,0},{2,10},{10,2},{4,12},{12,4},{6,14},{14,6},{16,24},{24,... | collective-permute-start | bytes 1179656 | tf_op jit(solution)/shard_map/ppermute | solution.py:575
  26.1 20.1 %collective-permute-start.8 = (f32[6,32,512]{2,1,0:T(8,128)S(1)}, f32[6,32,512]{2,1,0:T(8,128)S(1)}, u32[]{:S(2)}, u32[]{:S(2)}) collective-permute-start(f32[6,32,512]{2,1,0:T(8,128)S(1)} %get-tuple-element.85.odd_sent), channel_id=1, source_target_pairs={{8,16},{16,8},{10,18},{18,10},{12,20},{20,12},{14,22},{22,14},{24,... | collective-permute-start | bytes 1179656 | tf_op jit(solution)/shard_map/ppermute | solution.py:575
  32.9 18.1 %collective-permute-start.10 = (f32[4,32,512]{2,1,0:T(8,128)S(1)}, f32[4,32,512]{2,1,0:T(8,128)S(1)}, u32[]{:S(2)}, u32[]{:S(2)}) collective-permute-start(f32[4,32,512]{2,1,0:T(8,128)S(1)} %get-tuple-element.89), channel_id=1, source_target_pairs={{0,4},{2,6},{4,0},{6,2},{8,12},{10,14},{12,8},{14,10},{16,20},{18,... | collective-permute-start | bytes 786440 | tf_op jit(solution)/shard_map/ppermute | solution.py:546
  37.0 29.4 %collective-permute-start.12 = (f32[6,32,512]{2,1,0:T(8,128)S(1)}, f32[6,32,512]{2,1,0:T(8,128)S(1)}, u32[]{:S(2)}, u32[]{:S(2)}) collective-permute-start(f32[6,32,512]{2,1,0:T(8,128)S(1)} %get-tuple-element.93.even_sent), channel_id=1, source_target_pairs={{0,8},{8,0},{2,10},{10,2},{4,12},{12,4},{6,14},{14,6},{16,24},{24,... | collective-permute-start | bytes 1179656 | tf_op jit(solution)/shard_map/ppermute | solution.py:575
  38.4 31.9 %collective-permute-start.13 = (f32[6,32,512]{2,1,0:T(8,128)S(1)}, f32[6,32,512]{2,1,0:T(8,128)S(1)}, u32[]{:S(2)}, u32[]{:S(2)}) collective-permute-start(f32[6,32,512]{2,1,0:T(8,128)S(1)} %get-tuple-element.94.odd_sent), channel_id=1, source_target_pairs={{8,16},{16,8},{10,18},{18,10},{12,20},{20,12},{14,22},{22,14},{24,... | collective-permute-start | bytes 1179656 | tf_op jit(solution)/shard_map/ppermute | solution.py:575
  43.6 30.7 %collective-permute-start.14 = (f32[2,4,32,512]{3,2,1,0:T(8,128)S(1)}, f32[2,4,32,512]{3,2,1,0:T(8,128)S(1)}, u32[]{:S(2)}, u32[]{:S(2)}) collective-permute-start(f32[2,4,32,512]{3,2,1,0:T(8,128)S(1)} %get-tuple-element.97), channel_id=1, source_target_pairs={{0,4},{2,6},{4,0},{6,2},{8,12},{10,14},{12,8},{14,10},{16,20},{18,... | collective-permute-start | bytes 1572872 | tf_op jit(solution)/shard_map/ppermute | solution.py:546
  46.2 17.1 %collective-permute-start.11 = (f32[4,32,512]{2,1,0:T(8,128)S(1)}, f32[4,32,512]{2,1,0:T(8,128)S(1)}, u32[]{:S(2)}, u32[]{:S(2)}) collective-permute-start(f32[4,32,512]{2,1,0:T(8,128)S(1)} %get-tuple-element.90), channel_id=1, source_target_pairs={{0,6},{2,4},{4,2},{6,0},{8,14},{10,12},{12,10},{14,8},{16,22},{18,... | collective-permute-start | bytes 786440 | tf_op jit(solution)/shard_map/ppermute | solution.py:546
  51.0 19.6 %collective-permute-start.15 = (f32[4,32,512]{2,1,0:T(8,128)S(1)}, f32[4,32,512]{2,1,0:T(8,128)S(1)}, u32[]{:S(2)}, u32[]{:S(2)}) collective-permute-start(f32[4,32,512]{2,1,0:T(8,128)S(1)} %get-tuple-element.100), channel_id=1, source_target_pairs={{0,2},{2,0},{4,6},{6,4},{8,10},{10,8},{12,14},{14,12},{16,18},{18,... | collective-permute-start | bytes 786440 | tf_op jit(solution)/shard_map/ppermute | solution.py:546
  66.2 22.4 %collective-permute-start.18 = (f32[6,32,512]{2,1,0:T(8,128)S(1)}, f32[6,32,512]{2,1,0:T(8,128)S(1)}, u32[]{:S(2)}, u32[]{:S(2)}) collective-permute-start(f32[6,32,512]{2,1,0:T(8,128)S(1)} %get-tuple-element.105.even_sent), channel_id=1, source_target_pairs={{0,8},{8,0},{2,10},{10,2},{4,12},{12,4},{6,14},{14,6},{16,24},{24,... | collective-permute-start | bytes 1179656 | tf_op jit(solution)/shard_map/ppermute | solution.py:575
  66.4 22.5 %collective-permute-start.19 = (f32[6,32,512]{2,1,0:T(8,128)S(1)}, f32[6,32,512]{2,1,0:T(8,128)S(1)}, u32[]{:S(2)}, u32[]{:S(2)}) collective-permute-start(f32[6,32,512]{2,1,0:T(8,128)S(1)} %get-tuple-element.106.odd_sent), channel_id=1, source_target_pairs={{8,16},{16,8},{10,18},{18,10},{12,20},{20,12},{14,22},{22,14},{24,... | collective-permute-start | bytes 1179656 | tf_op jit(solution)/shard_map/ppermute | solution.py:575
  70.6 13.4 %collective-permute-start.17 = (f32[4,32,512]{2,1,0:T(8,128)S(1)}, f32[4,32,512]{2,1,0:T(8,128)S(1)}, u32[]{:S(2)}, u32[]{:S(2)}) collective-permute-start(f32[4,32,512]{2,1,0:T(8,128)S(1)} %get-tuple-element.102), channel_id=1, source_target_pairs={{0,6},{2,4},{4,2},{6,0},{8,14},{10,12},{12,10},{14,8},{16,22},{18,... | collective-permute-start | bytes 786440 | tf_op jit(solution)/shard_map/ppermute | solution.py:546
  74.3 21.8 %collective-permute-start.20 = (f32[4,32,512]{2,1,0:T(8,128)S(1)}, f32[4,32,512]{2,1,0:T(8,128)S(1)}, u32[]{:S(2)}, u32[]{:S(2)}) collective-permute-start(f32[4,32,512]{2,1,0:T(8,128)S(1)} %get-tuple-element.109), channel_id=1, source_target_pairs={{0,2},{2,0},{4,6},{6,4},{8,10},{10,8},{12,14},{14,12},{16,18},{18,... | collective-permute-start | bytes 786440 | tf_op jit(solution)/shard_map/ppermute | solution.py:546
  78.7 27.1 %collective-permute-start.23 = (f32[6,32,512]{2,1,0:T(8,128)S(1)}, f32[6,32,512]{2,1,0:T(8,128)S(1)}, u32[]{:S(2)}, u32[]{:S(2)}) collective-permute-start(f32[6,32,512]{2,1,0:T(8,128)S(1)} %get-tuple-element.115.even_sent), channel_id=1, source_target_pairs={{0,8},{8,0},{2,10},{10,2},{4,12},{12,4},{6,14},{14,6},{16,24},{24,... | collective-permute-start | bytes 1179656 | tf_op jit(solution)/shard_map/ppermute | solution.py:575
  84.1 21.8 %collective-permute-start.24 = (f32[6,32,512]{2,1,0:T(8,128)S(1)}, f32[6,32,512]{2,1,0:T(8,128)S(1)}, u32[]{:S(2)}, u32[]{:S(2)}) collective-permute-start(f32[6,32,512]{2,1,0:T(8,128)S(1)} %get-tuple-element.116.odd_sent), channel_id=1, source_target_pairs={{8,16},{16,8},{10,18},{18,10},{12,20},{20,12},{14,22},{22,14},{24,... | collective-permute-start | bytes 1179656 | tf_op jit(solution)/shard_map/ppermute | solution.py:575
  88.9 14.2 %collective-permute-start.22 = (f32[4,32,512]{2,1,0:T(8,128)S(1)}, f32[4,32,512]{2,1,0:T(8,128)S(1)}, u32[]{:S(2)}, u32[]{:S(2)}) collective-permute-start(f32[4,32,512]{2,1,0:T(8,128)S(1)} %get-tuple-element.111), channel_id=1, source_target_pairs={{0,6},{2,4},{4,2},{6,0},{8,14},{10,12},{12,10},{14,8},{16,22},{18,... | collective-permute-start | bytes 786440 | tf_op jit(solution)/shard_map/ppermute | solution.py:546
  96.1 14.5 %collective-permute-start.25 = (f32[4,32,512]{2,1,0:T(8,128)S(1)}, f32[4,32,512]{2,1,0:T(8,128)S(1)}, u32[]{:S(2)}, u32[]{:S(2)}) collective-permute-start(f32[4,32,512]{2,1,0:T(8,128)S(1)} %get-tuple-element.119), channel_id=1, source_target_pairs={{0,2},{2,0},{4,6},{6,4},{8,10},{10,8},{12,14},{14,12},{16,18},{18,... | collective-permute-start | bytes 786440 | tf_op jit(solution)/shard_map/ppermute | solution.py:546
  96.2 14.7 %collective-permute-start.26 = (f32[4,32,512]{2,1,0:T(8,128)S(1)}, f32[4,32,512]{2,1,0:T(8,128)S(1)}, u32[]{:S(2)}, u32[]{:S(2)}) collective-permute-start(f32[4,32,512]{2,1,0:T(8,128)S(1)} %get-tuple-element.120), channel_id=1, source_target_pairs={{0,4},{2,6},{4,0},{6,2},{8,12},{10,14},{12,8},{14,10},{16,20},{18,... | collective-permute-start | bytes 786440 | tf_op jit(solution)/shard_map/ppermute | solution.py:546
  103.0 11.2 %collective-permute-start.27 = (f32[4,32,512]{2,1,0:T(8,128)S(1)}, f32[4,32,512]{2,1,0:T(8,128)S(1)}, u32[]{:S(2)}, u32[]{:S(2)}) collective-permute-start(f32[4,32,512]{2,1,0:T(8,128)S(1)} %get-tuple-element.121), channel_id=1, source_target_pairs={{0,6},{2,4},{4,2},{6,0},{8,14},{10,12},{12,10},{14,8},{16,22},{18,... | collective-permute-start | bytes 786440 | tf_op jit(solution)/shard_map/ppermute | solution.py:546
  110.6 14.2 %collective-permute-start.30 = (f32[4,32,512]{2,1,0:T(8,128)S(1)}, f32[4,32,512]{2,1,0:T(8,128)S(1)}, u32[]{:S(2)}, u32[]{:S(2)}) collective-permute-start(f32[4,32,512]{2,1,0:T(8,128)S(1)} %get-tuple-element.127), channel_id=1, source_target_pairs={{0,6},{2,4},{4,2},{6,0},{8,14},{10,12},{12,10},{14,8},{16,22},{18,... | collective-permute-start | bytes 786440 | tf_op jit(solution)/shard_map/ppermute | solution.py:546
  (15 other events, 185.4 us)

commit v3 on v1

--- a/solution.py
+++ b/solution.py
@@ -16,10 +16,11 @@
 GANG = 4
 SERIES = 2 * SUBSTEPS
 LANES = 128
+WIDE = 256
 VMEM_LIMIT = 20 * 1024 * 1024
 CHUNKS = (((0, 0, 4),), ((0, 4, 4),), ((1, 0, 4),), ((1, 4, 4),))
-MEMBER, ABOVE, BELOW = range(3)
-SCALARS = 3
+MEMBER, ABOVE, BELOW, SECOND = range(4)
+SCALARS = 4
 ORDER = ("D1", "D3", "E0", "E1", "C0", "E2", "C1", "E3", "I0", "C2", "I1", "C3", "I2", "I3")
 
 
@@ -69,6 +70,32 @@
 def pass_on(info, token):
     for place in range(SCALARS):
         token[place] = info[place]
+
+
+def steepened_and_folded(wave, squared, parity):
+    half = wave.shape[1] // 2
+    sign = -1.0 if parity else 1.0
+
+    def fold(values, at):
+        return values[:, at : at + LANES] + sign * values[:, half + at : half + at + LANES]
+
+    lane = lax.broadcasted_iota(jnp.int32, (wave.shape[0], LANES), 1)
+    pieces = [fold(squared, at) for at in range(0, half, LANES)]
+    last_early = sign * squared[:, half - LANES : half]
+    first_late = squared[:, half : half + LANES]
+    before = [pltpu.roll(piece, 1, 1) for piece in [last_early] + pieces]
+    after = [pltpu.roll(piece, LANES - 1, 1) for piece in pieces + [first_late]]
+    steep = [
+        fold(wave, LANES * n)
+        + WAVE_BREAKING
+        * 0.25
+        * (
+            jnp.where(lane == LANES - 1, after[n + 1], after[n])
+            - jnp.where(lane == 0, before[n], before[n + 1])
+        )
+        for n in range(half // LANES)
+    ]
+    return jnp.concatenate(steep, axis=1)
 
 
 def forward_kernel(chunks, per_parity, info, freq, depth, pressure, *refs):
@@ -111,15 +138,10 @@
                     factors[2 * chunk + part][d] = jnp.broadcast_to(column, (share, block))
 
     wave = pressure[...].reshape(rows * block, n_time)
-    lane = lax.broadcasted_iota(jnp.int32, wave.shape, 1)
     squared = wave * wave
-    after = jnp.where(lane == n_time - 1, 0.0, pltpu.roll(squared, n_time - 1, 1))
-    before = jnp.where(lane == 0, 0.0, pltpu.roll(squared, 1, 1))
-    steep = wave + WAVE_BREAKING * 0.25 * (after - before)
-    early, late = steep[:, :half], steep[:, half:]
     folded = {}
     for parity in sorted(set(piece[0] for pieces in chunks for piece in pieces)):
-        folded[parity] = halves(early - late if parity else early + late)
+        folded[parity] = halves(steepened_and_folded(wave, squared, parity))
     for chunk, pieces in enumerate(chunks):
         factor_re, factor_im = factors[2 * chunk : 2 * chunk + 2]
         offset = 0
@@ -180,22 +202,26 @@
         scratch_shapes=scratch,
         compiler_params=pltpu.CompilerParams(vmem_limit_bytes=VMEM_LIMIT),
         cost_estimate=cost(2 + 2 * len(chunks)),
-    )(info, relax_freq, relax_depth, in_hbm(pressure), *flat)
+    )(info, in_hbm(relax_freq), in_hbm(relax_depth), in_hbm(pressure), *flat)
     return outs[-1], [outs[GANG * c : GANG * c + GANG] for c in range(len(chunks))]
 
 
-def bin_rates(pieces, per_parity, member, half_bins, tile, shape):
+def tile_of(share):
+    return 16 if share % 16 == 0 else 8
+
+
+def bin_rates(pieces, per_parity, member, half_bins, place, shape):
     start, offset = 0, 0
     for parity, first, count in pieces:
-        here = 2 * (member * per_parity + first + 8 * tile - offset) + parity
-        start = jnp.where(8 * tile >= offset, here, start)
+        here = 2 * (member * per_parity + first + place - offset) + parity
+        start = jnp.where(place >= offset, here, start)
         offset += count
     bins = (start + 2 * lax.broadcasted_iota(jnp.int32, shape, 0)).astype(jnp.float32)
     return RATE_TOP * jnp.minimum(bins, 1.0) * jnp.minimum(1.0, half_bins / jnp.maximum(bins, 1.0))
 
 
-def lateral(width):
-    lane = lax.broadcasted_iota(jnp.int32, (8, LANES), 1)
+def lateral(height, width):
+    lane = lax.broadcasted_iota(jnp.int32, (height, LANES), 1)
     first_lane, last_lane = lane == 0, lane == LANES - 1
 
     def apply(center):
@@ -215,13 +241,14 @@
 
 def evolve_kernel(pieces, per_parity, half_bins, info, *refs):
     parts = refs[:GANG]
-    done, top, bottom, token, real, imag = refs[GANG:]
-    member = info[MEMBER]
+    done, early_sent, late_sent, token, real, imag = refs[GANG:]
+    member, is_second = info[MEMBER], info[SECOND] != 0
     pass_on(info, token)
     units, share, width = parts[0].shape
     rows = units // 2
     count = GANG * rows
-    side = lateral(width)
+    height = tile_of(share)
+    side = lateral(height, width)
 
     def advance(field, other, scale):
         before, center = None, other[0]
@@ -236,11 +263,14 @@
             before, center = center, after
 
     def keep(place, here, field):
-        top[place, here], bottom[place, here] = field[0], field[count - 1]
+        top, bottom = field[0], field[count - 1]
+        early_sent[place, here] = jnp.where(is_second, top, bottom)
+        late_sent[place, here] = jnp.where(is_second, bottom, top)
 
     def tile(index, carry):
-        here = pl.ds(pl.multiple_of(8 * index, 8), 8)
-        rate = bin_rates(pieces, per_parity, member, half_bins, index, (8, width))
+        place = pl.multiple_of(height * index, height)
+        here = pl.ds(place, height)
+        rate = bin_rates(pieces, per_parity, member, half_bins, place, (height, width))
         for d in range(GANG):
             first = (member ^ d) * rows
             for row in range(rows):
@@ -256,7 +286,7 @@
             done[count + row, here] = imag[row]
         return carry
 
-    lax.fori_loop(0, share // 8, tile, 0)
+    lax.fori_loop(0, share // height, tile, 0)
 
 
 def in_vmem(count):
@@ -266,7 +296,7 @@
 def evolve_chunk(info, parts, pieces, per_parity, half_bins):
     units, share, width = parts[0].shape
     count = GANG * units // 2
-    scratch = pltpu.VMEM((count, 8, width), jnp.float32)
+    scratch = pltpu.VMEM((count, tile_of(share), width), jnp.float32)
     sizes = (2 * count, SERIES, SERIES)
     return pl.pallas_call(
         functools.partial(evolve_kernel, pieces, per_parity, half_bins),
@@ -280,15 +310,18 @@
     )(info, *parts)
 
 
-def correct_kernel(pieces, per_parity, half_bins, info, done, top, bottom, above, below, *refs):
+def correct_kernel(
+    pieces, per_parity, half_bins, info, done, early_sent, late_sent, early_got, late_got, *refs
+):
     outs = refs[:GANG]
-    token, total, near_re, near_im, far_re, far_im = refs[GANG:]
-    member = info[MEMBER]
+    token, total, *strips = refs[GANG:]
+    member, is_second = info[MEMBER], info[SECOND] != 0
     pass_on(info, token)
     units, share, width = done.shape
     count = units // 2
     rows = count // GANG
-    side = lateral(width)
+    height = tile_of(share)
+    side = lateral(height, width)
 
     def advance(field, source, edge, scale, half_step, deep):
         before, center = edge, source[0] if half_step > 0 else None
@@ -304,26 +337,34 @@
             before, center = center, after
 
     def tile(index, carry):
-        here = pl.ds(pl.multiple_of(8 * index, 8), 8)
-        rate = bin_rates(pieces, per_parity, member, half_bins, index, (8, width))
+        place = pl.multiple_of(height * index, height)
+        here = pl.ds(place, height)
+        rate = bin_rates(pieces, per_parity, member, half_bins, place, (height, width))
         for unit in range(units):
             total[unit] = done[unit, here]
-        for own, other, flag, order in (
-            (top, above, info[ABOVE], range(count)),
-            (bottom, below, info[BELOW], range(count - 1, -1, -1)),
-        ):
-            rate_far = rate * flag.astype(jnp.float32)
-            for half_step in range(SERIES):
-                own_edge, far_edge = own[half_step, here], other[half_step, here]
-                near, near_from = (near_re, near_im) if half_step % 2 == 0 else (near_im, near_re)
-                back, back_from = (far_re, far_im) if half_step % 2 == 0 else (far_im, far_re)
-                sign = 1.0 if half_step % 2 else -1.0
+        early, late = (early_sent, early_got), (late_sent, late_got)
+        edges = (
+            (early, late, info[ABOVE], strips[:4], range(count)),
+            (late, early, info[BELOW], strips[4:], range(count - 1, -1, -1)),
+        )
+        for half_step in range(SERIES):
+            for if_second, if_first, flag, (near_re, near_im, far_re, far_im), _ in edges:
+                own_edge, far_edge = (
+                    jnp.where(is_second, one[half_step, here], two[half_step, here])
+                    for one, two in zip(if_second, if_first)
+                )
+                of_imag = half_step % 2
+                near, near_from = (near_im, near_re) if of_imag else (near_re, near_im)
+                far, far_from = (far_im, far_re) if of_imag else (far_re, far_im)
+                scale = rate if of_imag else -rate
                 if half_step > 0:
                     own_edge = own_edge + near_from[0]
-                    far_edge = far_edge + back_from[0]
-                reach = min(half_step + 1, SERIES - 1 - half_step)
-                advance(near, near_from, far_edge, sign * rate, half_step, half_step + 1)
-                advance(back, back_from, own_edge, sign * rate_far, half_step, reach)
+                    far_edge = far_edge + far_from[0]
+                back = min(half_step + 1, SERIES - 1 - half_step)
+                advance(near, near_from, far_edge, scale, half_step, half_step + 1)
+                scale = scale * flag.astype(jnp.float32)
+                advance(far, far_from, own_edge, scale, half_step, back)
+        for _, _, _, (near_re, near_im, _, _), order in edges:
             for row in range(SERIES - 1):
                 total[order[row]] = total[order[row]] + near_re[row]
             for row in range(SERIES):
@@ -335,19 +376,19 @@
                 outs[d][rows + row, here] = total[count + first + row]
         return carry
 
-    lax.fori_loop(0, share // 8, tile, 0)
+    lax.fori_loop(0, share // height, tile, 0)
 
 
 def correct_chunk(info, state, pieces, per_parity, half_bins):
     units, share, width = state[0].shape
     shape = jax.ShapeDtypeStruct((units // GANG, share, width), jnp.float32)
-    strip = pltpu.VMEM((SERIES, 8, width), jnp.float32)
+    strip = pltpu.VMEM((SERIES, tile_of(share), width), jnp.float32)
     return pl.pallas_call(
         functools.partial(correct_kernel, pieces, per_parity, half_bins),
         in_specs=[scalars()] + in_vmem(5),
         out_specs=in_vmem(GANG) + [scalars()],
         out_shape=[shape] * GANG + [token_shape()],
-        scratch_shapes=[pltpu.VMEM((units, 8, width), jnp.float32)] + [strip] * 4,
+        scratch_shapes=[pltpu.VMEM((units, tile_of(share), width), jnp.float32)] + [strip] * 8,
         compiler_params=pltpu.CompilerParams(vmem_limit_bytes=VMEM_LIMIT),
         cost_estimate=cost(3.5),
     )(info, *state)
@@ -392,19 +433,19 @@
     flat = [t for chunk in tables for pair in chunk for t in pair]
     held = sorted(sums)
     fresh = sorted(set(held) | set(piece[0] for pieces in chunks for piece in pieces))
-    state = pl.BlockSpec((rows, LANES, half), lambda i: (0, i, 0))
+    state = pl.BlockSpec((rows, WIDE, half), lambda i: (0, i, 0))
     state_shape = jax.ShapeDtypeStruct((rows, width, half), jnp.float32)
     if last:
-        out_specs = [pl.BlockSpec((rows, LANES, 2 * half), lambda i: (0, i, 0))]
+        out_specs = [pl.BlockSpec((rows, WIDE, 2 * half), lambda i: (0, i, 0))]
         out_shape = [jax.ShapeDtypeStruct((rows, width, 2 * half), jnp.float32)]
     else:
         out_specs, out_shape = [state] * len(fresh), [state_shape] * len(fresh)
     in_specs = [scalars()]
     for chunk in parts:
-        in_specs += [pl.BlockSpec(chunk[0].shape[:2] + (LANES,), lambda i: (0, 0, i))] * GANG
+        in_specs += [pl.BlockSpec(chunk[0].shape[:2] + (WIDE,), lambda i: (0, 0, i))] * GANG
     outs = pl.pallas_call(
         functools.partial(inverse_kernel, chunks, held, last),
-        grid=(width // LANES,),
+        grid=(width // WIDE,),
         in_specs=in_specs
         + [pl.BlockSpec(t.shape, lambda i: (0, 0)) for t in flat]
         + [state] * len(held),
@@ -431,12 +472,19 @@
         [(device(b, m), device(b, m ^ d)) for b in range(blocks) for m in range(GANG)]
         for d in range(GANG)
     ]
-    down = [(device(b, m), device(b + 1, m)) for b in range(blocks - 1) for m in range(GANG)]
-    up = [(target, source) for source, target in down]
+    pairs = [
+        [
+            (device(b + side, m), device(b + 1 - side, m))
+            for b in range(first, blocks - 1, 2)
+            for m in range(GANG)
+            for side in range(2)
+        ]
+        for first in (1, 0)
+    ]
 
     place = lax.axis_index("narrow") * wide + lax.axis_index("wide")
     block = place // GANG
-    info = [place % GANG, block > 0, block < blocks - 1]
+    info = [place % GANG, block > 0, block < blocks - 1, (block + 1) % 2]
     info = jnp.stack([jnp.asarray(value, jnp.int32) for value in info])
 
     def swap(parts):
@@ -456,10 +504,9 @@
             info, parts = forward_chunks(info, *inputs, forward[some], chunks[some], per_parity)
             held[some] = [swap(part) for part in parts]
         elif kernel == "E":
-            done, top, bottom, info = evolve_chunk(info, held[c], *shape)
-            above = lax.ppermute(bottom, axes, down)
-            below = lax.ppermute(top, axes, up)
-            held[c] = (done, top, bottom, above, below)
+            done, *sent, info = evolve_chunk(info, held[c], *shape)
+            got = [lax.ppermute(values, axes, some) for values, some in zip(sent, pairs)]
+            held[c] = (done, *sent, *got)
         elif kernel == "C":
             *parts, info = correct_chunk(info, held[c], *shape)
             held[c] = swap(parts)

time: 125 us -> 120 us (0.960)
  waiting for transfers between devices: 17.4 us -> 28.3 us
  starting transfers between devices: 49.8 us -> 41.3 us
  Pallas kernels: 55.3 us -> 48.3 us
  local copies, waits for them, and re-layouts: 1.37 us -> 0.05 us
    ppermute x8, waiting for transfers between devices: 1.44 us -> 10.4 us  [shards(): lax.ppermute(values, axes, some)]
    ppermute x8, starting transfers between devices: 28.2 us -> 21.1 us  [shards(): lax.ppermute(values, axes, some)]
    pallas_call x4, Pallas kernels: 14.4 us -> 11.3 us  [correct_chunk(): pl.pallas_call(functools.partial(correct_kernel, pieces, per_parity, half...]
    pallas_call x4, Pallas kernels: 14.2 us -> 11.7 us  [inverse_chunks(): pl.pallas_call(functools.partial(inverse_kernel, chunks, held, last), gri...]
    ppermute x24, waiting for transfers between devices: 15.9 us -> 17.9 us  [swap(): lax.ppermute(parts[d], axes, swaps[d])]
    unnamed x24 -> x16, local copies, waits for them, and re-layouts: 1.37 us -> 0.05 us
    ppermute x24, starting transfers between devices: 21.5 us -> 20.2 us  [swap(): lax.ppermute(parts[d], axes, swaps[d])]
    pallas_call x2, Pallas kernels: 15 us -> 13.7 us  [forward_chunks(): pl.pallas_call(functools.partial(forward_kernel, chunks, per_parity), gri...]
  transfers between devices with their start and end apart: 32 -> 32, of which waited for: 7 -> 10; matrix products, arithmetic and copies ran while one was open for 0% -> 0% of each run, Pallas kernels for 35% -> 32%
where the time goes in v3:
time: 120 us; the launch traced here: 118 us
  Pallas kernels  48.3 us (40%)
  starting transfers between devices  41.3 us (34%)
  waiting for transfers between devices  28.3 us (24%)
    ppermute x8, starting transfers between devices, shards(): lax.ppermute(values, axes, some)  21.1 us
    ppermute x24, starting transfers between devices, swap(): lax.ppermute(parts[d], axes, swaps[d])  20.2 us
    ppermute x24, waiting for transfers between devices, swap(): lax.ppermute(parts[d], axes, swaps[d])  17.9 us
    pallas_call x2, Pallas kernels, forward_chunks(): pl.pallas_call(functools.partial(forward_kernel, chunks, per_parity), gri...  13.7 us
    pallas_call x4, Pallas kernels, inverse_chunks(): pl.pallas_call(functools.partial(inverse_kernel, chunks, held, last), gri...  11.7 us
    pallas_call x4, Pallas kernels, evolve_chunk(): pl.pallas_call(functools.partial(evolve_kernel, pieces, per_parity, half_...  11.7 us
    pallas_call x4, Pallas kernels, correct_chunk(): pl.pallas_call(functools.partial(correct_kernel, pieces, per_parity, half...  11.3 us
    ppermute x8, waiting for transfers between devices, shards(): lax.ppermute(values, axes, some)  10.4 us
  transfers between devices with their start and end apart: 32, of which 10 were waited for; matrix products, arithmetic and copies ran while one was open for 0% of the time, Pallas kernels for 32%

profile of v3, /device:TPU:3, one launch (start us, length us, event | category | flops | bytes accessed | tf_op | source)
XLA Modules:
  0.0 118.4 jit_solution(6943072338581657106)
XLA Ops:
  0.1 6.8 %shard_map.181 = (f32[4,32,512]{2,1,0:T(8,128)S(1)}, f32[4,32,512]{2,1,0:T(8,128)S(1)}, f32[4,32,512]{2,1,0:T(8,128)S(1)}, f32[4,32,512]{2,1,0:T(8,128)S(1)}, f3...) custom-call(s32[4]{0:T(128)S(1)} %pad_add_fusion.info, ...), custom_call_target="tpu_custom_call" | custom-call | flops 6918000 | bytes 22140000 | tf_op jit(solution)/shard_map/pallas_call | solution.py:194
  11.5 6.8 %shard_map.182 = (f32[4,32,512]{2,1,0:T(8,128)S(1)}, f32[4,32,512]{2,1,0:T(8,128)S(1)}, f32[4,32,512]{2,1,0:T(8,128)S(1)}, f32[4,32,512]{2,1,0:T(8,128)S(1)}, f3...) custom-call(s32[4]{0:T(128)S(1)} %get-tuple-element.67.info, ...), custom_call_target="tpu_custom_call" | custom-call | flops 6918000 | bytes 22140000 | tf_op jit(solution)/shard_map/pallas_call | solution.py:194
  18.4 3.4 %collective-permute-done.2.refs_3_ = f32[4,32,512]{2,1,0:T(8,128)S(1)} collective-permute-done((f32[4,32,512]{2,1,0:T(8,128)S(1)}, f32[4,32,512]{2,1,0:T(8,128)S(1)}, u32[]{:S(2)}, u32[]{:S(2)}) %collective-permute-start.2) | collective-permute-done | bytes 262176 | tf_op jit(solution)/shard_map/ppermute | solution.py:491
  21.8 2.9 %shard_map.183 = (f32[16,32,512]{2,1,0:T(8,128)S(1)}, f32[6,32,512]{2,1,0:T(8,128)S(1)}, f32[6,32,512]{2,1,0:T(8,128)S(1)}, s32[4]{0:T(128)S(1)}) custom-call(s32[4]{0:T(128)S(1)} %get-tuple-element.68.info, f32[4,32,512]{2,1,0:T(8,128)S(1)} %get-tuple-element.69.refs_0_, f32[4,32,512]{2,1,0:T(8,128)S(1)} %collective-permute-done.refs_1_, ...), custom_call_target="tpu_custom_call" | custom-call | flops 3459000 | bytes 11070000 | tf_op jit(solution)/shard_map/pallas_call | solution.py:301
  24.7 5.2 %collective-permute-start.6 = (f32[6,32,512]{2,1,0:T(8,128)S(1)}, f32[6,32,512]{2,1,0:T(8,128)S(1)}, u32[]{:S(2)}, u32[]{:S(2)}) collective-permute-start(f32[6,32,512]{2,1,0:T(8,128)S(1)} %get-tuple-element.80.early_sent), channel_id=1, source_target_pairs={{8,16},{16,8},{10,18},{18,10},{12,20},{20,12},{14,22},{22,14},{24,... | collective-permute-start | bytes 1179656 | tf_op jit(solution)/shard_map/ppermute | solution.py:508
  33.9 2.9 %shard_map.184 = (f32[16,32,512]{2,1,0:T(8,128)S(1)}, f32[6,32,512]{2,1,0:T(8,128)S(1)}, f32[6,32,512]{2,1,0:T(8,128)S(1)}, s32[4]{0:T(128)S(1)}) custom-call(s32[4]{0:T(128)S(1)} %get-tuple-element.73.info, f32[4,32,512]{2,1,0:T(8,128)S(1)} %get-tuple-element.74.refs_0_, f32[4,32,512]{2,1,0:T(8,128)S(1)} %collective-permute-done.3.refs_1_, ...), custom_call_target="tpu_custom_call" | custom-call | flops 3459000 | bytes 11070000 | tf_op jit(solution)/shard_map/pallas_call | solution.py:301
  36.9 5.2 %collective-permute-start.11 = (f32[6,32,512]{2,1,0:T(8,128)S(1)}, f32[6,32,512]{2,1,0:T(8,128)S(1)}, u32[]{:S(2)}, u32[]{:S(2)}) collective-permute-start(f32[6,32,512]{2,1,0:T(8,128)S(1)} %get-tuple-element.89.early_sent), channel_id=1, source_target_pairs={{8,16},{16,8},{10,18},{18,10},{12,20},{20,12},{14,22},{22,14},{24,... | collective-permute-start | bytes 1179656 | tf_op jit(solution)/shard_map/ppermute | solution.py:508
  49.0 2.8 %shard_map.185 = (f32[4,32,512]{2,1,0:T(8,128)S(1)}, f32[4,32,512]{2,1,0:T(8,128)S(1)}, f32[4,32,512]{2,1,0:T(8,128)S(1)}, f32[4,32,512]{2,1,0:T(8,128)S(1)}, s32[4]{0:T(128)S(1)}) custom-call(s32[4]{0:T(128)S(1)} %get-tuple-element.78.info, f32[16,32,512]{2,1,0:T(8,128)S(1)} %get-tuple-element.79.done, f32[6,32,512]{2,1,0:T(8,128)S(1)} %get-tuple-element.80.early_sent, ...), custom_call_target="tpu_custom_call" | custom-call | flops 4035500 | bytes 12915000 | tf_op jit(solution)/shard_map/pallas_call | solution.py:386
  52.0 2.9 %shard_map.186 = (f32[16,32,512]{2,1,0:T(8,128)S(1)}, f32[6,32,512]{2,1,0:T(8,128)S(1)}, f32[6,32,512]{2,1,0:T(8,128)S(1)}, s32[4]{0:T(128)S(1)}) custom-call(s32[4]{0:T(128)S(1)} %get-tuple-element.82.info, f32[4,32,512]{2,1,0:T(8,128)S(1)} %get-tuple-element.83.refs_0_, f32[4,32,512]{2,1,0:T(8,128)S(1)} %collective-permute-done.8.refs_1_, ...), custom_call_target="tpu_custom_call" | custom-call | flops 3459000 | bytes 11070000 | tf_op jit(solution)/shard_map/pallas_call | solution.py:301
  54.9 2.9 %collective-permute-start.19 = (f32[6,32,512]{2,1,0:T(8,128)S(1)}, f32[6,32,512]{2,1,0:T(8,128)S(1)}, u32[]{:S(2)}, u32[]{:S(2)}) collective-permute-start(f32[6,32,512]{2,1,0:T(8,128)S(1)} %get-tuple-element.103.early_sent), channel_id=1, source_target_pairs={{8,16},{16,8},{10,18},{18,10},{12,20},{20,12},{14,22},{22,14},{24,... | collective-permute-start | bytes 1179656 | tf_op jit(solution)/shard_map/ppermute | solution.py:508
  61.5 2.4 %collective-permute-done.12.late_got = f32[6,32,512]{2,1,0:T(8,128)S(1)} collective-permute-done((f32[6,32,512]{2,1,0:T(8,128)S(1)}, f32[6,32,512]{2,1,0:T(8,128)S(1)}, u32[]{:S(2)}, u32[]{:S(2)}) %collective-permute-start.12) | collective-permute-done | bytes 393248 | tf_op jit(solution)/shard_map/ppermute | solution.py:508
  65.9 2.8 %shard_map.187 = (f32[4,32,512]{2,1,0:T(8,128)S(1)}, f32[4,32,512]{2,1,0:T(8,128)S(1)}, f32[4,32,512]{2,1,0:T(8,128)S(1)}, f32[4,32,512]{2,1,0:T(8,128)S(1)}, s32[4]{0:T(128)S(1)}) custom-call(s32[4]{0:T(128)S(1)} %get-tuple-element.87.info, f32[16,32,512]{2,1,0:T(8,128)S(1)} %get-tuple-element.88.done, f32[6,32,512]{2,1,0:T(8,128)S(1)} %get-tuple-element.89.early_sent, ...), custom_call_target="tpu_custom_call" | custom-call | flops 4035500 | bytes 12915000 | tf_op jit(solution)/shard_map/pallas_call | solution.py:386
  68.9 2.9 %shard_map.188 = (f32[16,32,512]{2,1,0:T(8,128)S(1)}, f32[6,32,512]{2,1,0:T(8,128)S(1)}, f32[6,32,512]{2,1,0:T(8,128)S(1)}, s32[4]{0:T(128)S(1)}) custom-call(s32[4]{0:T(128)S(1)} %get-tuple-element.91.info, f32[4,32,512]{2,1,0:T(8,128)S(1)} %get-tuple-element.92.refs_0_, f32[4,32,512]{2,1,0:T(8,128)S(1)} %collective-permute-done.13.refs_1_, ...), custom_call_target="tpu_custom_call" | custom-call | flops 3459000 | bytes 11070000 | tf_op jit(solution)/shard_map/pallas_call | solution.py:301
  71.8 3.0 %collective-permute-start.24 = (f32[6,32,512]{2,1,0:T(8,128)S(1)}, f32[6,32,512]{2,1,0:T(8,128)S(1)}, u32[]{:S(2)}, u32[]{:S(2)}) collective-permute-start(f32[6,32,512]{2,1,0:T(8,128)S(1)} %get-tuple-element.113.early_sent), channel_id=1, source_target_pairs={{8,16},{16,8},{10,18},{18,10},{12,20},{20,12},{14,22},{22,14},{24,... | collective-permute-start | bytes 1179656 | tf_op jit(solution)/shard_map/ppermute | solution.py:508
  78.3 2.5 %collective-permute-done.20.late_got = f32[6,32,512]{2,1,0:T(8,128)S(1)} collective-permute-done((f32[6,32,512]{2,1,0:T(8,128)S(1)}, f32[6,32,512]{2,1,0:T(8,128)S(1)}, u32[]{:S(2)}, u32[]{:S(2)}) %collective-permute-start.20) | collective-permute-done | bytes 393248 | tf_op jit(solution)/shard_map/ppermute | solution.py:508
  82.9 2.6 %shard_map.189 = (f32[2,512,512]{2,1,0:T(8,128)S(1)}, s32[4]{0:T(128)S(1)}) custom-call(s32[4]{0:T(128)S(1)} %get-tuple-element.96.info, f32[4,32,512]{2,1,0:T(8,128)S(1)} %get-tuple-element.97.refs_0_, f32[4,32,512]{2,1,0:T(8,128)S(1)} %collective-permute-done.16.refs_1_, f32[4,32,512]{2,1,0:T(8,128)S(1)} %collective-permute-done.17.refs_2_, ...), custom_call_target="tpu_custom_call" | custom-call | flops 4612000 | bytes 14760000 | tf_op jit(solution)/shard_map/pallas_call | solution.py:446
  85.5 2.8 %shard_map.190 = (f32[4,32,512]{2,1,0:T(8,128)S(1)}, f32[4,32,512]{2,1,0:T(8,128)S(1)}, f32[4,32,512]{2,1,0:T(8,128)S(1)}, f32[4,32,512]{2,1,0:T(8,128)S(1)}, s32[4]{0:T(128)S(1)}) custom-call(s32[4]{0:T(128)S(1)} %get-tuple-element.101.info, f32[16,32,512]{2,1,0:T(8,128)S(1)} %get-tuple-element.102.done, f32[6,32,512]{2,1,0:T(8,128)S(1)} %get-tuple-element.103.early_sent, ...), custom_call_target="tpu_custom_call" | custom-call | flops 4035500 | bytes 12915000 | tf_op jit(solution)/shard_map/pallas_call | solution.py:386
  91.5 2.7 %shard_map.191 = (f32[2,512,512]{2,1,0:T(8,128)S(1)}, s32[4]{0:T(128)S(1)}) custom-call(s32[4]{0:T(128)S(1)} %get-tuple-element.105.info, f32[4,32,512]{2,1,0:T(8,128)S(1)} %get-tuple-element.106.refs_0_, f32[4,32,512]{2,1,0:T(8,128)S(1)} %collective-permute-done.21.refs_1_, f32[4,32,512]{2,1,0:T(8,128)S(1)} %collective-permute-done.22.refs_2_, ...), custom_call_target="tpu_custom_call" | custom-call | flops 4612000 | bytes 14760000 | tf_op jit(solution)/shard_map/pallas_call | solution.py:446
  94.3 3.4 %collective-permute-done.25.late_got = f32[6,32,512]{2,1,0:T(8,128)S(1)} collective-permute-done((f32[6,32,512]{2,1,0:T(8,128)S(1)}, f32[6,32,512]{2,1,0:T(8,128)S(1)}, u32[]{:S(2)}, u32[]{:S(2)}) %collective-permute-start.25) | collective-permute-done | bytes 393248 | tf_op jit(solution)/shard_map/ppermute | solution.py:508
  97.7 2.8 %shard_map.192 = (f32[4,32,512]{2,1,0:T(8,128)S(1)}, f32[4,32,512]{2,1,0:T(8,128)S(1)}, f32[4,32,512]{2,1,0:T(8,128)S(1)}, f32[4,32,512]{2,1,0:T(8,128)S(1)}, s32[4]{0:T(128)S(1)}) custom-call(s32[4]{0:T(128)S(1)} %get-tuple-element.111.info, f32[16,32,512]{2,1,0:T(8,128)S(1)} %get-tuple-element.112.done, f32[6,32,512]{2,1,0:T(8,128)S(1)} %get-tuple-element.113.early_sent, ...), custom_call_target="tpu_custom_call" | custom-call | flops 4035500 | bytes 12915000 | tf_op jit(solution)/shard_map/pallas_call | solution.py:386
  103.0 2.9 %shard_map.193 = (f32[2,512,512]{2,1,0:T(8,128)S(1)}, f32[2,512,512]{2,1,0:T(8,128)S(1)}, s32[4]{0:T(128)S(1)}) custom-call(s32[4]{0:T(128)S(1)} %get-tuple-element.115.info, f32[4,32,512]{2,1,0:T(8,128)S(1)} %get-tuple-element.116.refs_0_, f32[4,32,512]{2,1,0:T(8,128)S(1)} %collective-permute-done.26.refs_1_, ...), custom_call_target="tpu_custom_call" | custom-call | flops 4612000 | bytes 14760000 | tf_op jit(solution)/shard_map/pallas_call | solution.py:446
  106.0 3.2 %collective-permute-done.30.refs_2_ = f32[4,32,512]{2,1,0:T(8,128)S(1)} collective-permute-done((f32[4,32,512]{2,1,0:T(8,128)S(1)}, f32[4,32,512]{2,1,0:T(8,128)S(1)}, u32[]{:S(2)}, u32[]{:S(2)}) %collective-permute-start.30) | collective-permute-done | bytes 262176 | tf_op jit(solution)/shard_map/ppermute | solution.py:491
  109.2 5.8 %collective-permute-done.31.refs_3_ = f32[4,32,512]{2,1,0:T(8,128)S(1)} collective-permute-done((f32[4,32,512]{2,1,0:T(8,128)S(1)}, f32[4,32,512]{2,1,0:T(8,128)S(1)}, u32[]{:S(2)}, u32[]{:S(2)}) %collective-permute-start.31) | collective-permute-done | bytes 262176 | tf_op jit(solution)/shard_map/ppermute | solution.py:491
  115.0 3.4 %shard_map.194 = (f32[2,512,1024]{2,1,0:T(8,128)}, s32[4]{0:T(128)}) custom-call(s32[4]{0:T(128)S(1)} %get-tuple-element.121.info, f32[4,32,512]{2,1,0:T(8,128)S(1)} %get-tuple-element.122.refs_0_, f32[4,32,512]{2,1,0:T(8,128)S(1)} %collective-permute-done.29.refs_1_, f32[4,32,512]{2,1,0:T(8,128)S(1)} %collective-permute-done.30.refs_2_, ...), custom_call_target="tpu_custom_call" | custom-call | flops 4612000 | bytes 14760000 | tf_op jit(solution)/shard_map/pallas_call | solution.py:446
  (71 shorter events, 32.7 us)
Async XLA Ops:
  8.9 12.9 %collective-permute-start.2 = (f32[4,32,512]{2,1,0:T(8,128)S(1)}, f32[4,32,512]{2,1,0:T(8,128)S(1)}, u32[]{:S(2)}, u32[]{:S(2)}) collective-permute-start(f32[4,32,512]{2,1,0:T(8,128)S(1)} %get-tuple-element.72), channel_id=1, source_target_pairs={{0,6},{2,4},{4,2},{6,0},{8,14},{10,12},{12,10},{14,8},{16,22},{18,... | collective-permute-start | bytes 786440 | tf_op jit(solution)/shard_map/ppermute | solution.py:491
  9.4 20.6 %collective-permute-start.3 = (f32[4,32,512]{2,1,0:T(8,128)S(1)}, f32[4,32,512]{2,1,0:T(8,128)S(1)}, u32[]{:S(2)}, u32[]{:S(2)}) collective-permute-start(f32[4,32,512]{2,1,0:T(8,128)S(1)} %get-tuple-element.75), channel_id=1, source_target_pairs={{0,2},{2,0},{4,6},{6,4},{8,10},{10,8},{12,14},{14,12},{16,18},{18,... | collective-permute-start | bytes 786440 | tf_op jit(solution)/shard_map/ppermute | solution.py:491
  9.5 20.6 %collective-permute-start.4 = (f32[4,32,512]{2,1,0:T(8,128)S(1)}, f32[4,32,512]{2,1,0:T(8,128)S(1)}, u32[]{:S(2)}, u32[]{:S(2)}) collective-permute-start(f32[4,32,512]{2,1,0:T(8,128)S(1)} %get-tuple-element.76), channel_id=1, source_target_pairs={{0,4},{2,6},{4,0},{6,2},{8,12},{10,14},{12,8},{14,10},{16,20},{18,... | collective-permute-start | bytes 786440 | tf_op jit(solution)/shard_map/ppermute | solution.py:491
  10.8 22.1 %collective-permute-start.5 = (f32[4,32,512]{2,1,0:T(8,128)S(1)}, f32[4,32,512]{2,1,0:T(8,128)S(1)}, u32[]{:S(2)}, u32[]{:S(2)}) collective-permute-start(f32[4,32,512]{2,1,0:T(8,128)S(1)} %get-tuple-element.77), channel_id=1, source_target_pairs={{0,6},{2,4},{4,2},{6,0},{8,14},{10,12},{12,10},{14,8},{16,22},{18,... | collective-permute-start | bytes 786440 | tf_op jit(solution)/shard_map/ppermute | solution.py:491
  24.7 19.1 %collective-permute-start.6 = (f32[6,32,512]{2,1,0:T(8,128)S(1)}, f32[6,32,512]{2,1,0:T(8,128)S(1)}, u32[]{:S(2)}, u32[]{:S(2)}) collective-permute-start(f32[6,32,512]{2,1,0:T(8,128)S(1)} %get-tuple-element.80.early_sent), channel_id=1, source_target_pairs={{8,16},{16,8},{10,18},{18,10},{12,20},{20,12},{14,22},{22,14},{24,... | collective-permute-start | bytes 1179656 | tf_op jit(solution)/shard_map/ppermute | solution.py:508
  29.9 17.1 %collective-permute-start.7 = (f32[6,32,512]{2,1,0:T(8,128)S(1)}, f32[6,32,512]{2,1,0:T(8,128)S(1)}, u32[]{:S(2)}, u32[]{:S(2)}) collective-permute-start(f32[6,32,512]{2,1,0:T(8,128)S(1)} %get-tuple-element.81.late_sent), channel_id=1, source_target_pairs={{0,8},{8,0},{2,10},{10,2},{4,12},{12,4},{6,14},{14,6},{16,24},{24,... | collective-permute-start | bytes 1179656 | tf_op jit(solution)/shard_map/ppermute | solution.py:508
  30.1 11.9 %collective-permute-start.9 = (f32[4,32,512]{2,1,0:T(8,128)S(1)}, f32[4,32,512]{2,1,0:T(8,128)S(1)}, u32[]{:S(2)}, u32[]{:S(2)}) collective-permute-start(f32[4,32,512]{2,1,0:T(8,128)S(1)} %get-tuple-element.85), channel_id=1, source_target_pairs={{0,4},{2,6},{4,0},{6,2},{8,12},{10,14},{12,8},{14,10},{16,20},{18,... | collective-permute-start | bytes 786440 | tf_op jit(solution)/shard_map/ppermute | solution.py:491
  32.9 10.9 %collective-permute-start.10 = (f32[4,32,512]{2,1,0:T(8,128)S(1)}, f32[4,32,512]{2,1,0:T(8,128)S(1)}, u32[]{:S(2)}, u32[]{:S(2)}) collective-permute-start(f32[4,32,512]{2,1,0:T(8,128)S(1)} %get-tuple-element.86), channel_id=1, source_target_pairs={{0,6},{2,4},{4,2},{6,0},{8,14},{10,12},{12,10},{14,8},{16,22},{18,... | collective-permute-start | bytes 786440 | tf_op jit(solution)/shard_map/ppermute | solution.py:491
  36.9 23.4 %collective-permute-start.11 = (f32[6,32,512]{2,1,0:T(8,128)S(1)}, f32[6,32,512]{2,1,0:T(8,128)S(1)}, u32[]{:S(2)}, u32[]{:S(2)}) collective-permute-start(f32[6,32,512]{2,1,0:T(8,128)S(1)} %get-tuple-element.89.early_sent), channel_id=1, source_target_pairs={{8,16},{16,8},{10,18},{18,10},{12,20},{20,12},{14,22},{22,14},{24,... | collective-permute-start | bytes 1179656 | tf_op jit(solution)/shard_map/ppermute | solution.py:508
  42.1 21.9 %collective-permute-start.12 = (f32[6,32,512]{2,1,0:T(8,128)S(1)}, f32[6,32,512]{2,1,0:T(8,128)S(1)}, u32[]{:S(2)}, u32[]{:S(2)}) collective-permute-start(f32[6,32,512]{2,1,0:T(8,128)S(1)} %get-tuple-element.90.late_sent), channel_id=1, source_target_pairs={{0,8},{8,0},{2,10},{10,2},{4,12},{12,4},{6,14},{14,6},{16,24},{24,... | collective-permute-start | bytes 1179656 | tf_op jit(solution)/shard_map/ppermute | solution.py:508
  43.8 11.1 %collective-permute-start.14 = (f32[4,32,512]{2,1,0:T(8,128)S(1)}, f32[4,32,512]{2,1,0:T(8,128)S(1)}, u32[]{:S(2)}, u32[]{:S(2)}) collective-permute-start(f32[4,32,512]{2,1,0:T(8,128)S(1)} %get-tuple-element.94), channel_id=1, source_target_pairs={{0,4},{2,6},{4,0},{6,2},{8,12},{10,14},{12,8},{14,10},{16,20},{18,... | collective-permute-start | bytes 786440 | tf_op jit(solution)/shard_map/ppermute | solution.py:491
  51.9 16.9 %collective-permute-start.16 = (f32[4,32,512]{2,1,0:T(8,128)S(1)}, f32[4,32,512]{2,1,0:T(8,128)S(1)}, u32[]{:S(2)}, u32[]{:S(2)}) collective-permute-start(f32[4,32,512]{2,1,0:T(8,128)S(1)} %get-tuple-element.98), channel_id=1, source_target_pairs={{0,2},{2,0},{4,6},{6,4},{8,10},{10,8},{12,14},{14,12},{16,18},{18,... | collective-permute-start | bytes 786440 | tf_op jit(solution)/shard_map/ppermute | solution.py:491
  54.9 22.2 %collective-permute-start.19 = (f32[6,32,512]{2,1,0:T(8,128)S(1)}, f32[6,32,512]{2,1,0:T(8,128)S(1)}, u32[]{:S(2)}, u32[]{:S(2)}) collective-permute-start(f32[6,32,512]{2,1,0:T(8,128)S(1)} %get-tuple-element.103.early_sent), channel_id=1, source_target_pairs={{8,16},{16,8},{10,18},{18,10},{12,20},{20,12},{14,22},{22,14},{24,... | collective-permute-start | bytes 1179656 | tf_op jit(solution)/shard_map/ppermute | solution.py:508
  57.9 23.0 %collective-permute-start.20 = (f32[6,32,512]{2,1,0:T(8,128)S(1)}, f32[6,32,512]{2,1,0:T(8,128)S(1)}, u32[]{:S(2)}, u32[]{:S(2)}) collective-permute-start(f32[6,32,512]{2,1,0:T(8,128)S(1)} %get-tuple-element.104.late_sent), channel_id=1, source_target_pairs={{0,8},{8,0},{2,10},{10,2},{4,12},{12,4},{6,14},{14,6},{16,24},{24,... | collective-permute-start | bytes 1179656 | tf_op jit(solution)/shard_map/ppermute | solution.py:508
  60.2 11.6 %collective-permute-start.17 = (f32[4,32,512]{2,1,0:T(8,128)S(1)}, f32[4,32,512]{2,1,0:T(8,128)S(1)}, u32[]{:S(2)}, u32[]{:S(2)}) collective-permute-start(f32[4,32,512]{2,1,0:T(8,128)S(1)} %get-tuple-element.99), channel_id=1, source_target_pairs={{0,4},{2,6},{4,0},{6,2},{8,12},{10,14},{12,8},{14,10},{16,20},{18,... | collective-permute-start | bytes 786440 | tf_op jit(solution)/shard_map/ppermute | solution.py:491
  63.9 10.8 %collective-permute-start.18 = (f32[4,32,512]{2,1,0:T(8,128)S(1)}, f32[4,32,512]{2,1,0:T(8,128)S(1)}, u32[]{:S(2)}, u32[]{:S(2)}) collective-permute-start(f32[4,32,512]{2,1,0:T(8,128)S(1)} %get-tuple-element.100), channel_id=1, source_target_pairs={{0,6},{2,4},{4,2},{6,0},{8,14},{10,12},{12,10},{14,8},{16,22},{18,... | collective-permute-start | bytes 786440 | tf_op jit(solution)/shard_map/ppermute | solution.py:491
  68.8 19.5 %collective-permute-start.21 = (f32[4,32,512]{2,1,0:T(8,128)S(1)}, f32[4,32,512]{2,1,0:T(8,128)S(1)}, u32[]{:S(2)}, u32[]{:S(2)}) collective-permute-start(f32[4,32,512]{2,1,0:T(8,128)S(1)} %get-tuple-element.107), channel_id=1, source_target_pairs={{0,2},{2,0},{4,6},{6,4},{8,10},{10,8},{12,14},{14,12},{16,18},{18,... | collective-permute-start | bytes 786440 | tf_op jit(solution)/shard_map/ppermute | solution.py:491
  71.8 22.5 %collective-permute-start.24 = (f32[6,32,512]{2,1,0:T(8,128)S(1)}, f32[6,32,512]{2,1,0:T(8,128)S(1)}, u32[]{:S(2)}, u32[]{:S(2)}) collective-permute-start(f32[6,32,512]{2,1,0:T(8,128)S(1)} %get-tuple-element.113.early_sent), channel_id=1, source_target_pairs={{8,16},{16,8},{10,18},{18,10},{12,20},{20,12},{14,22},{22,14},{24,... | collective-permute-start | bytes 1179656 | tf_op jit(solution)/shard_map/ppermute | solution.py:508
  74.8 22.9 %collective-permute-start.25 = (f32[6,32,512]{2,1,0:T(8,128)S(1)}, f32[6,32,512]{2,1,0:T(8,128)S(1)}, u32[]{:S(2)}, u32[]{:S(2)}) collective-permute-start(f32[6,32,512]{2,1,0:T(8,128)S(1)} %get-tuple-element.114.late_sent), channel_id=1, source_target_pairs={{0,8},{8,0},{2,10},{10,2},{4,12},{12,4},{6,14},{14,6},{16,24},{24,... | collective-permute-start | bytes 1179656 | tf_op jit(solution)/shard_map/ppermute | solution.py:508
  77.1 11.3 %collective-permute-start.22 = (f32[4,32,512]{2,1,0:T(8,128)S(1)}, f32[4,32,512]{2,1,0:T(8,128)S(1)}, u32[]{:S(2)}, u32[]{:S(2)}) collective-permute-start(f32[4,32,512]{2,1,0:T(8,128)S(1)} %get-tuple-element.108), channel_id=1, source_target_pairs={{0,4},{2,6},{4,0},{6,2},{8,12},{10,14},{12,8},{14,10},{16,20},{18,... | collective-permute-start | bytes 786440 | tf_op jit(solution)/shard_map/ppermute | solution.py:491
  88.3 14.2 %collective-permute-start.26 = (f32[4,32,512]{2,1,0:T(8,128)S(1)}, f32[4,32,512]{2,1,0:T(8,128)S(1)}, u32[]{:S(2)}, u32[]{:S(2)}) collective-permute-start(f32[4,32,512]{2,1,0:T(8,128)S(1)} %get-tuple-element.117), channel_id=1, source_target_pairs={{0,2},{2,0},{4,6},{6,4},{8,10},{10,8},{12,14},{14,12},{16,18},{18,... | collective-permute-start | bytes 786440 | tf_op jit(solution)/shard_map/ppermute | solution.py:491
  88.4 14.6 %collective-permute-start.27 = (f32[4,32,512]{2,1,0:T(8,128)S(1)}, f32[4,32,512]{2,1,0:T(8,128)S(1)}, u32[]{:S(2)}, u32[]{:S(2)}) collective-permute-start(f32[4,32,512]{2,1,0:T(8,128)S(1)} %get-tuple-element.118), channel_id=1, source_target_pairs={{0,4},{2,6},{4,0},{6,2},{8,12},{10,14},{12,8},{14,10},{16,20},{18,... | collective-permute-start | bytes 786440 | tf_op jit(solution)/shard_map/ppermute | solution.py:491
  91.0 12.0 %collective-permute-start.28 = (f32[4,32,512]{2,1,0:T(8,128)S(1)}, f32[4,32,512]{2,1,0:T(8,128)S(1)}, u32[]{:S(2)}, u32[]{:S(2)}) collective-permute-start(f32[4,32,512]{2,1,0:T(8,128)S(1)} %get-tuple-element.119), channel_id=1, source_target_pairs={{0,6},{2,4},{4,2},{6,0},{8,14},{10,12},{12,10},{14,8},{16,22},{18,... | collective-permute-start | bytes 786440 | tf_op jit(solution)/shard_map/ppermute | solution.py:491
  102.5 12.4 %collective-permute-start.31 = (f32[4,32,512]{2,1,0:T(8,128)S(1)}, f32[4,32,512]{2,1,0:T(8,128)S(1)}, u32[]{:S(2)}, u32[]{:S(2)}) collective-permute-start(f32[4,32,512]{2,1,0:T(8,128)S(1)} %get-tuple-element.125), channel_id=1, source_target_pairs={{0,6},{2,4},{4,2},{6,0},{8,14},{10,12},{12,10},{14,8},{16,22},{18,... | collective-permute-start | bytes 786440 | tf_op jit(solution)/shard_map/ppermute | solution.py:491
  (16 other events, 183.3 us)

commit v4 on v3

--- a/solution.py
+++ b/solution.py
@@ -207,7 +207,7 @@
 
 
 def tile_of(share):
-    return 16 if share % 16 == 0 else 8
+    return next(height for height in (32, 16, 8) if share % height == 0)
 
 
 def bin_rates(pieces, per_parity, member, half_bins, place, shape):

time: 120 us -> 119 us (level)
  Pallas kernels: 48.3 us -> 46.4 us
    ppermute x24, waiting for transfers between devices: 17.9 us -> 19.9 us  [swap(): lax.ppermute(parts[d], axes, swaps[d])]
    pallas_call x4, Pallas kernels: 11.7 us -> 9.67 us  [evolve_chunk(): pl.pallas_call(functools.partial(evolve_kernel, pieces, per_parity, half_...]
  transfers between devices with their start and end apart: 32 -> 32, of which waited for: 10 -> 12; matrix products, arithmetic and copies ran while one was open for 0% -> 0% of each run, Pallas kernels for 32% -> 31%
where the time goes in v4:
time: 119 us; the launch traced here: 118 us
  Pallas kernels  46.4 us (39%)
  starting transfers between devices  41.5 us (35%)
  waiting for transfers between devices  29.5 us (25%)
    ppermute x8, starting transfers between devices, shards(): lax.ppermute(values, axes, some)  21.5 us
    ppermute x24, starting transfers between devices, swap(): lax.ppermute(parts[d], axes, swaps[d])  20 us
    ppermute x24, waiting for transfers between devices, swap(): lax.ppermute(parts[d], axes, swaps[d])  19.9 us
    pallas_call x2, Pallas kernels, forward_chunks(): pl.pallas_call(functools.partial(forward_kernel, chunks, per_parity), gri...  13.7 us
    pallas_call x4, Pallas kernels, inverse_chunks(): pl.pallas_call(functools.partial(inverse_kernel, chunks, held, last), gri...  11.7 us
    pallas_call x4, Pallas kernels, correct_chunk(): pl.pallas_call(functools.partial(correct_kernel, pieces, per_parity, half...  11.4 us
    ppermute x8, waiting for transfers between devices, shards(): lax.ppermute(values, axes, some)  9.68 us
    pallas_call x4, Pallas kernels, evolve_chunk(): pl.pallas_call(functools.partial(evolve_kernel, pieces, per_parity, half_...  9.67 us
  transfers between devices with their start and end apart: 32, of which 12 were waited for; matrix products, arithmetic and copies ran while one was open for 0% of the time, Pallas kernels for 31%

profile of v4, /device:TPU:3, one launch (start us, length us, event | category | flops | bytes accessed | tf_op | source)
XLA Modules:
  0.0 117.9 jit_solution(5605716146214582767)
XLA Ops:
  0.1 6.8 %shard_map.181 = (f32[4,32,512]{2,1,0:T(8,128)S(1)}, f32[4,32,512]{2,1,0:T(8,128)S(1)}, f32[4,32,512]{2,1,0:T(8,128)S(1)}, f32[4,32,512]{2,1,0:T(8,128)S(1)}, f3...) custom-call(s32[4]{0:T(128)S(1)} %pad_add_fusion.info, ...), custom_call_target="tpu_custom_call" | custom-call | flops 6918000 | bytes 22140000 | tf_op jit(solution)/shard_map/pallas_call | solution.py:194
  11.5 6.8 %shard_map.182 = (f32[4,32,512]{2,1,0:T(8,128)S(1)}, f32[4,32,512]{2,1,0:T(8,128)S(1)}, f32[4,32,512]{2,1,0:T(8,128)S(1)}, f32[4,32,512]{2,1,0:T(8,128)S(1)}, f3...) custom-call(s32[4]{0:T(128)S(1)} %get-tuple-element.67.info, ...), custom_call_target="tpu_custom_call" | custom-call | flops 6918000 | bytes 22140000 | tf_op jit(solution)/shard_map/pallas_call | solution.py:194
  18.4 3.4 %collective-permute-done.2.refs_3_ = f32[4,32,512]{2,1,0:T(8,128)S(1)} collective-permute-done((f32[4,32,512]{2,1,0:T(8,128)S(1)}, f32[4,32,512]{2,1,0:T(8,128)S(1)}, u32[]{:S(2)}, u32[]{:S(2)}) %collective-permute-start.2) | collective-permute-done | bytes 262176 | tf_op jit(solution)/shard_map/ppermute | solution.py:491
  24.2 5.2 %collective-permute-start.6 = (f32[6,32,512]{2,1,0:T(8,128)S(1)}, f32[6,32,512]{2,1,0:T(8,128)S(1)}, u32[]{:S(2)}, u32[]{:S(2)}) collective-permute-start(f32[6,32,512]{2,1,0:T(8,128)S(1)} %get-tuple-element.80.early_sent), channel_id=1, source_target_pairs={{8,16},{16,8},{10,18},{18,10},{12,20},{20,12},{14,22},{22,14},{24,... | collective-permute-start | bytes 1179656 | tf_op jit(solution)/shard_map/ppermute | solution.py:508
  30.9 2.4 %collective-permute-done.5.refs_3_ = f32[4,32,512]{2,1,0:T(8,128)S(1)} collective-permute-done((f32[4,32,512]{2,1,0:T(8,128)S(1)}, f32[4,32,512]{2,1,0:T(8,128)S(1)}, u32[]{:S(2)}, u32[]{:S(2)}) %collective-permute-start.5) | collective-permute-done | bytes 262176 | tf_op jit(solution)/shard_map/ppermute | solution.py:491
  36.4 5.2 %collective-permute-start.11 = (f32[6,32,512]{2,1,0:T(8,128)S(1)}, f32[6,32,512]{2,1,0:T(8,128)S(1)}, u32[]{:S(2)}, u32[]{:S(2)}) collective-permute-start(f32[6,32,512]{2,1,0:T(8,128)S(1)} %get-tuple-element.89.early_sent), channel_id=1, source_target_pairs={{8,16},{16,8},{10,18},{18,10},{12,20},{20,12},{14,22},{22,14},{24,... | collective-permute-start | bytes 1179656 | tf_op jit(solution)/shard_map/ppermute | solution.py:508
  48.6 2.8 %shard_map.185 = (f32[4,32,512]{2,1,0:T(8,128)S(1)}, f32[4,32,512]{2,1,0:T(8,128)S(1)}, f32[4,32,512]{2,1,0:T(8,128)S(1)}, f32[4,32,512]{2,1,0:T(8,128)S(1)}, s32[4]{0:T(128)S(1)}) custom-call(s32[4]{0:T(128)S(1)} %get-tuple-element.78.info, f32[16,32,512]{2,1,0:T(8,128)S(1)} %get-tuple-element.79.done, f32[6,32,512]{2,1,0:T(8,128)S(1)} %get-tuple-element.80.early_sent, ...), custom_call_target="tpu_custom_call" | custom-call | flops 4035500 | bytes 12915000 | tf_op jit(solution)/shard_map/pallas_call | solution.py:386
  51.5 2.4 %shard_map.186 = (f32[16,32,512]{2,1,0:T(8,128)S(1)}, f32[6,32,512]{2,1,0:T(8,128)S(1)}, f32[6,32,512]{2,1,0:T(8,128)S(1)}, s32[4]{0:T(128)S(1)}) custom-call(s32[4]{0:T(128)S(1)} %get-tuple-element.82.info, f32[4,32,512]{2,1,0:T(8,128)S(1)} %get-tuple-element.83.refs_0_, f32[4,32,512]{2,1,0:T(8,128)S(1)} %collective-permute-done.8.refs_1_, ...), custom_call_target="tpu_custom_call" | custom-call | flops 3459000 | bytes 11070000 | tf_op jit(solution)/shard_map/pallas_call | solution.py:301
  54.0 3.2 %collective-permute-start.19 = (f32[6,32,512]{2,1,0:T(8,128)S(1)}, f32[6,32,512]{2,1,0:T(8,128)S(1)}, u32[]{:S(2)}, u32[]{:S(2)}) collective-permute-start(f32[6,32,512]{2,1,0:T(8,128)S(1)} %get-tuple-element.103.early_sent), channel_id=1, source_target_pairs={{8,16},{16,8},{10,18},{18,10},{12,20},{20,12},{14,22},{22,14},{24,... | collective-permute-start | bytes 1179656 | tf_op jit(solution)/shard_map/ppermute | solution.py:508
  61.0 2.4 %collective-permute-done.12.late_got = f32[6,32,512]{2,1,0:T(8,128)S(1)} collective-permute-done((f32[6,32,512]{2,1,0:T(8,128)S(1)}, f32[6,32,512]{2,1,0:T(8,128)S(1)}, u32[]{:S(2)}, u32[]{:S(2)}) %collective-permute-start.12) | collective-permute-done | bytes 393248 | tf_op jit(solution)/shard_map/ppermute | solution.py:508
  65.5 2.8 %shard_map.187 = (f32[4,32,512]{2,1,0:T(8,128)S(1)}, f32[4,32,512]{2,1,0:T(8,128)S(1)}, f32[4,32,512]{2,1,0:T(8,128)S(1)}, f32[4,32,512]{2,1,0:T(8,128)S(1)}, s32[4]{0:T(128)S(1)}) custom-call(s32[4]{0:T(128)S(1)} %get-tuple-element.87.info, f32[16,32,512]{2,1,0:T(8,128)S(1)} %get-tuple-element.88.done, f32[6,32,512]{2,1,0:T(8,128)S(1)} %get-tuple-element.89.early_sent, ...), custom_call_target="tpu_custom_call" | custom-call | flops 4035500 | bytes 12915000 | tf_op jit(solution)/shard_map/pallas_call | solution.py:386
  68.4 2.4 %shard_map.188 = (f32[16,32,512]{2,1,0:T(8,128)S(1)}, f32[6,32,512]{2,1,0:T(8,128)S(1)}, f32[6,32,512]{2,1,0:T(8,128)S(1)}, s32[4]{0:T(128)S(1)}) custom-call(s32[4]{0:T(128)S(1)} %get-tuple-element.91.info, f32[4,32,512]{2,1,0:T(8,128)S(1)} %get-tuple-element.92.refs_0_, f32[4,32,512]{2,1,0:T(8,128)S(1)} %collective-permute-done.13.refs_1_, ...), custom_call_target="tpu_custom_call" | custom-call | flops 3459000 | bytes 11070000 | tf_op jit(solution)/shard_map/pallas_call | solution.py:301
  70.8 2.8 %collective-permute-start.24 = (f32[6,32,512]{2,1,0:T(8,128)S(1)}, f32[6,32,512]{2,1,0:T(8,128)S(1)}, u32[]{:S(2)}, u32[]{:S(2)}) collective-permute-start(f32[6,32,512]{2,1,0:T(8,128)S(1)} %get-tuple-element.113.early_sent), channel_id=1, source_target_pairs={{8,16},{16,8},{10,18},{18,10},{12,20},{20,12},{14,22},{22,14},{24,... | collective-permute-start | bytes 1179656 | tf_op jit(solution)/shard_map/ppermute | solution.py:508
  73.7 2.9 %collective-permute-start.25 = (f32[6,32,512]{2,1,0:T(8,128)S(1)}, f32[6,32,512]{2,1,0:T(8,128)S(1)}, u32[]{:S(2)}, u32[]{:S(2)}) collective-permute-start(f32[6,32,512]{2,1,0:T(8,128)S(1)} %get-tuple-element.114.late_sent), channel_id=1, source_target_pairs={{0,8},{8,0},{2,10},{10,2},{4,12},{12,4},{6,14},{14,6},{16,24},{24,... | collective-permute-start | bytes 1179656 | tf_op jit(solution)/shard_map/ppermute | solution.py:508
  77.8 2.5 %collective-permute-done.20.late_got = f32[6,32,512]{2,1,0:T(8,128)S(1)} collective-permute-done((f32[6,32,512]{2,1,0:T(8,128)S(1)}, f32[6,32,512]{2,1,0:T(8,128)S(1)}, u32[]{:S(2)}, u32[]{:S(2)}) %collective-permute-start.20) | collective-permute-done | bytes 393248 | tf_op jit(solution)/shard_map/ppermute | solution.py:508
  82.4 2.6 %shard_map.189 = (f32[2,512,512]{2,1,0:T(8,128)S(1)}, s32[4]{0:T(128)S(1)}) custom-call(s32[4]{0:T(128)S(1)} %get-tuple-element.96.info, f32[4,32,512]{2,1,0:T(8,128)S(1)} %get-tuple-element.97.refs_0_, f32[4,32,512]{2,1,0:T(8,128)S(1)} %collective-permute-done.16.refs_1_, f32[4,32,512]{2,1,0:T(8,128)S(1)} %collective-permute-done.17.refs_2_, ...), custom_call_target="tpu_custom_call" | custom-call | flops 4612000 | bytes 14760000 | tf_op jit(solution)/shard_map/pallas_call | solution.py:446
  85.0 2.9 %shard_map.190 = (f32[4,32,512]{2,1,0:T(8,128)S(1)}, f32[4,32,512]{2,1,0:T(8,128)S(1)}, f32[4,32,512]{2,1,0:T(8,128)S(1)}, f32[4,32,512]{2,1,0:T(8,128)S(1)}, s32[4]{0:T(128)S(1)}) custom-call(s32[4]{0:T(128)S(1)} %get-tuple-element.101.info, f32[16,32,512]{2,1,0:T(8,128)S(1)} %get-tuple-element.102.done, f32[6,32,512]{2,1,0:T(8,128)S(1)} %get-tuple-element.103.early_sent, ...), custom_call_target="tpu_custom_call" | custom-call | flops 4035500 | bytes 12915000 | tf_op jit(solution)/shard_map/pallas_call | solution.py:386
  91.0 2.7 %shard_map.191 = (f32[2,512,512]{2,1,0:T(8,128)S(1)}, s32[4]{0:T(128)S(1)}) custom-call(s32[4]{0:T(128)S(1)} %get-tuple-element.105.info, f32[4,32,512]{2,1,0:T(8,128)S(1)} %get-tuple-element.106.refs_0_, f32[4,32,512]{2,1,0:T(8,128)S(1)} %collective-permute-done.21.refs_1_, f32[4,32,512]{2,1,0:T(8,128)S(1)} %collective-permute-done.22.refs_2_, ...), custom_call_target="tpu_custom_call" | custom-call | flops 4612000 | bytes 14760000 | tf_op jit(solution)/shard_map/pallas_call | solution.py:446
  93.8 3.5 %collective-permute-done.25.late_got = f32[6,32,512]{2,1,0:T(8,128)S(1)} collective-permute-done((f32[6,32,512]{2,1,0:T(8,128)S(1)}, f32[6,32,512]{2,1,0:T(8,128)S(1)}, u32[]{:S(2)}, u32[]{:S(2)}) %collective-permute-start.25) | collective-permute-done | bytes 393248 | tf_op jit(solution)/shard_map/ppermute | solution.py:508
  97.2 2.8 %shard_map.192 = (f32[4,32,512]{2,1,0:T(8,128)S(1)}, f32[4,32,512]{2,1,0:T(8,128)S(1)}, f32[4,32,512]{2,1,0:T(8,128)S(1)}, f32[4,32,512]{2,1,0:T(8,128)S(1)}, s32[4]{0:T(128)S(1)}) custom-call(s32[4]{0:T(128)S(1)} %get-tuple-element.111.info, f32[16,32,512]{2,1,0:T(8,128)S(1)} %get-tuple-element.112.done, f32[6,32,512]{2,1,0:T(8,128)S(1)} %get-tuple-element.113.early_sent, ...), custom_call_target="tpu_custom_call" | custom-call | flops 4035500 | bytes 12915000 | tf_op jit(solution)/shard_map/pallas_call | solution.py:386
  102.6 2.9 %shard_map.193 = (f32[2,512,512]{2,1,0:T(8,128)S(1)}, f32[2,512,512]{2,1,0:T(8,128)S(1)}, s32[4]{0:T(128)S(1)}) custom-call(s32[4]{0:T(128)S(1)} %get-tuple-element.115.info, f32[4,32,512]{2,1,0:T(8,128)S(1)} %get-tuple-element.116.refs_0_, f32[4,32,512]{2,1,0:T(8,128)S(1)} %collective-permute-done.26.refs_1_, ...), custom_call_target="tpu_custom_call" | custom-call | flops 4612000 | bytes 14760000 | tf_op jit(solution)/shard_map/pallas_call | solution.py:446
  105.5 3.2 %collective-permute-done.30.refs_2_ = f32[4,32,512]{2,1,0:T(8,128)S(1)} collective-permute-done((f32[4,32,512]{2,1,0:T(8,128)S(1)}, f32[4,32,512]{2,1,0:T(8,128)S(1)}, u32[]{:S(2)}, u32[]{:S(2)}) %collective-permute-start.30) | collective-permute-done | bytes 262176 | tf_op jit(solution)/shard_map/ppermute | solution.py:491
  108.7 5.8 %collective-permute-done.31.refs_3_ = f32[4,32,512]{2,1,0:T(8,128)S(1)} collective-permute-done((f32[4,32,512]{2,1,0:T(8,128)S(1)}, f32[4,32,512]{2,1,0:T(8,128)S(1)}, u32[]{:S(2)}, u32[]{:S(2)}) %collective-permute-start.31) | collective-permute-done | bytes 262176 | tf_op jit(solution)/shard_map/ppermute | solution.py:491
  114.5 3.4 %shard_map.194 = (f32[2,512,1024]{2,1,0:T(8,128)}, s32[4]{0:T(128)}) custom-call(s32[4]{0:T(128)S(1)} %get-tuple-element.121.info, f32[4,32,512]{2,1,0:T(8,128)S(1)} %get-tuple-element.122.refs_0_, f32[4,32,512]{2,1,0:T(8,128)S(1)} %collective-permute-done.29.refs_1_, f32[4,32,512]{2,1,0:T(8,128)S(1)} %collective-permute-done.30.refs_2_, ...), custom_call_target="tpu_custom_call" | custom-call | flops 4612000 | bytes 14760000 | tf_op jit(solution)/shard_map/pallas_call | solution.py:446
  (71 shorter events, 33.5 us)
Async XLA Ops:
  7.7 10.7 %collective-permute-start.1 = (f32[4,32,512]{2,1,0:T(8,128)S(1)}, f32[4,32,512]{2,1,0:T(8,128)S(1)}, u32[]{:S(2)}, u32[]{:S(2)}) collective-permute-start(f32[4,32,512]{2,1,0:T(8,128)S(1)} %get-tuple-element.71), channel_id=1, source_target_pairs={{0,4},{2,6},{4,0},{6,2},{8,12},{10,14},{12,8},{14,10},{16,20},{18,... | collective-permute-start | bytes 786440 | tf_op jit(solution)/shard_map/ppermute | solution.py:491
  8.9 12.9 %collective-permute-start.2 = (f32[4,32,512]{2,1,0:T(8,128)S(1)}, f32[4,32,512]{2,1,0:T(8,128)S(1)}, u32[]{:S(2)}, u32[]{:S(2)}) collective-permute-start(f32[4,32,512]{2,1,0:T(8,128)S(1)} %get-tuple-element.72), channel_id=1, source_target_pairs={{0,6},{2,4},{4,2},{6,0},{8,14},{10,12},{12,10},{14,8},{16,22},{18,... | collective-permute-start | bytes 786440 | tf_op jit(solution)/shard_map/ppermute | solution.py:491
  9.4 20.1 %collective-permute-start.3 = (f32[4,32,512]{2,1,0:T(8,128)S(1)}, f32[4,32,512]{2,1,0:T(8,128)S(1)}, u32[]{:S(2)}, u32[]{:S(2)}) collective-permute-start(f32[4,32,512]{2,1,0:T(8,128)S(1)} %get-tuple-element.75), channel_id=1, source_target_pairs={{0,2},{2,0},{4,6},{6,4},{8,10},{10,8},{12,14},{14,12},{16,18},{18,... | collective-permute-start | bytes 786440 | tf_op jit(solution)/shard_map/ppermute | solution.py:491
  9.5 20.1 %collective-permute-start.4 = (f32[4,32,512]{2,1,0:T(8,128)S(1)}, f32[4,32,512]{2,1,0:T(8,128)S(1)}, u32[]{:S(2)}, u32[]{:S(2)}) collective-permute-start(f32[4,32,512]{2,1,0:T(8,128)S(1)} %get-tuple-element.76), channel_id=1, source_target_pairs={{0,4},{2,6},{4,0},{6,2},{8,12},{10,14},{12,8},{14,10},{16,20},{18,... | collective-permute-start | bytes 786440 | tf_op jit(solution)/shard_map/ppermute | solution.py:491
  10.8 22.5 %collective-permute-start.5 = (f32[4,32,512]{2,1,0:T(8,128)S(1)}, f32[4,32,512]{2,1,0:T(8,128)S(1)}, u32[]{:S(2)}, u32[]{:S(2)}) collective-permute-start(f32[4,32,512]{2,1,0:T(8,128)S(1)} %get-tuple-element.77), channel_id=1, source_target_pairs={{0,6},{2,4},{4,2},{6,0},{8,14},{10,12},{12,10},{14,8},{16,22},{18,... | collective-permute-start | bytes 786440 | tf_op jit(solution)/shard_map/ppermute | solution.py:491
  24.2 19.8 %collective-permute-start.6 = (f32[6,32,512]{2,1,0:T(8,128)S(1)}, f32[6,32,512]{2,1,0:T(8,128)S(1)}, u32[]{:S(2)}, u32[]{:S(2)}) collective-permute-start(f32[6,32,512]{2,1,0:T(8,128)S(1)} %get-tuple-element.80.early_sent), channel_id=1, source_target_pairs={{8,16},{16,8},{10,18},{18,10},{12,20},{20,12},{14,22},{22,14},{24,... | collective-permute-start | bytes 1179656 | tf_op jit(solution)/shard_map/ppermute | solution.py:508
  29.4 17.1 %collective-permute-start.7 = (f32[6,32,512]{2,1,0:T(8,128)S(1)}, f32[6,32,512]{2,1,0:T(8,128)S(1)}, u32[]{:S(2)}, u32[]{:S(2)}) collective-permute-start(f32[6,32,512]{2,1,0:T(8,128)S(1)} %get-tuple-element.81.late_sent), channel_id=1, source_target_pairs={{0,8},{8,0},{2,10},{10,2},{4,12},{12,4},{6,14},{14,6},{16,24},{24,... | collective-permute-start | bytes 1179656 | tf_op jit(solution)/shard_map/ppermute | solution.py:508
  29.6 11.9 %collective-permute-start.9 = (f32[4,32,512]{2,1,0:T(8,128)S(1)}, f32[4,32,512]{2,1,0:T(8,128)S(1)}, u32[]{:S(2)}, u32[]{:S(2)}) collective-permute-start(f32[4,32,512]{2,1,0:T(8,128)S(1)} %get-tuple-element.85), channel_id=1, source_target_pairs={{0,4},{2,6},{4,0},{6,2},{8,12},{10,14},{12,8},{14,10},{16,20},{18,... | collective-permute-start | bytes 786440 | tf_op jit(solution)/shard_map/ppermute | solution.py:491
  33.3 10.5 %collective-permute-start.10 = (f32[4,32,512]{2,1,0:T(8,128)S(1)}, f32[4,32,512]{2,1,0:T(8,128)S(1)}, u32[]{:S(2)}, u32[]{:S(2)}) collective-permute-start(f32[4,32,512]{2,1,0:T(8,128)S(1)} %get-tuple-element.86), channel_id=1, source_target_pairs={{0,6},{2,4},{4,2},{6,0},{8,14},{10,12},{12,10},{14,8},{16,22},{18,... | collective-permute-start | bytes 786440 | tf_op jit(solution)/shard_map/ppermute | solution.py:491
  36.4 23.4 %collective-permute-start.11 = (f32[6,32,512]{2,1,0:T(8,128)S(1)}, f32[6,32,512]{2,1,0:T(8,128)S(1)}, u32[]{:S(2)}, u32[]{:S(2)}) collective-permute-start(f32[6,32,512]{2,1,0:T(8,128)S(1)} %get-tuple-element.89.early_sent), channel_id=1, source_target_pairs={{8,16},{16,8},{10,18},{18,10},{12,20},{20,12},{14,22},{22,14},{24,... | collective-permute-start | bytes 1179656 | tf_op jit(solution)/shard_map/ppermute | solution.py:508
  41.6 21.9 %collective-permute-start.12 = (f32[6,32,512]{2,1,0:T(8,128)S(1)}, f32[6,32,512]{2,1,0:T(8,128)S(1)}, u32[]{:S(2)}, u32[]{:S(2)}) collective-permute-start(f32[6,32,512]{2,1,0:T(8,128)S(1)} %get-tuple-element.90.late_sent), channel_id=1, source_target_pairs={{0,8},{8,0},{2,10},{10,2},{4,12},{12,4},{6,14},{14,6},{16,24},{24,... | collective-permute-start | bytes 1179656 | tf_op jit(solution)/shard_map/ppermute | solution.py:508
  46.5 11.1 %collective-permute-start.15 = (f32[4,32,512]{2,1,0:T(8,128)S(1)}, f32[4,32,512]{2,1,0:T(8,128)S(1)}, u32[]{:S(2)}, u32[]{:S(2)}) collective-permute-start(f32[4,32,512]{2,1,0:T(8,128)S(1)} %get-tuple-element.95), channel_id=1, source_target_pairs={{0,6},{2,4},{4,2},{6,0},{8,14},{10,12},{12,10},{14,8},{16,22},{18,... | collective-permute-start | bytes 786440 | tf_op jit(solution)/shard_map/ppermute | solution.py:491
  51.4 16.9 %collective-permute-start.16 = (f32[4,32,512]{2,1,0:T(8,128)S(1)}, f32[4,32,512]{2,1,0:T(8,128)S(1)}, u32[]{:S(2)}, u32[]{:S(2)}) collective-permute-start(f32[4,32,512]{2,1,0:T(8,128)S(1)} %get-tuple-element.98), channel_id=1, source_target_pairs={{0,2},{2,0},{4,6},{6,4},{8,10},{10,8},{12,14},{14,12},{16,18},{18,... | collective-permute-start | bytes 786440 | tf_op jit(solution)/shard_map/ppermute | solution.py:491
  54.0 22.6 %collective-permute-start.19 = (f32[6,32,512]{2,1,0:T(8,128)S(1)}, f32[6,32,512]{2,1,0:T(8,128)S(1)}, u32[]{:S(2)}, u32[]{:S(2)}) collective-permute-start(f32[6,32,512]{2,1,0:T(8,128)S(1)} %get-tuple-element.103.early_sent), channel_id=1, source_target_pairs={{8,16},{16,8},{10,18},{18,10},{12,20},{20,12},{14,22},{22,14},{24,... | collective-permute-start | bytes 1179656 | tf_op jit(solution)/shard_map/ppermute | solution.py:508
  57.7 22.6 %collective-permute-start.20 = (f32[6,32,512]{2,1,0:T(8,128)S(1)}, f32[6,32,512]{2,1,0:T(8,128)S(1)}, u32[]{:S(2)}, u32[]{:S(2)}) collective-permute-start(f32[6,32,512]{2,1,0:T(8,128)S(1)} %get-tuple-element.104.late_sent), channel_id=1, source_target_pairs={{0,8},{8,0},{2,10},{10,2},{4,12},{12,4},{6,14},{14,6},{16,24},{24,... | collective-permute-start | bytes 1179656 | tf_op jit(solution)/shard_map/ppermute | solution.py:508
  59.7 11.1 %collective-permute-start.17 = (f32[4,32,512]{2,1,0:T(8,128)S(1)}, f32[4,32,512]{2,1,0:T(8,128)S(1)}, u32[]{:S(2)}, u32[]{:S(2)}) collective-permute-start(f32[4,32,512]{2,1,0:T(8,128)S(1)} %get-tuple-element.99), channel_id=1, source_target_pairs={{0,4},{2,6},{4,0},{6,2},{8,12},{10,14},{12,8},{14,10},{16,20},{18,... | collective-permute-start | bytes 786440 | tf_op jit(solution)/shard_map/ppermute | solution.py:491
  68.3 19.6 %collective-permute-start.21 = (f32[4,32,512]{2,1,0:T(8,128)S(1)}, f32[4,32,512]{2,1,0:T(8,128)S(1)}, u32[]{:S(2)}, u32[]{:S(2)}) collective-permute-start(f32[4,32,512]{2,1,0:T(8,128)S(1)} %get-tuple-element.107), channel_id=1, source_target_pairs={{0,2},{2,0},{4,6},{6,4},{8,10},{10,8},{12,14},{14,12},{16,18},{18,... | collective-permute-start | bytes 786440 | tf_op jit(solution)/shard_map/ppermute | solution.py:491
  70.8 22.9 %collective-permute-start.24 = (f32[6,32,512]{2,1,0:T(8,128)S(1)}, f32[6,32,512]{2,1,0:T(8,128)S(1)}, u32[]{:S(2)}, u32[]{:S(2)}) collective-permute-start(f32[6,32,512]{2,1,0:T(8,128)S(1)} %get-tuple-element.113.early_sent), channel_id=1, source_target_pairs={{8,16},{16,8},{10,18},{18,10},{12,20},{20,12},{14,22},{22,14},{24,... | collective-permute-start | bytes 1179656 | tf_op jit(solution)/shard_map/ppermute | solution.py:508
  73.7 23.5 %collective-permute-start.25 = (f32[6,32,512]{2,1,0:T(8,128)S(1)}, f32[6,32,512]{2,1,0:T(8,128)S(1)}, u32[]{:S(2)}, u32[]{:S(2)}) collective-permute-start(f32[6,32,512]{2,1,0:T(8,128)S(1)} %get-tuple-element.114.late_sent), channel_id=1, source_target_pairs={{0,8},{8,0},{2,10},{10,2},{4,12},{12,4},{6,14},{14,6},{16,24},{24,... | collective-permute-start | bytes 1179656 | tf_op jit(solution)/shard_map/ppermute | solution.py:508
  76.6 11.4 %collective-permute-start.22 = (f32[4,32,512]{2,1,0:T(8,128)S(1)}, f32[4,32,512]{2,1,0:T(8,128)S(1)}, u32[]{:S(2)}, u32[]{:S(2)}) collective-permute-start(f32[4,32,512]{2,1,0:T(8,128)S(1)} %get-tuple-element.108), channel_id=1, source_target_pairs={{0,4},{2,6},{4,0},{6,2},{8,12},{10,14},{12,8},{14,10},{16,20},{18,... | collective-permute-start | bytes 786440 | tf_op jit(solution)/shard_map/ppermute | solution.py:491
  87.9 14.2 %collective-permute-start.26 = (f32[4,32,512]{2,1,0:T(8,128)S(1)}, f32[4,32,512]{2,1,0:T(8,128)S(1)}, u32[]{:S(2)}, u32[]{:S(2)}) collective-permute-start(f32[4,32,512]{2,1,0:T(8,128)S(1)} %get-tuple-element.117), channel_id=1, source_target_pairs={{0,2},{2,0},{4,6},{6,4},{8,10},{10,8},{12,14},{14,12},{16,18},{18,... | collective-permute-start | bytes 786440 | tf_op jit(solution)/shard_map/ppermute | solution.py:491
  88.0 14.6 %collective-permute-start.27 = (f32[4,32,512]{2,1,0:T(8,128)S(1)}, f32[4,32,512]{2,1,0:T(8,128)S(1)}, u32[]{:S(2)}, u32[]{:S(2)}) collective-permute-start(f32[4,32,512]{2,1,0:T(8,128)S(1)} %get-tuple-element.118), channel_id=1, source_target_pairs={{0,4},{2,6},{4,0},{6,2},{8,12},{10,14},{12,8},{14,10},{16,20},{18,... | collective-permute-start | bytes 786440 | tf_op jit(solution)/shard_map/ppermute | solution.py:491
  90.5 12.0 %collective-permute-start.28 = (f32[4,32,512]{2,1,0:T(8,128)S(1)}, f32[4,32,512]{2,1,0:T(8,128)S(1)}, u32[]{:S(2)}, u32[]{:S(2)}) collective-permute-start(f32[4,32,512]{2,1,0:T(8,128)S(1)} %get-tuple-element.119), channel_id=1, source_target_pairs={{0,6},{2,4},{4,2},{6,0},{8,14},{10,12},{12,10},{14,8},{16,22},{18,... | collective-permute-start | bytes 786440 | tf_op jit(solution)/shard_map/ppermute | solution.py:491
  102.1 12.4 %collective-permute-start.31 = (f32[4,32,512]{2,1,0:T(8,128)S(1)}, f32[4,32,512]{2,1,0:T(8,128)S(1)}, u32[]{:S(2)}, u32[]{:S(2)}) collective-permute-start(f32[4,32,512]{2,1,0:T(8,128)S(1)} %get-tuple-element.125), channel_id=1, source_target_pairs={{0,6},{2,4},{4,2},{6,0},{8,14},{10,12},{12,10},{14,8},{16,22},{18,... | collective-permute-start | bytes 786440 | tf_op jit(solution)/shard_map/ppermute | solution.py:491
  (16 other events, 182.5 us)

commit v5 on v4

--- a/solution.py
+++ b/solution.py
@@ -187,15 +187,15 @@
     out_specs, out_shape, scratch = [], [], []
     for pieces in chunks:
         share = sum(piece[2] for piece in pieces)
-        block = pl.BlockSpec((2 * rows, share, LANES), lambda i: (0, 0, i))
+        block = pl.BlockSpec((2 * rows, share, WIDE), lambda i: (0, 0, i))
         out_specs += [block] * GANG
         out_shape += [jax.ShapeDtypeStruct((2 * rows, share, width), jnp.float32)] * GANG
-        scratch += [pltpu.VMEM((GANG, share, LANES), jnp.float32)] * 2
+        scratch += [pltpu.VMEM((GANG, share, WIDE), jnp.float32)] * 2
     outs = pl.pallas_call(
         functools.partial(forward_kernel, chunks, per_parity),
-        grid=(width // LANES,),
+        grid=(width // WIDE,),
         in_specs=[scalars()] * 3
-        + [pl.BlockSpec((rows, LANES, n_time), lambda i: (0, i, 0))]
+        + [pl.BlockSpec((rows, WIDE, n_time), lambda i: (0, i, 0))]
         + [pl.BlockSpec(t.shape, lambda i: (0, 0)) for t in flat],
         out_specs=out_specs + [scalars()],
         out_shape=out_shape + [token_shape()],

time: 119 us -> 119 us (level)
  transfers between devices with their start and end apart: 32 -> 32, of which waited for: 12 -> 11; matrix products, arithmetic and copies ran while one was open for 0% -> 0% of each run, Pallas kernels for 31% -> 30%
where the time goes in v5:
time: 119 us; the launch traced here: 117 us
  Pallas kernels  45.5 us (38%)
  starting transfers between devices  41.5 us (35%)
  waiting for transfers between devices  29.9 us (25%)
    ppermute x8, starting transfers between devices, shards(): lax.ppermute(values, axes, some)  21.5 us
    ppermute x24, waiting for transfers between devices, swap(): lax.ppermute(parts[d], axes, swaps[d])  20.2 us
    ppermute x24, starting transfers between devices, swap(): lax.ppermute(parts[d], axes, swaps[d])  20 us
    pallas_call x2, Pallas kernels, forward_chunks(): pl.pallas_call(functools.partial(forward_kernel, chunks, per_parity), gri...  12.8 us
    pallas_call x4, Pallas kernels, inverse_chunks(): pl.pallas_call(functools.partial(inverse_kernel, chunks, held, last), gri...  11.7 us
    pallas_call x4, Pallas kernels, correct_chunk(): pl.pallas_call(functools.partial(correct_kernel, pieces, per_parity, half...  11.4 us
    ppermute x8, waiting for transfers between devices, shards(): lax.ppermute(values, axes, some)  9.69 us
    pallas_call x4, Pallas kernels, evolve_chunk(): pl.pallas_call(functools.partial(evolve_kernel, pieces, per_parity, half_...  9.67 us
  transfers between devices with their start and end apart: 32, of which 11 were waited for; matrix products, arithmetic and copies ran while one was open for 0% of the time, Pallas kernels for 30%

profile of v5, /device:TPU:3, one launch (start us, length us, event | category | flops | bytes accessed | tf_op | source)
XLA Modules:
  0.0 117.4 jit_solution(4226147334611977326)
XLA Ops:
  0.1 6.4 %shard_map.181 = (f32[4,32,512]{2,1,0:T(8,128)S(1)}, f32[4,32,512]{2,1,0:T(8,128)S(1)}, f32[4,32,512]{2,1,0:T(8,128)S(1)}, f32[4,32,512]{2,1,0:T(8,128)S(1)}, f3...) custom-call(s32[4]{0:T(128)S(1)} %pad_add_fusion.info, ...), custom_call_target="tpu_custom_call" | custom-call | flops 6918000 | bytes 22140000 | tf_op jit(solution)/shard_map/pallas_call | solution.py:194
  11.1 6.4 %shard_map.182 = (f32[4,32,512]{2,1,0:T(8,128)S(1)}, f32[4,32,512]{2,1,0:T(8,128)S(1)}, f32[4,32,512]{2,1,0:T(8,128)S(1)}, f32[4,32,512]{2,1,0:T(8,128)S(1)}, f3...) custom-call(s32[4]{0:T(128)S(1)} %get-tuple-element.67.info, ...), custom_call_target="tpu_custom_call" | custom-call | flops 6918000 | bytes 22140000 | tf_op jit(solution)/shard_map/pallas_call | solution.py:194
  17.5 3.8 %collective-permute-done.2.refs_3_ = f32[4,32,512]{2,1,0:T(8,128)S(1)} collective-permute-done((f32[4,32,512]{2,1,0:T(8,128)S(1)}, f32[4,32,512]{2,1,0:T(8,128)S(1)}, u32[]{:S(2)}, u32[]{:S(2)}) %collective-permute-start.2) | collective-permute-done | bytes 262176 | tf_op jit(solution)/shard_map/ppermute | solution.py:491
  21.3 2.4 %shard_map.183 = (f32[16,32,512]{2,1,0:T(8,128)S(1)}, f32[6,32,512]{2,1,0:T(8,128)S(1)}, f32[6,32,512]{2,1,0:T(8,128)S(1)}, s32[4]{0:T(128)S(1)}) custom-call(s32[4]{0:T(128)S(1)} %get-tuple-element.68.info, f32[4,32,512]{2,1,0:T(8,128)S(1)} %get-tuple-element.69.refs_0_, f32[4,32,512]{2,1,0:T(8,128)S(1)} %collective-permute-done.refs_1_, ...), custom_call_target="tpu_custom_call" | custom-call | flops 3459000 | bytes 11070000 | tf_op jit(solution)/shard_map/pallas_call | solution.py:301
  23.7 5.2 %collective-permute-start.6 = (f32[6,32,512]{2,1,0:T(8,128)S(1)}, f32[6,32,512]{2,1,0:T(8,128)S(1)}, u32[]{:S(2)}, u32[]{:S(2)}) collective-permute-start(f32[6,32,512]{2,1,0:T(8,128)S(1)} %get-tuple-element.80.early_sent), channel_id=1, source_target_pairs={{8,16},{16,8},{10,18},{18,10},{12,20},{20,12},{14,22},{22,14},{24,... | collective-permute-start | bytes 1179656 | tf_op jit(solution)/shard_map/ppermute | solution.py:508
  35.9 5.4 %collective-permute-start.11 = (f32[6,32,512]{2,1,0:T(8,128)S(1)}, f32[6,32,512]{2,1,0:T(8,128)S(1)}, u32[]{:S(2)}, u32[]{:S(2)}) collective-permute-start(f32[6,32,512]{2,1,0:T(8,128)S(1)} %get-tuple-element.89.early_sent), channel_id=1, source_target_pairs={{8,16},{16,8},{10,18},{18,10},{12,20},{20,12},{14,22},{22,14},{24,... | collective-permute-start | bytes 1179656 | tf_op jit(solution)/shard_map/ppermute | solution.py:508
  48.1 2.8 %shard_map.185 = (f32[4,32,512]{2,1,0:T(8,128)S(1)}, f32[4,32,512]{2,1,0:T(8,128)S(1)}, f32[4,32,512]{2,1,0:T(8,128)S(1)}, f32[4,32,512]{2,1,0:T(8,128)S(1)}, s32[4]{0:T(128)S(1)}) custom-call(s32[4]{0:T(128)S(1)} %get-tuple-element.78.info, f32[16,32,512]{2,1,0:T(8,128)S(1)} %get-tuple-element.79.done, f32[6,32,512]{2,1,0:T(8,128)S(1)} %get-tuple-element.80.early_sent, ...), custom_call_target="tpu_custom_call" | custom-call | flops 4035500 | bytes 12915000 | tf_op jit(solution)/shard_map/pallas_call | solution.py:386
  51.0 2.4 %shard_map.186 = (f32[16,32,512]{2,1,0:T(8,128)S(1)}, f32[6,32,512]{2,1,0:T(8,128)S(1)}, f32[6,32,512]{2,1,0:T(8,128)S(1)}, s32[4]{0:T(128)S(1)}) custom-call(s32[4]{0:T(128)S(1)} %get-tuple-element.82.info, f32[4,32,512]{2,1,0:T(8,128)S(1)} %get-tuple-element.83.refs_0_, f32[4,32,512]{2,1,0:T(8,128)S(1)} %collective-permute-done.8.refs_1_, ...), custom_call_target="tpu_custom_call" | custom-call | flops 3459000 | bytes 11070000 | tf_op jit(solution)/shard_map/pallas_call | solution.py:301
  53.5 3.0 %collective-permute-start.19 = (f32[6,32,512]{2,1,0:T(8,128)S(1)}, f32[6,32,512]{2,1,0:T(8,128)S(1)}, u32[]{:S(2)}, u32[]{:S(2)}) collective-permute-start(f32[6,32,512]{2,1,0:T(8,128)S(1)} %get-tuple-element.103.early_sent), channel_id=1, source_target_pairs={{8,16},{16,8},{10,18},{18,10},{12,20},{20,12},{14,22},{22,14},{24,... | collective-permute-start | bytes 1179656 | tf_op jit(solution)/shard_map/ppermute | solution.py:508
  60.5 2.5 %collective-permute-done.12.late_got = f32[6,32,512]{2,1,0:T(8,128)S(1)} collective-permute-done((f32[6,32,512]{2,1,0:T(8,128)S(1)}, f32[6,32,512]{2,1,0:T(8,128)S(1)}, u32[]{:S(2)}, u32[]{:S(2)}) %collective-permute-start.12) | collective-permute-done | bytes 393248 | tf_op jit(solution)/shard_map/ppermute | solution.py:508
  65.0 2.8 %shard_map.187 = (f32[4,32,512]{2,1,0:T(8,128)S(1)}, f32[4,32,512]{2,1,0:T(8,128)S(1)}, f32[4,32,512]{2,1,0:T(8,128)S(1)}, f32[4,32,512]{2,1,0:T(8,128)S(1)}, s32[4]{0:T(128)S(1)}) custom-call(s32[4]{0:T(128)S(1)} %get-tuple-element.87.info, f32[16,32,512]{2,1,0:T(8,128)S(1)} %get-tuple-element.88.done, f32[6,32,512]{2,1,0:T(8,128)S(1)} %get-tuple-element.89.early_sent, ...), custom_call_target="tpu_custom_call" | custom-call | flops 4035500 | bytes 12915000 | tf_op jit(solution)/shard_map/pallas_call | solution.py:386
  67.9 2.4 %shard_map.188 = (f32[16,32,512]{2,1,0:T(8,128)S(1)}, f32[6,32,512]{2,1,0:T(8,128)S(1)}, f32[6,32,512]{2,1,0:T(8,128)S(1)}, s32[4]{0:T(128)S(1)}) custom-call(s32[4]{0:T(128)S(1)} %get-tuple-element.91.info, f32[4,32,512]{2,1,0:T(8,128)S(1)} %get-tuple-element.92.refs_0_, f32[4,32,512]{2,1,0:T(8,128)S(1)} %collective-permute-done.13.refs_1_, ...), custom_call_target="tpu_custom_call" | custom-call | flops 3459000 | bytes 11070000 | tf_op jit(solution)/shard_map/pallas_call | solution.py:301
  70.4 3.0 %collective-permute-start.24 = (f32[6,32,512]{2,1,0:T(8,128)S(1)}, f32[6,32,512]{2,1,0:T(8,128)S(1)}, u32[]{:S(2)}, u32[]{:S(2)}) collective-permute-start(f32[6,32,512]{2,1,0:T(8,128)S(1)} %get-tuple-element.113.early_sent), channel_id=1, source_target_pairs={{8,16},{16,8},{10,18},{18,10},{12,20},{20,12},{14,22},{22,14},{24,... | collective-permute-start | bytes 1179656 | tf_op jit(solution)/shard_map/ppermute | solution.py:508
  73.4 2.7 %collective-permute-start.25 = (f32[6,32,512]{2,1,0:T(8,128)S(1)}, f32[6,32,512]{2,1,0:T(8,128)S(1)}, u32[]{:S(2)}, u32[]{:S(2)}) collective-permute-start(f32[6,32,512]{2,1,0:T(8,128)S(1)} %get-tuple-element.114.late_sent), channel_id=1, source_target_pairs={{0,8},{8,0},{2,10},{10,2},{4,12},{12,4},{6,14},{14,6},{16,24},{24,... | collective-permute-start | bytes 1179656 | tf_op jit(solution)/shard_map/ppermute | solution.py:508
  77.4 2.5 %collective-permute-done.20.late_got = f32[6,32,512]{2,1,0:T(8,128)S(1)} collective-permute-done((f32[6,32,512]{2,1,0:T(8,128)S(1)}, f32[6,32,512]{2,1,0:T(8,128)S(1)}, u32[]{:S(2)}, u32[]{:S(2)}) %collective-permute-start.20) | collective-permute-done | bytes 393248 | tf_op jit(solution)/shard_map/ppermute | solution.py:508
  81.9 2.6 %shard_map.189 = (f32[2,512,512]{2,1,0:T(8,128)S(1)}, s32[4]{0:T(128)S(1)}) custom-call(s32[4]{0:T(128)S(1)} %get-tuple-element.96.info, f32[4,32,512]{2,1,0:T(8,128)S(1)} %get-tuple-element.97.refs_0_, f32[4,32,512]{2,1,0:T(8,128)S(1)} %collective-permute-done.16.refs_1_, f32[4,32,512]{2,1,0:T(8,128)S(1)} %collective-permute-done.17.refs_2_, ...), custom_call_target="tpu_custom_call" | custom-call | flops 4612000 | bytes 14760000 | tf_op jit(solution)/shard_map/pallas_call | solution.py:446
  84.6 2.9 %shard_map.190 = (f32[4,32,512]{2,1,0:T(8,128)S(1)}, f32[4,32,512]{2,1,0:T(8,128)S(1)}, f32[4,32,512]{2,1,0:T(8,128)S(1)}, f32[4,32,512]{2,1,0:T(8,128)S(1)}, s32[4]{0:T(128)S(1)}) custom-call(s32[4]{0:T(128)S(1)} %get-tuple-element.101.info, f32[16,32,512]{2,1,0:T(8,128)S(1)} %get-tuple-element.102.done, f32[6,32,512]{2,1,0:T(8,128)S(1)} %get-tuple-element.103.early_sent, ...), custom_call_target="tpu_custom_call" | custom-call | flops 4035500 | bytes 12915000 | tf_op jit(solution)/shard_map/pallas_call | solution.py:386
  90.6 2.7 %shard_map.191 = (f32[2,512,512]{2,1,0:T(8,128)S(1)}, s32[4]{0:T(128)S(1)}) custom-call(s32[4]{0:T(128)S(1)} %get-tuple-element.105.info, f32[4,32,512]{2,1,0:T(8,128)S(1)} %get-tuple-element.106.refs_0_, f32[4,32,512]{2,1,0:T(8,128)S(1)} %collective-permute-done.21.refs_1_, f32[4,32,512]{2,1,0:T(8,128)S(1)} %collective-permute-done.22.refs_2_, ...), custom_call_target="tpu_custom_call" | custom-call | flops 4612000 | bytes 14760000 | tf_op jit(solution)/shard_map/pallas_call | solution.py:446
  93.3 3.5 %collective-permute-done.25.late_got = f32[6,32,512]{2,1,0:T(8,128)S(1)} collective-permute-done((f32[6,32,512]{2,1,0:T(8,128)S(1)}, f32[6,32,512]{2,1,0:T(8,128)S(1)}, u32[]{:S(2)}, u32[]{:S(2)}) %collective-permute-start.25) | collective-permute-done | bytes 393248 | tf_op jit(solution)/shard_map/ppermute | solution.py:508
  96.8 2.8 %shard_map.192 = (f32[4,32,512]{2,1,0:T(8,128)S(1)}, f32[4,32,512]{2,1,0:T(8,128)S(1)}, f32[4,32,512]{2,1,0:T(8,128)S(1)}, f32[4,32,512]{2,1,0:T(8,128)S(1)}, s32[4]{0:T(128)S(1)}) custom-call(s32[4]{0:T(128)S(1)} %get-tuple-element.111.info, f32[16,32,512]{2,1,0:T(8,128)S(1)} %get-tuple-element.112.done, f32[6,32,512]{2,1,0:T(8,128)S(1)} %get-tuple-element.113.early_sent, ...), custom_call_target="tpu_custom_call" | custom-call | flops 4035500 | bytes 12915000 | tf_op jit(solution)/shard_map/pallas_call | solution.py:386
  102.1 2.9 %shard_map.193 = (f32[2,512,512]{2,1,0:T(8,128)S(1)}, f32[2,512,512]{2,1,0:T(8,128)S(1)}, s32[4]{0:T(128)S(1)}) custom-call(s32[4]{0:T(128)S(1)} %get-tuple-element.115.info, f32[4,32,512]{2,1,0:T(8,128)S(1)} %get-tuple-element.116.refs_0_, f32[4,32,512]{2,1,0:T(8,128)S(1)} %collective-permute-done.26.refs_1_, ...), custom_call_target="tpu_custom_call" | custom-call | flops 4612000 | bytes 14760000 | tf_op jit(solution)/shard_map/pallas_call | solution.py:446
  105.0 3.2 %collective-permute-done.30.refs_2_ = f32[4,32,512]{2,1,0:T(8,128)S(1)} collective-permute-done((f32[4,32,512]{2,1,0:T(8,128)S(1)}, f32[4,32,512]{2,1,0:T(8,128)S(1)}, u32[]{:S(2)}, u32[]{:S(2)}) %collective-permute-start.30) | collective-permute-done | bytes 262176 | tf_op jit(solution)/shard_map/ppermute | solution.py:491
  108.2 5.8 %collective-permute-done.31.refs_3_ = f32[4,32,512]{2,1,0:T(8,128)S(1)} collective-permute-done((f32[4,32,512]{2,1,0:T(8,128)S(1)}, f32[4,32,512]{2,1,0:T(8,128)S(1)}, u32[]{:S(2)}, u32[]{:S(2)}) %collective-permute-start.31) | collective-permute-done | bytes 262176 | tf_op jit(solution)/shard_map/ppermute | solution.py:491
  114.0 3.4 %shard_map.194 = (f32[2,512,1024]{2,1,0:T(8,128)}, s32[4]{0:T(128)}) custom-call(s32[4]{0:T(128)S(1)} %get-tuple-element.121.info, f32[4,32,512]{2,1,0:T(8,128)S(1)} %get-tuple-element.122.refs_0_, f32[4,32,512]{2,1,0:T(8,128)S(1)} %collective-permute-done.29.refs_1_, f32[4,32,512]{2,1,0:T(8,128)S(1)} %collective-permute-done.30.refs_2_, ...), custom_call_target="tpu_custom_call" | custom-call | flops 4612000 | bytes 14760000 | tf_op jit(solution)/shard_map/pallas_call | solution.py:446
  (71 shorter events, 33.4 us)
Async XLA Ops:
  8.5 12.9 %collective-permute-start.2 = (f32[4,32,512]{2,1,0:T(8,128)S(1)}, f32[4,32,512]{2,1,0:T(8,128)S(1)}, u32[]{:S(2)}, u32[]{:S(2)}) collective-permute-start(f32[4,32,512]{2,1,0:T(8,128)S(1)} %get-tuple-element.72), channel_id=1, source_target_pairs={{0,6},{2,4},{4,2},{6,0},{8,14},{10,12},{12,10},{14,8},{16,22},{18,... | collective-permute-start | bytes 786440 | tf_op jit(solution)/shard_map/ppermute | solution.py:491
  8.9 20.1 %collective-permute-start.3 = (f32[4,32,512]{2,1,0:T(8,128)S(1)}, f32[4,32,512]{2,1,0:T(8,128)S(1)}, u32[]{:S(2)}, u32[]{:S(2)}) collective-permute-start(f32[4,32,512]{2,1,0:T(8,128)S(1)} %get-tuple-element.75), channel_id=1, source_target_pairs={{0,2},{2,0},{4,6},{6,4},{8,10},{10,8},{12,14},{14,12},{16,18},{18,... | collective-permute-start | bytes 786440 | tf_op jit(solution)/shard_map/ppermute | solution.py:491
  9.1 20.1 %collective-permute-start.4 = (f32[4,32,512]{2,1,0:T(8,128)S(1)}, f32[4,32,512]{2,1,0:T(8,128)S(1)}, u32[]{:S(2)}, u32[]{:S(2)}) collective-permute-start(f32[4,32,512]{2,1,0:T(8,128)S(1)} %get-tuple-element.76), channel_id=1, source_target_pairs={{0,4},{2,6},{4,0},{6,2},{8,12},{10,14},{12,8},{14,10},{16,20},{18,... | collective-permute-start | bytes 786440 | tf_op jit(solution)/shard_map/ppermute | solution.py:491
  10.3 22.5 %collective-permute-start.5 = (f32[4,32,512]{2,1,0:T(8,128)S(1)}, f32[4,32,512]{2,1,0:T(8,128)S(1)}, u32[]{:S(2)}, u32[]{:S(2)}) collective-permute-start(f32[4,32,512]{2,1,0:T(8,128)S(1)} %get-tuple-element.77), channel_id=1, source_target_pairs={{0,6},{2,4},{4,2},{6,0},{8,14},{10,12},{12,10},{14,8},{16,22},{18,... | collective-permute-start | bytes 786440 | tf_op jit(solution)/shard_map/ppermute | solution.py:491
  23.7 19.8 %collective-permute-start.6 = (f32[6,32,512]{2,1,0:T(8,128)S(1)}, f32[6,32,512]{2,1,0:T(8,128)S(1)}, u32[]{:S(2)}, u32[]{:S(2)}) collective-permute-start(f32[6,32,512]{2,1,0:T(8,128)S(1)} %get-tuple-element.80.early_sent), channel_id=1, source_target_pairs={{8,16},{16,8},{10,18},{18,10},{12,20},{20,12},{14,22},{22,14},{24,... | collective-permute-start | bytes 1179656 | tf_op jit(solution)/shard_map/ppermute | solution.py:508
  28.9 17.1 %collective-permute-start.7 = (f32[6,32,512]{2,1,0:T(8,128)S(1)}, f32[6,32,512]{2,1,0:T(8,128)S(1)}, u32[]{:S(2)}, u32[]{:S(2)}) collective-permute-start(f32[6,32,512]{2,1,0:T(8,128)S(1)} %get-tuple-element.81.late_sent), channel_id=1, source_target_pairs={{0,8},{8,0},{2,10},{10,2},{4,12},{12,4},{6,14},{14,6},{16,24},{24,... | collective-permute-start | bytes 1179656 | tf_op jit(solution)/shard_map/ppermute | solution.py:508
  29.2 12.1 %collective-permute-start.9 = (f32[4,32,512]{2,1,0:T(8,128)S(1)}, f32[4,32,512]{2,1,0:T(8,128)S(1)}, u32[]{:S(2)}, u32[]{:S(2)}) collective-permute-start(f32[4,32,512]{2,1,0:T(8,128)S(1)} %get-tuple-element.85), channel_id=1, source_target_pairs={{0,4},{2,6},{4,0},{6,2},{8,12},{10,14},{12,8},{14,10},{16,20},{18,... | collective-permute-start | bytes 786440 | tf_op jit(solution)/shard_map/ppermute | solution.py:491
  32.8 10.5 %collective-permute-start.10 = (f32[4,32,512]{2,1,0:T(8,128)S(1)}, f32[4,32,512]{2,1,0:T(8,128)S(1)}, u32[]{:S(2)}, u32[]{:S(2)}) collective-permute-start(f32[4,32,512]{2,1,0:T(8,128)S(1)} %get-tuple-element.86), channel_id=1, source_target_pairs={{0,6},{2,4},{4,2},{6,0},{8,14},{10,12},{12,10},{14,8},{16,22},{18,... | collective-permute-start | bytes 786440 | tf_op jit(solution)/shard_map/ppermute | solution.py:491
  35.9 23.4 %collective-permute-start.11 = (f32[6,32,512]{2,1,0:T(8,128)S(1)}, f32[6,32,512]{2,1,0:T(8,128)S(1)}, u32[]{:S(2)}, u32[]{:S(2)}) collective-permute-start(f32[6,32,512]{2,1,0:T(8,128)S(1)} %get-tuple-element.89.early_sent), channel_id=1, source_target_pairs={{8,16},{16,8},{10,18},{18,10},{12,20},{20,12},{14,22},{22,14},{24,... | collective-permute-start | bytes 1179656 | tf_op jit(solution)/shard_map/ppermute | solution.py:508
  41.3 21.7 %collective-permute-start.12 = (f32[6,32,512]{2,1,0:T(8,128)S(1)}, f32[6,32,512]{2,1,0:T(8,128)S(1)}, u32[]{:S(2)}, u32[]{:S(2)}) collective-permute-start(f32[6,32,512]{2,1,0:T(8,128)S(1)} %get-tuple-element.90.late_sent), channel_id=1, source_target_pairs={{0,8},{8,0},{2,10},{10,2},{4,12},{12,4},{6,14},{14,6},{16,24},{24,... | collective-permute-start | bytes 1179656 | tf_op jit(solution)/shard_map/ppermute | solution.py:508
  46.1 11.1 %collective-permute-start.15 = (f32[4,32,512]{2,1,0:T(8,128)S(1)}, f32[4,32,512]{2,1,0:T(8,128)S(1)}, u32[]{:S(2)}, u32[]{:S(2)}) collective-permute-start(f32[4,32,512]{2,1,0:T(8,128)S(1)} %get-tuple-element.95), channel_id=1, source_target_pairs={{0,6},{2,4},{4,2},{6,0},{8,14},{10,12},{12,10},{14,8},{16,22},{18,... | collective-permute-start | bytes 786440 | tf_op jit(solution)/shard_map/ppermute | solution.py:491
  51.0 16.9 %collective-permute-start.16 = (f32[4,32,512]{2,1,0:T(8,128)S(1)}, f32[4,32,512]{2,1,0:T(8,128)S(1)}, u32[]{:S(2)}, u32[]{:S(2)}) collective-permute-start(f32[4,32,512]{2,1,0:T(8,128)S(1)} %get-tuple-element.98), channel_id=1, source_target_pairs={{0,2},{2,0},{4,6},{6,4},{8,10},{10,8},{12,14},{14,12},{16,18},{18,... | collective-permute-start | bytes 786440 | tf_op jit(solution)/shard_map/ppermute | solution.py:491
  53.5 22.6 %collective-permute-start.19 = (f32[6,32,512]{2,1,0:T(8,128)S(1)}, f32[6,32,512]{2,1,0:T(8,128)S(1)}, u32[]{:S(2)}, u32[]{:S(2)}) collective-permute-start(f32[6,32,512]{2,1,0:T(8,128)S(1)} %get-tuple-element.103.early_sent), channel_id=1, source_target_pairs={{8,16},{16,8},{10,18},{18,10},{12,20},{20,12},{14,22},{22,14},{24,... | collective-permute-start | bytes 1179656 | tf_op jit(solution)/shard_map/ppermute | solution.py:508
  57.2 22.7 %collective-permute-start.20 = (f32[6,32,512]{2,1,0:T(8,128)S(1)}, f32[6,32,512]{2,1,0:T(8,128)S(1)}, u32[]{:S(2)}, u32[]{:S(2)}) collective-permute-start(f32[6,32,512]{2,1,0:T(8,128)S(1)} %get-tuple-element.104.late_sent), channel_id=1, source_target_pairs={{0,8},{8,0},{2,10},{10,2},{4,12},{12,4},{6,14},{14,6},{16,24},{24,... | collective-permute-start | bytes 1179656 | tf_op jit(solution)/shard_map/ppermute | solution.py:508
  59.3 11.1 %collective-permute-start.17 = (f32[4,32,512]{2,1,0:T(8,128)S(1)}, f32[4,32,512]{2,1,0:T(8,128)S(1)}, u32[]{:S(2)}, u32[]{:S(2)}) collective-permute-start(f32[4,32,512]{2,1,0:T(8,128)S(1)} %get-tuple-element.99), channel_id=1, source_target_pairs={{0,4},{2,6},{4,0},{6,2},{8,12},{10,14},{12,8},{14,10},{16,20},{18,... | collective-permute-start | bytes 786440 | tf_op jit(solution)/shard_map/ppermute | solution.py:491
  63.0 10.4 %collective-permute-start.18 = (f32[4,32,512]{2,1,0:T(8,128)S(1)}, f32[4,32,512]{2,1,0:T(8,128)S(1)}, u32[]{:S(2)}, u32[]{:S(2)}) collective-permute-start(f32[4,32,512]{2,1,0:T(8,128)S(1)} %get-tuple-element.100), channel_id=1, source_target_pairs={{0,6},{2,4},{4,2},{6,0},{8,14},{10,12},{12,10},{14,8},{16,22},{18,... | collective-permute-start | bytes 786440 | tf_op jit(solution)/shard_map/ppermute | solution.py:491
  67.9 19.5 %collective-permute-start.21 = (f32[4,32,512]{2,1,0:T(8,128)S(1)}, f32[4,32,512]{2,1,0:T(8,128)S(1)}, u32[]{:S(2)}, u32[]{:S(2)}) collective-permute-start(f32[4,32,512]{2,1,0:T(8,128)S(1)} %get-tuple-element.107), channel_id=1, source_target_pairs={{0,2},{2,0},{4,6},{6,4},{8,10},{10,8},{12,14},{14,12},{16,18},{18,... | collective-permute-start | bytes 786440 | tf_op jit(solution)/shard_map/ppermute | solution.py:491
  70.4 22.9 %collective-permute-start.24 = (f32[6,32,512]{2,1,0:T(8,128)S(1)}, f32[6,32,512]{2,1,0:T(8,128)S(1)}, u32[]{:S(2)}, u32[]{:S(2)}) collective-permute-start(f32[6,32,512]{2,1,0:T(8,128)S(1)} %get-tuple-element.113.early_sent), channel_id=1, source_target_pairs={{8,16},{16,8},{10,18},{18,10},{12,20},{20,12},{14,22},{22,14},{24,... | collective-permute-start | bytes 1179656 | tf_op jit(solution)/shard_map/ppermute | solution.py:508
  73.4 23.4 %collective-permute-start.25 = (f32[6,32,512]{2,1,0:T(8,128)S(1)}, f32[6,32,512]{2,1,0:T(8,128)S(1)}, u32[]{:S(2)}, u32[]{:S(2)}) collective-permute-start(f32[6,32,512]{2,1,0:T(8,128)S(1)} %get-tuple-element.114.late_sent), channel_id=1, source_target_pairs={{0,8},{8,0},{2,10},{10,2},{4,12},{12,4},{6,14},{14,6},{16,24},{24,... | collective-permute-start | bytes 1179656 | tf_op jit(solution)/shard_map/ppermute | solution.py:508
  76.1 11.4 %collective-permute-start.22 = (f32[4,32,512]{2,1,0:T(8,128)S(1)}, f32[4,32,512]{2,1,0:T(8,128)S(1)}, u32[]{:S(2)}, u32[]{:S(2)}) collective-permute-start(f32[4,32,512]{2,1,0:T(8,128)S(1)} %get-tuple-element.108), channel_id=1, source_target_pairs={{0,4},{2,6},{4,0},{6,2},{8,12},{10,14},{12,8},{14,10},{16,20},{18,... | collective-permute-start | bytes 786440 | tf_op jit(solution)/shard_map/ppermute | solution.py:491
  87.4 14.2 %collective-permute-start.26 = (f32[4,32,512]{2,1,0:T(8,128)S(1)}, f32[4,32,512]{2,1,0:T(8,128)S(1)}, u32[]{:S(2)}, u32[]{:S(2)}) collective-permute-start(f32[4,32,512]{2,1,0:T(8,128)S(1)} %get-tuple-element.117), channel_id=1, source_target_pairs={{0,2},{2,0},{4,6},{6,4},{8,10},{10,8},{12,14},{14,12},{16,18},{18,... | collective-permute-start | bytes 786440 | tf_op jit(solution)/shard_map/ppermute | solution.py:491
  87.5 14.6 %collective-permute-start.27 = (f32[4,32,512]{2,1,0:T(8,128)S(1)}, f32[4,32,512]{2,1,0:T(8,128)S(1)}, u32[]{:S(2)}, u32[]{:S(2)}) collective-permute-start(f32[4,32,512]{2,1,0:T(8,128)S(1)} %get-tuple-element.118), channel_id=1, source_target_pairs={{0,4},{2,6},{4,0},{6,2},{8,12},{10,14},{12,8},{14,10},{16,20},{18,... | collective-permute-start | bytes 786440 | tf_op jit(solution)/shard_map/ppermute | solution.py:491
  90.1 12.0 %collective-permute-start.28 = (f32[4,32,512]{2,1,0:T(8,128)S(1)}, f32[4,32,512]{2,1,0:T(8,128)S(1)}, u32[]{:S(2)}, u32[]{:S(2)}) collective-permute-start(f32[4,32,512]{2,1,0:T(8,128)S(1)} %get-tuple-element.119), channel_id=1, source_target_pairs={{0,6},{2,4},{4,2},{6,0},{8,14},{10,12},{12,10},{14,8},{16,22},{18,... | collective-permute-start | bytes 786440 | tf_op jit(solution)/shard_map/ppermute | solution.py:491
  101.6 12.4 %collective-permute-start.31 = (f32[4,32,512]{2,1,0:T(8,128)S(1)}, f32[4,32,512]{2,1,0:T(8,128)S(1)}, u32[]{:S(2)}, u32[]{:S(2)}) collective-permute-start(f32[4,32,512]{2,1,0:T(8,128)S(1)} %get-tuple-element.125), channel_id=1, source_target_pairs={{0,6},{2,4},{4,2},{6,0},{8,14},{10,12},{12,10},{14,8},{16,22},{18,... | collective-permute-start | bytes 786440 | tf_op jit(solution)/shard_map/ppermute | solution.py:491
  (16 other events, 182.6 us)
